TPU v7x, 256 devices: a whole 4x4x8 slice. The times are simulated.
256 devices in a mesh: fsdp: 64 (over z, x, core), rep: 4 (over y).
Axes of the slice: x: 4, y: 4, z: 8, core: 2. Of those that a mesh axis runs over, the one named last changes fastest.
Arguments:
- acts: bfloat16 [262144, 1536], P(('fsdp', 'rep')), may hold values from -24 to 24
- cotangent: bfloat16 [262144, 4096], P(('fsdp', 'rep')), may hold values from -0.01171875 to 0.01171875
- master: float32 [1536, 4096], P(('fsdp', 'rep')), may hold values from -6 to 6
- moment: float32 [1536, 4096], P(('fsdp', 'rep')), may hold values from -4 to 4
- second: float32 [1536, 4096], P(('fsdp', 'rep')), may hold values from 0.01 to 2
Outputs:
- new_master: float32 [1536, 4096], P(('fsdp', 'rep'))
- new_moment: float32 [1536, 4096], P(('fsdp', 'rep'))
- new_second: float32 [1536, 4096], P(('fsdp', 'rep'))
- params: bfloat16 [1536, 4096], P('fsdp')
All inputs are finite; a program needn't handle non-finite values.
Results may differ from a plain program's by a relative error of at most 0.0049.
Values may be sent and summed in bfloat16 or wider, within the bound.
No kernel may reach another device: no remote copies, remote signals or barrier semaphores. Data moves between devices by JAX's collectives and lax.ppermute only.
A program may use at most 128 MiB of HBM per device.

v0:
```python
import jax
import jax.numpy as jnp
from jax import lax
from jax.sharding import PartitionSpec as P


def body(acts, cotangent, master, moment, second):
    partial_grad = lax.psum_scatter(
        lax.dot_general(
            acts, cotangent, (((0,), (0,)), ((), ())), preferred_element_type=jnp.float32
        ),
        "fsdp",
        scatter_dimension=0,
        tiled=True,
    )
    grad = lax.psum_scatter(
        partial_grad.astype(jnp.bfloat16), "rep", scatter_dimension=0, tiled=True
    ).astype(jnp.float32)
    new_moment = 0.9 * moment + 0.1 * grad
    new_second = 0.95 * second + 0.05 * grad * grad
    corr_one = 1.0 - 0.9**10
    corr_two = 1.0 - 0.95**10
    update = new_moment / corr_one / (jnp.sqrt(new_second / corr_two) + 1e-08)
    new_master = master - 0.02 * (update + 0.1 * master)
    rounded = new_master.astype(jnp.bfloat16)
    params = lax.all_gather(rounded, "rep", axis=0, tiled=True)
    return (new_master, new_moment, new_second, params)


def solution(mesh):
    in_specs = (
        P(("fsdp", "rep"), None),
        P(("fsdp", "rep"), None),
        P(("fsdp", "rep"), None),
        P(("fsdp", "rep"), None),
        P(("fsdp", "rep"), None),
    )
    out_specs = (
        P(("fsdp", "rep"), None),
        P(("fsdp", "rep"), None),
        P(("fsdp", "rep"), None),
        P("fsdp", None),
    )
    return jax.shard_map(body, mesh=mesh, in_specs=in_specs, out_specs=out_specs, check_vma=False)
```

profile of v0, /device:TPU:8, one launch (start us, length us, event | category | flops | bytes accessed | tf_op | source)
XLA Modules:
  0.0 293.5 jit_solution(13874500856414093044)
XLA Ops:
  7.2 0.0 copy-start
  7.2 0.0 reduce-scatter.6.cloned.1.call-start
  7.2 1.8 copy-done
  9.1 20.2 %fusion.5 = f32[1536,4096]{1,0:T(8,128)} fusion(bf16[1024,1536]{1,0:T(8,128)(2,1)S(1)} %copy-done, bf16[1024,4096]{1,0:T(8,128)(2,1)} %param.6), kind=kOutput, calls=%fused_computation.6 | convolution fusion | flops 12884901888 | bytes 36700160 | tf_op jit(solution)/shard_map/dot_general | solution.py:9
  29.2 0.0 copy-start.2
  29.2 0.0 copy-start.1
  29.2 0.0 reduce-scatter.6.cloned.1.call-update
  29.3 223.4 %reduce-scatter.6.cloned.1.call-done = f32[24,4096]{1,0:T(8,128)} async-done(((f32[1536,4096]{1,0:T(8,128)}), f32[24,4096]{1,0:T(8,128)}) %reduce-scatter.6.cloned.1.call-update) | async-done | bytes 393232
  252.6 1.0 convert_element_type.9
  253.7 12.6 %fusion = bf16[8,4096]{1,0:T(8,128)(2,1)S(1)} fusion(bf16[24,4096]{1,0:T(8,128)(2,1)S(1)} %convert_element_type.9), kind=kCustom, calls=%all-reduce-scatter | all-reduce-scatter fusion | flops 131073 | bytes 263168
  266.3 1.9 collective-permute-start
  268.3 0.0 copy-done.2
  268.3 0.6 dynamic-slice.6
  269.5 3.3 %collective-permute-done = bf16[6,4096]{1,0:T(8,128)(2,1)S(1)} collective-permute-done((bf16[6,4096]{1,0:T(8,128)(2,1)S(1)}, bf16[6,4096]{1,0:T(8,128)(2,1)S(1)}, u32[]{:S(2)}, u32[]{:S(2)}) %collective-permute-start) | collective-permute-done | bytes 49184
  272.8 0.2 concatenate
  273.0 0.0 copy-done.1
  273.1 1.8 convert_bitcast_fusion
  274.9 11.0 %all-gather = bf16[4,6,4096]{2,1,0:T(8,128)(2,1)S(1)} all-gather(bf16[1,6,4096]{2,1,0:T(8,128)(2,1)S(1)} %get-tuple-element.4), channel_id=1, replica_groups=mesh['fsdp'=64,'rep'=4] {'rep'}, dimensions={0}, use_global_device_ids=true | all-gather | bytes 245760 | tf_op jit(solution)/shard_map/all_gather | solution.py:26
  285.9 0.7 reshape.9
  (1 shorter events, 0.0 us)
Async XLA Ops:
  7.2 1.9 copy-start
  7.2 245.5 %reduce-scatter.6.cloned.1.call-start = ((), (), s32[]{:S(2)}) async-start(), calls=%async_computation.1 | async-start | bytes 25559040
  29.2 239.0 %copy-start.2 = (u32[256]{0:T(256)S(1)}, u32[256]{0:T(256)}, u32[]{:S(2)}) copy-start(u32[256]{0:T(256)} %constant.27) | copy-start | bytes 3076
  29.2 243.8 %copy-start.1 = (f32[6,4096]{1,0:T(8,128)S(1)}, f32[6,4096]{1,0:T(8,128)}, u32[]{:S(2)}) copy-start(f32[6,4096]{1,0:T(8,128)} %param.7) | copy-start | bytes 294916
  266.3 6.5 %collective-permute-start = (bf16[6,4096]{1,0:T(8,128)(2,1)S(1)}, bf16[6,4096]{1,0:T(8,128)(2,1)S(1)}, u32[]{:S(2)}, u32[]{:S(2)}) collective-permute-start(bf16[6,4096]{1,0:T(8,128)(2,1)S(1)} %slice), channel_id=1, source_target_pairs={{0,1},{1,2},{2,3},{4,5},{5,6},{6,7},{8,9},{9,10},{10,11},{12,13},{... | collective-permute-start | bytes 147464
Sparse Core Ops, SparseCore 0:
  29.4 223.1 reduce-scatter.5
where the time goes:
time: 294 us; the launch traced here: 293 us
  waiting for transfers between devices  227 us (77%)
  blocking collectives  23.7 us (8%)
  matrix products  20.2 us (7%)
  between operations  14.7 us (5%)
  local copies, waits for them, and re-layouts  3.4 us (1%)
    unnamed x3, waiting for transfers between devices  227 us
    dot_general x1, matrix products, body(): lax.dot_general(acts, cotangent, (((0,), (0,)), ((), ())), preferred_elem...  20.2 us
    unnamed x1, blocking collectives  12.6 us
    all_gather x1, blocking collectives, body(): params = lax.all_gather(rounded, 'rep', axis=0, tiled=True)  11 us
  transfers between devices with their start and end apart: 2, of which 2 were waited for; matrix products, arithmetic and copies ran while one was open for 0% of the time, Pallas kernels for 0%

commit v1 on v0

v1 whole, which is shorter than its diff:
```python
import jax
import jax.numpy as jnp
from jax import lax
from jax.experimental import pallas as pl
from jax.experimental.pallas import tpu as pltpu
from jax.sharding import Mesh, PartitionSpec as P

NZ, NX, NC, NY = 8, 4, 2, 4
D, FFW = 1536, 4096
HALF = FFW // 2
TN = 256
BLK = D // (NZ * NX)
FLOW_C = 1024
FLOW_B = 1024
T = 1024
F32, BF16 = jnp.float32, jnp.bfloat16
VMEM_LIMIT = 48 * 1024 * 1024
DN = (((0,), (0,)), ((), ()))


def params_of(flops, nbytes):
    return dict(
        compiler_params=pltpu.CompilerParams(vmem_limit_bytes=VMEM_LIMIT),
        cost_estimate=pl.CostEstimate(flops=flops, bytes_accessed=nbytes, transcendentals=0),
    )


def shift(v, axis, n, s):
    return lax.ppermute(v, axis, [(i, (i + s) % n) for i in range(n)])


def product(acts, cot, idx, base, ncols):
    def kernel(idx_ref, a, c, o):
        o[...] = lax.dot_general(a[...], c[...], DN, preferred_element_type=F32).astype(BF16)

    return pl.pallas_call(
        kernel,
        grid_spec=pltpu.PrefetchScalarGridSpec(
            num_scalar_prefetch=1,
            grid=(ncols // TN,),
            in_specs=[
                pl.BlockSpec((T, D), lambda j, s: (0, 0)),
                pl.BlockSpec((T, TN), lambda j, s: (0, (1 - s[0]) * (HALF // TN) + base // TN + j)),
            ],
            out_specs=pl.BlockSpec((D, TN), lambda j, s: (0, j)),
        ),
        out_shape=jax.ShapeDtypeStruct((D, ncols), BF16),
        name="product_theirs",
        **params_of(2 * T * D * ncols, 2 * (T * D + T * ncols + D * ncols)),
    )(idx, acts, cot)


def product_for_y(acts, cot, got, idx, base):
    def kernel(idx_ref, a, c, r, *outs):
        acc = lax.dot_general(a[...], c[...], DN, preferred_element_type=F32) + r[...].astype(F32)
        for o in range(NY):

            @pl.when(pl.program_id(0) == o)
            def _():
                outs[o][...] = acc.astype(BF16)

    return pl.pallas_call(
        kernel,
        grid_spec=pltpu.PrefetchScalarGridSpec(
            num_scalar_prefetch=1,
            grid=(NY,),
            in_specs=[
                pl.BlockSpec((T, D), lambda j, s: (0, 0)),
                pl.BlockSpec((T, TN), lambda j, s: (0, s[0] * (HALF // TN) + base // TN + lax.rem(s[2] + j, NY))),
                pl.BlockSpec((D, TN), lambda j, s: (0, lax.rem(s[2] + j, NY))),
            ],
            out_specs=[pl.BlockSpec((D, TN), lambda j, s: (0, 0))] * NY,
        ),
        out_shape=[jax.ShapeDtypeStruct((D, TN), BF16)] * NY,
        name="product_for_y",
        **params_of(2 * T * D * TN * NY, 2 * (T * D + T * TN * NY + 2 * D * TN * NY)),
    )(idx, acts, cot, got)


def product_for_x(acts, cot, got, idx, base, ncols):
    def kernel(idx_ref, a, c, r, *rest):
        outs, acc = rest[:NX], rest[NX]
        acc[...] = lax.dot_general(a[...], c[...], DN, preferred_element_type=F32) + r[...].astype(F32)
        for o in range(NX):
            target = lax.rem(idx_ref[1] + o, NX)
            for z in range(NZ):
                rows = pl.ds(pl.multiple_of((z * NX + target) * BLK, BLK), BLK)
                outs[o][z] = acc[rows, :].astype(BF16)

    return pl.pallas_call(
        kernel,
        grid_spec=pltpu.PrefetchScalarGridSpec(
            num_scalar_prefetch=1,
            grid=(ncols // TN,),
            in_specs=[
                pl.BlockSpec((T, D), lambda j, s: (0, 0)),
                pl.BlockSpec((T, TN), lambda j, s: (0, s[0] * (HALF // TN) + base // TN + j)),
                pl.BlockSpec((D, TN), lambda j, s: (0, j)),
            ],
            out_specs=[pl.BlockSpec((NZ, BLK, TN), lambda j, s: (0, 0, j))] * NX,
            scratch_shapes=[pltpu.VMEM((D, TN), F32)],
        ),
        out_shape=[jax.ShapeDtypeStruct((NZ, BLK, ncols), BF16)] * NX,
        name="product_for_x",
        **params_of(2 * T * D * ncols, 2 * (T * D + T * ncols + 2 * D * ncols)),
    )(idx, acts, cot, got)


def sum_for_x(parts, idx):
    width = parts[0].shape[-1]

    def kernel(idx_ref, *refs):
        ins, outs = refs[:NY], refs[NY:]
        total = ins[0][...].astype(F32)
        for r in ins[1:]:
            total = total + r[...].astype(F32)
        for o in range(NX):

            @pl.when(pl.program_id(0) == o)
            def _():
                outs[o][...] = total[:, 0].astype(BF16)

    return pl.pallas_call(
        kernel,
        grid_spec=pltpu.PrefetchScalarGridSpec(
            num_scalar_prefetch=1,
            grid=(NX,),
            in_specs=[pl.BlockSpec((NZ, 1, BLK, width), lambda j, s: (0, lax.rem(s[1] + j, NX), 0, 0))] * NY,
            out_specs=[pl.BlockSpec((NZ, BLK, width), lambda j, s: (0, 0, 0))] * NX,
        ),
        out_shape=[jax.ShapeDtypeStruct((NZ, BLK, width), BF16)] * NX,
        name="sum_for_x",
        **params_of(4 * D * width, 2 * 5 * D * width),
    )(idx, *[p.reshape(NZ, NX, BLK, width) for p in parts])


def sum_for_z(first, second, idx):
    wa, wb = first[0].shape[-1], second[0].shape[-1]

    def kernel(idx_ref, *refs):
        ins, outs = refs[: 2 * NX], refs[2 * NX :]
        sums = []
        for group in (ins[:NX], ins[NX:]):
            total = group[0][0].astype(F32)
            for r in group[1:]:
                total = total + r[0].astype(F32)
            sums.append(total.astype(BF16))
        for o in range(NZ):

            @pl.when(pl.program_id(0) == o)
            def _():
                outs[o][:, :wa] = sums[0]
                outs[o][:, wa:] = sums[1]

    spec = lambda w: pl.BlockSpec((1, BLK, w), lambda j, s: (lax.rem(s[3] + j, NZ), 0, 0))
    return pl.pallas_call(
        kernel,
        grid_spec=pltpu.PrefetchScalarGridSpec(
            num_scalar_prefetch=1,
            grid=(NZ,),
            in_specs=[spec(wa)] * NX + [spec(wb)] * NX,
            out_specs=[pl.BlockSpec((BLK, wa + wb), lambda j, s: (0, 0))] * NZ,
        ),
        out_shape=[jax.ShapeDtypeStruct((BLK, wa + wb), BF16)] * NZ,
        name="sum_for_z",
        **params_of(4 * NZ * BLK * (wa + wb), 2 * 5 * NZ * BLK * (wa + wb)),
    )(idx, *first, *second)


def sum_for_core(parts, idx):
    width = parts[0].shape[-1]
    rows = BLK // NC

    def kernel(idx_ref, *refs):
        ins, mine, theirs, acc = refs[:NZ], refs[NZ], refs[NZ + 1], refs[NZ + 2]
        total = ins[0][...].astype(F32)
        for r in ins[1:]:
            total = total + r[...].astype(F32)
        acc[...] = total
        c = idx_ref[0]
        mine[...] = acc[pl.ds(pl.multiple_of(c * rows, rows), rows), :].astype(BF16)
        theirs[...] = acc[pl.ds(pl.multiple_of((1 - c) * rows, rows), rows), :].astype(BF16)

    whole = lambda h: pl.BlockSpec((h, width), lambda j, s: (0, 0))
    return pl.pallas_call(
        kernel,
        grid_spec=pltpu.PrefetchScalarGridSpec(
            num_scalar_prefetch=1,
            grid=(1,),
            in_specs=[whole(BLK)] * NZ,
            out_specs=[whole(rows)] * NC,
            scratch_shapes=[pltpu.VMEM((BLK, width), F32)],
        ),
        out_shape=[jax.ShapeDtypeStruct((rows, width), BF16)] * NC,
        name="sum_for_core",
        **params_of(NZ * BLK * width, 2 * 9 * BLK * width),
    )(idx, *parts)


def body(acts, cotangent, master, moment, second):
    z, x, c, y = (lax.axis_index(a) for a in ("z", "x", "c", "y"))
    idx = jnp.stack([c, x, y, z]).astype(jnp.int32)
    theirs_c = product(acts, cotangent, idx, 0, FLOW_C)
    got_c = shift(theirs_c, "c", NC, 1)
    theirs_b = product(acts, cotangent, idx, FLOW_C, FLOW_B)
    got_b = shift(theirs_b, "c", NC, 1)
    pieces_c = product_for_y(acts, cotangent, got_c, idx, 0)
    over_y = [pieces_c[0]] + [shift(pieces_c[s], "y", NY, s) for s in (1, 3, 2)]
    pieces_b = product_for_x(acts, cotangent, got_b, idx, FLOW_C, FLOW_B)
    over_x = [pieces_b[0]] + [shift(pieces_b[s], "x", NX, s) for s in (1, 3, 2)]
    pieces_cx = sum_for_x(over_y, idx)
    over_cx = [pieces_cx[0]] + [shift(pieces_cx[s], "x", NX, s) for s in (1, 3, 2)]
    pieces_z = sum_for_z(over_cx, over_x, idx)
    over_z = [pieces_z[0]] + [shift(pieces_z[s], "z", NZ, s) for s in (4, 3, 5, 2, 6, 1, 7)]
    mine, theirs = sum_for_core(over_z, idx)
    got = shift(theirs, "c", NC, 1)
    pair = jnp.stack([jnp.where(c == 0, mine, got), jnp.where(c == 0, got, mine)])
    rows = BLK // NC // NY
    piece = lambda s: lax.dynamic_slice_in_dim(pair, lax.rem(y + s, NY) * rows, rows, 1)
    from_y = [piece(0)] + [shift(piece(s), "y", NY, s) for s in (1, 2, 3)]
    width = FLOW_C // NY
    by_source = [lax.select_n(lax.rem(y - k + NY, NY), *[p[:, :, :width] for p in from_y]) for k in range(NY)]
    part_c = jnp.concatenate(by_source, axis=-1).astype(F32)
    part_b = sum(p[:, :, width:].astype(F32) for p in from_y)
    halves = jnp.concatenate([part_c, part_b], axis=-1)
    grad = jnp.concatenate([halves[0], halves[1]], axis=-1)
    new_moment = 0.9 * moment + 0.1 * grad
    new_second = 0.95 * second + 0.05 * grad * grad
    corr_one = 1.0 - 0.9**10
    corr_two = 1.0 - 0.95**10
    update = new_moment / corr_one / (jnp.sqrt(new_second / corr_two) + 1e-08)
    new_master = master - 0.02 * (update + 0.1 * master)
    rounded = new_master.astype(BF16)
    every = [rounded] + [shift(rounded, "y", NY, s) for s in (1, 2, 3)]
    params = jnp.concatenate([lax.select_n(lax.rem(y - k + NY, NY), *every) for k in range(NY)], axis=0)
    return (new_master, new_moment, new_second, params)


def solution(mesh):
    fine = Mesh(mesh.devices.reshape(NZ, NX, NC, NY), ("z", "x", "c", "y"))
    split = P(("z", "x", "c", "y"), None)
    return jax.shard_map(
        body,
        mesh=fine,
        in_specs=(split,) * 5,
        out_specs=(split, split, split, P(("z", "x", "c"), None)),
        check_vma=False,
    )
```

time: 294 us -> 134 us (0.46)
  the two profiles are of different devices: /device:TPU:8 before, /device:TPU:1 now
where the time goes in v1:
time: 134 us; the launch traced here: 133 us
  waiting for transfers between devices  55.4 us (41%)
  starting transfers between devices  39.2 us (29%)
  Pallas kernels  34.4 us (26%)
  other arithmetic  1.88 us (1%)
  local copies, waits for them, and re-layouts  1.65 us (1%)
    ppermute x25, waiting for transfers between devices, shift(): return lax.ppermute(v, axis, [(i, (i + s) % n) for i in range(n)])  55.4 us
    ppermute x25, starting transfers between devices, shift(): return lax.ppermute(v, axis, [(i, (i + s) % n) for i in range(n)])  39.2 us
    pallas_call x2, Pallas kernels, product(): pl.pallas_call(kernel, grid_spec=pltpu.PrefetchScalarGridSpec(num_scalar_...  14.4 us
    pallas_call x1, Pallas kernels, product_for_x(): pl.pallas_call(kernel, grid_spec=pltpu.PrefetchScalarGridSpec(num_scalar_...  8.42 us
    pallas_call x1, Pallas kernels, product_for_y(): pl.pallas_call(kernel, grid_spec=pltpu.PrefetchScalarGridSpec(num_scalar_...  7.63 us
  transfers between devices with their start and end apart: 25, of which 16 were waited for; matrix products, arithmetic and copies ran while one was open for 0% of the time, Pallas kernels for 19%

profile of v1, /device:TPU:1, one launch (start us, length us, event | category | flops | bytes accessed | tf_op | source)
XLA Modules:
  0.0 133.3 jit_solution(7476680255334341812)
XLA Ops:
  0.7 7.2 %product_theirs.2 = bf16[1536,1024]{1,0:T(8,128)(2,1)S(1)} custom-call(s32[4]{0:T(128)S(1)} %pad_add_fusion.idx_ref, bf16[1024,1536]{1,0:T(8,128)(2,1)} %a.7, bf16[1024,4096]{1,0:T(8,128)(2,1)} %c.7), custom_call_target="tpu_custom_call" | custom-call | flops 3221225472 | bytes 8388608 | tf_op jit(solution)/shard_map/product_theirs/pallas_call | solution.py:36
  7.9 3.3 %collective-permute-start = (bf16[1536,1024]{1,0:T(8,128)(2,1)S(1)}, bf16[1536,1024]{1,0:T(8,128)(2,1)}, u32[]{:S(2)}, u32[]{:S(2)}) collective-permute-start(bf16[1536,1024]{1,0:T(8,128)(2,1)S(1)} %product_theirs.2), channel_id=1, source_target_pairs={{0,4},{4,0},{1,5},{5,1},{2,6},{6,2},{3,7},{7,3},{8,12},{12,8},{9,1... | collective-permute-start | bytes 9437192 | tf_op jit(solution)/shard_map/ppermute | solution.py:29
  11.2 7.2 %product_theirs.3 = bf16[1536,1024]{1,0:T(8,128)(2,1)S(1)} custom-call(s32[4]{0:T(128)S(1)} %pad_add_fusion.idx_ref, bf16[1024,1536]{1,0:T(8,128)(2,1)} %a.7, bf16[1024,4096]{1,0:T(8,128)(2,1)} %c.7), custom_call_target="tpu_custom_call" | custom-call | flops 3221225472 | bytes 8388608 | tf_op jit(solution)/shard_map/product_theirs/pallas_call | solution.py:36
  18.5 7.6 %product_for_y.1 = (bf16[1536,256]{1,0:T(8,128)(2,1)S(1)}, bf16[1536,256]{1,0:T(8,128)(2,1)S(1)}, bf16[1536,256]{1,0:T(8,128)(2,1)S(1)}, bf16[1536,256]{1,0:T(8,128)(2,1)S(1)}) custom-call(s32[4]{0:T(128)S(1)} %pad_add_fusion.idx_ref, bf16[1024,1536]{1,0:T(8,128)(2,1)} %a.7, bf16[1024,4096]{1,0:T(8,128)(2,1)} %c.7, bf16[1536,1024]{1,0:T(8,128)(2,1)} %collective-permute-done.r), custom_call_target="tpu_custom_call" | custom-call | flops 3221225472 | bytes 11534336 | tf_op jit(solution)/shard_map/product_for_y/pallas_call | solution.py:62
  26.3 2.7 %collective-permute-start.2 = (bf16[1536,256]{1,0:T(8,128)(2,1)S(1)}, bf16[1536,256]{1,0:T(8,128)(2,1)S(1)}, u32[]{:S(2)}, u32[]{:S(2)}) collective-permute-start(bf16[1536,256]{1,0:T(8,128)(2,1)S(1)} %get-tuple-element.28), channel_id=1, source_target_pairs={{0,3},{1,0},{2,1},{3,2},{4,7},{5,4},{6,5},{7,6},{8,11},{9,8},{10,9... | collective-permute-start | bytes 2359304 | tf_op jit(solution)/shard_map/ppermute | solution.py:29
  28.9 1.6 %copy-done = bf16[1536,1024]{1,0:T(8,128)(2,1)} copy-done((bf16[1536,1024]{1,0:T(8,128)(2,1)}, bf16[1536,1024]{1,0:T(8,128)(2,1)S(1)}, u32[]{:S(2)}) %copy-start) | copy-done | bytes 3145752
  30.6 8.4 %product_for_x.1 = (bf16[8,48,1024]{2,1,0:T(8,128)(2,1)S(1)}, bf16[8,48,1024]{2,1,0:T(8,128)(2,1)S(1)}, bf16[8,48,1024]{2,1,0:T(8,128)(2,1)S(1)}, bf16[8,48,1024]{2,1,0:T(8,128)(2,1)S(1)}) custom-call(s32[4]{0:T(128)S(1)} %pad_add_fusion.idx_ref, bf16[1024,1536]{1,0:T(8,128)(2,1)} %a.7, bf16[1024,4096]{1,0:T(8,128)(2,1)} %c.7, bf16[1536,1024]{1,0:T(8,128)(2,1)} %copy-done), custom_call_target="tpu_custom_call" | custom-call | flops 3221225472 | bytes 11534336 | tf_op jit(solution)/shard_map/product_for_x/pallas_call | solution.py:90
  39.0 2.8 %collective-permute-start.10 = (bf16[8,48,1024]{2,1,0:T(8,128)(2,1)S(1)}, bf16[8,48,1024]{2,1,0:T(8,128)(2,1)S(1)}, u32[]{:S(2)}, u32[]{:S(2)}) collective-permute-start(bf16[8,48,1024]{2,1,0:T(8,128)(2,1)S(1)} %get-tuple-element.37), channel_id=1, source_target_pairs={{0,16},{8,24},{16,0},{24,8},{1,17},{9,25},{17,1},{25,9},{2,18},{10... | collective-permute-start | bytes 2359304 | tf_op jit(solution)/shard_map/ppermute | solution.py:29
  42.1 4.5 %collective-permute-done.1 = bf16[1536,256]{1,0:T(8,128)(2,1)S(1)} collective-permute-done((bf16[1536,256]{1,0:T(8,128)(2,1)S(1)}, bf16[1536,256]{1,0:T(8,128)(2,1)S(1)}, u32[]{:S(2)}, u32[]{:S(2)}) %collective-permute-start.1) | collective-permute-done | bytes 786464 | tf_op jit(solution)/shard_map/ppermute | solution.py:29
  47.0 15.5 %collective-permute-done.3 = bf16[1536,256]{1,0:T(8,128)(2,1)S(1)} collective-permute-done((bf16[1536,256]{1,0:T(8,128)(2,1)S(1)}, bf16[1536,256]{1,0:T(8,128)(2,1)S(1)}, u32[]{:S(2)}, u32[]{:S(2)}) %collective-permute-start.3) | collective-permute-done | bytes 786464 | tf_op jit(solution)/shard_map/ppermute | solution.py:29
  62.5 1.7 %sum_for_x.1 = (bf16[8,48,256]{2,1,0:T(8,128)(2,1)S(1)}, bf16[8,48,256]{2,1,0:T(8,128)(2,1)S(1)}, bf16[8,48,256]{2,1,0:T(8,128)(2,1)S(1)}, bf16[8,48,256]{2,1,0:T(8,128)(2,1)S(1)}) custom-call(s32[4]{0:T(128)S(1)} %pad_add_fusion.idx_ref, bf16[8,4,48,256]{3,2,1,0:T(8,128)(2,1)S(1)} %bitcast.16, bf16[8,4,48,256]{3,2,1,0:T(8,128)(2,1)S(1)} %bitcast.17, ...), custom_call_target="tpu_custom_call" | custom-call | flops 1572864 | bytes 3932160 | tf_op jit(solution)/shard_map/sum_for_x/pallas_call | solution.py:123
  68.5 8.4 %collective-permute-done.8.refs_5_ = bf16[8,48,1024]{2,1,0:T(8,128)(2,1)S(1)} collective-permute-done((bf16[8,48,1024]{2,1,0:T(8,128)(2,1)S(1)}, bf16[8,48,1024]{2,1,0:T(8,128)(2,1)S(1)}, u32[]{:S(2)}, u32[]{:S(2)}) %collective-permute-start.8) | collective-permute-done | bytes 786464 | tf_op jit(solution)/shard_map/ppermute | solution.py:29
  76.9 5.9 %collective-permute-done.4.refs_1_ = bf16[8,48,256]{2,1,0:T(8,128)(2,1)S(1)} collective-permute-done((bf16[8,48,256]{2,1,0:T(8,128)(2,1)S(1)}, bf16[8,48,256]{2,1,0:T(8,128)(2,1)S(1)}, u32[]{:S(2)}, u32[]{:S(2)}) %collective-permute-start.4) | collective-permute-done | bytes 196640 | tf_op jit(solution)/shard_map/ppermute | solution.py:29
  85.2 6.9 %collective-permute-start.11 = (bf16[48,1280]{1,0:T(8,128)(2,1)S(1)}, bf16[48,1280]{1,0:T(8,128)(2,1)S(1)}, u32[]{:S(2)}, u32[]{:S(2)}) collective-permute-start(bf16[48,1280]{1,0:T(8,128)(2,1)S(1)} %get-tuple-element.39), channel_id=1, source_target_pairs={{0,128},{32,160},{64,192},{96,224},{128,0},{160,32},{192,64},{224,... | collective-permute-start | bytes 368648 | tf_op jit(solution)/shard_map/ppermute | solution.py:29
  92.1 1.7 %collective-permute-start.12 = (bf16[48,1280]{1,0:T(8,128)(2,1)S(1)}, bf16[48,1280]{1,0:T(8,128)(2,1)S(1)}, u32[]{:S(2)}, u32[]{:S(2)}) collective-permute-start(bf16[48,1280]{1,0:T(8,128)(2,1)S(1)} %get-tuple-element.40), channel_id=1, source_target_pairs={{0,96},{32,128},{64,160},{96,192},{128,224},{160,0},{192,32},{224,... | collective-permute-start | bytes 368648 | tf_op jit(solution)/shard_map/ppermute | solution.py:29
  93.8 2.8 %collective-permute-start.13 = (bf16[48,1280]{1,0:T(8,128)(2,1)S(1)}, bf16[48,1280]{1,0:T(8,128)(2,1)S(1)}, u32[]{:S(2)}, u32[]{:S(2)}) collective-permute-start(bf16[48,1280]{1,0:T(8,128)(2,1)S(1)} %get-tuple-element.41), channel_id=1, source_target_pairs={{0,160},{32,192},{64,224},{96,0},{128,32},{160,64},{192,96},{224,1... | collective-permute-start | bytes 368648 | tf_op jit(solution)/shard_map/ppermute | solution.py:29
  97.8 2.4 %collective-permute-start.15 = (bf16[48,1280]{1,0:T(8,128)(2,1)S(1)}, bf16[48,1280]{1,0:T(8,128)(2,1)S(1)}, u32[]{:S(2)}, u32[]{:S(2)}) collective-permute-start(bf16[48,1280]{1,0:T(8,128)(2,1)S(1)} %get-tuple-element.43), channel_id=1, source_target_pairs={{0,192},{32,224},{64,0},{96,32},{128,64},{160,96},{192,128},{224,1... | collective-permute-start | bytes 368648 | tf_op jit(solution)/shard_map/ppermute | solution.py:29
  100.9 8.2 %collective-permute-done.12.refs_2_ = bf16[48,1280]{1,0:T(8,128)(2,1)S(1)} collective-permute-done((bf16[48,1280]{1,0:T(8,128)(2,1)S(1)}, bf16[48,1280]{1,0:T(8,128)(2,1)S(1)}, u32[]{:S(2)}, u32[]{:S(2)}) %collective-permute-start.12) | collective-permute-done | bytes 122912 | tf_op jit(solution)/shard_map/ppermute | solution.py:29
  109.8 3.4 %collective-permute-done.16.refs_6_ = bf16[48,1280]{1,0:T(8,128)(2,1)S(1)} collective-permute-done((bf16[48,1280]{1,0:T(8,128)(2,1)S(1)}, bf16[48,1280]{1,0:T(8,128)(2,1)S(1)}, u32[]{:S(2)}, u32[]{:S(2)}) %collective-permute-start.16) | collective-permute-done | bytes 122912 | tf_op jit(solution)/shard_map/ppermute | solution.py:29
  113.2 1.6 %collective-permute-done.17.refs_7_ = bf16[48,1280]{1,0:T(8,128)(2,1)S(1)} collective-permute-done((bf16[48,1280]{1,0:T(8,128)(2,1)S(1)}, bf16[48,1280]{1,0:T(8,128)(2,1)S(1)}, u32[]{:S(2)}, u32[]{:S(2)}) %collective-permute-start.17) | collective-permute-done | bytes 122912 | tf_op jit(solution)/shard_map/ppermute | solution.py:29
  118.4 1.5 %collective-permute-start.20 = (bf16[2,6,1280]{2,1,0:T(8,128)(2,1)S(1)}, bf16[2,6,1280]{2,1,0:T(8,128)(2,1)S(1)}, u32[]{:S(2)}, u32[]{:S(2)}) collective-permute-start(bf16[2,6,1280]{2,1,0:T(8,128)(2,1)S(1)} %get-tuple-element.64), channel_id=1, source_target_pairs={{0,2},{1,3},{2,0},{3,1},{4,6},{5,7},{6,4},{7,5},{8,10},{9,11},{10,... | collective-permute-start | bytes 92168 | tf_op jit(solution)/shard_map/ppermute | solution.py:29
  120.0 1.8 %collective-permute-start.21 = (bf16[2,6,1280]{2,1,0:T(8,128)(2,1)S(1)}, bf16[2,6,1280]{2,1,0:T(8,128)(2,1)S(1)}, u32[]{:S(2)}, u32[]{:S(2)}) collective-permute-start(bf16[2,6,1280]{2,1,0:T(8,128)(2,1)S(1)} %get-tuple-element.65), channel_id=1, source_target_pairs={{0,3},{1,0},{2,1},{3,2},{4,7},{5,4},{6,5},{7,6},{8,11},{9,8},{10,9... | collective-permute-start | bytes 92168 | tf_op jit(solution)/shard_map/ppermute | solution.py:29
  125.1 3.4 %collective-permute-start.23 = (bf16[6,4096]{1,0:T(8,128)(2,1)S(1)}, bf16[6,4096]{1,0:T(8,128)(2,1)S(1)}, u32[]{:S(2)}, u32[]{:S(2)}) collective-permute-start(bf16[6,4096]{1,0:T(8,128)(2,1)S(1)} %get-tuple-element.48), channel_id=1, source_target_pairs={{0,2},{1,3},{2,0},{3,1},{4,6},{5,7},{6,4},{7,5},{8,10},{9,11},{10,... | collective-permute-start | bytes 147464 | tf_op jit(solution)/shard_map/ppermute | solution.py:29
  129.0 2.0 %collective-permute-done.23 = bf16[6,4096]{1,0:T(8,128)(2,1)S(1)} collective-permute-done((bf16[6,4096]{1,0:T(8,128)(2,1)S(1)}, bf16[6,4096]{1,0:T(8,128)(2,1)S(1)}, u32[]{:S(2)}, u32[]{:S(2)}) %collective-permute-start.23) | collective-permute-done | bytes 49184 | tf_op jit(solution)/shard_map/ppermute | solution.py:29
  (52 shorter events, 20.1 us)
Async XLA Ops:
  7.9 10.6 %collective-permute-start = (bf16[1536,1024]{1,0:T(8,128)(2,1)S(1)}, bf16[1536,1024]{1,0:T(8,128)(2,1)}, u32[]{:S(2)}, u32[]{:S(2)}) collective-permute-start(bf16[1536,1024]{1,0:T(8,128)(2,1)S(1)} %product_theirs.2), channel_id=1, source_target_pairs={{0,4},{4,0},{1,5},{5,1},{2,6},{6,2},{3,7},{7,3},{8,12},{12,8},{9,1... | collective-permute-start | bytes 9437192 | tf_op jit(solution)/shard_map/ppermute | solution.py:29
  18.4 10.5 %collective-permute-start.7 = (bf16[1536,1024]{1,0:T(8,128)(2,1)S(1)}, bf16[1536,1024]{1,0:T(8,128)(2,1)S(1)}, u32[]{:S(2)}, u32[]{:S(2)}) collective-permute-start(bf16[1536,1024]{1,0:T(8,128)(2,1)S(1)} %product_theirs.3), channel_id=1, source_target_pairs={{0,4},{4,0},{1,5},{5,1},{2,6},{6,2},{3,7},{7,3},{8,12},{12,8},{9,1... | collective-permute-start | bytes 9437192 | tf_op jit(solution)/shard_map/ppermute | solution.py:29
  26.2 20.4 %collective-permute-start.1 = (bf16[1536,256]{1,0:T(8,128)(2,1)S(1)}, bf16[1536,256]{1,0:T(8,128)(2,1)S(1)}, u32[]{:S(2)}, u32[]{:S(2)}) collective-permute-start(bf16[1536,256]{1,0:T(8,128)(2,1)S(1)} %get-tuple-element.27), channel_id=1, source_target_pairs={{0,1},{1,2},{2,3},{3,0},{4,5},{5,6},{6,7},{7,4},{8,9},{9,10},{10,1... | collective-permute-start | bytes 2359304 | tf_op jit(solution)/shard_map/ppermute | solution.py:29
  26.3 20.7 %collective-permute-start.2 = (bf16[1536,256]{1,0:T(8,128)(2,1)S(1)}, bf16[1536,256]{1,0:T(8,128)(2,1)S(1)}, u32[]{:S(2)}, u32[]{:S(2)}) collective-permute-start(bf16[1536,256]{1,0:T(8,128)(2,1)S(1)} %get-tuple-element.28), channel_id=1, source_target_pairs={{0,3},{1,0},{2,1},{3,2},{4,7},{5,4},{6,5},{7,6},{8,11},{9,8},{10,9... | collective-permute-start | bytes 2359304 | tf_op jit(solution)/shard_map/ppermute | solution.py:29
  28.9 33.6 %collective-permute-start.3 = (bf16[1536,256]{1,0:T(8,128)(2,1)S(1)}, bf16[1536,256]{1,0:T(8,128)(2,1)S(1)}, u32[]{:S(2)}, u32[]{:S(2)}) collective-permute-start(bf16[1536,256]{1,0:T(8,128)(2,1)S(1)} %get-tuple-element.29), channel_id=1, source_target_pairs={{0,2},{1,3},{2,0},{3,1},{4,6},{5,7},{6,4},{7,5},{8,10},{9,11},{10,... | collective-permute-start | bytes 2359304 | tf_op jit(solution)/shard_map/ppermute | solution.py:29
  39.0 28.0 %collective-permute-start.10 = (bf16[8,48,1024]{2,1,0:T(8,128)(2,1)S(1)}, bf16[8,48,1024]{2,1,0:T(8,128)(2,1)S(1)}, u32[]{:S(2)}, u32[]{:S(2)}) collective-permute-start(bf16[8,48,1024]{2,1,0:T(8,128)(2,1)S(1)} %get-tuple-element.37), channel_id=1, source_target_pairs={{0,16},{8,24},{16,0},{24,8},{1,17},{9,25},{17,1},{25,9},{2,18},{10... | collective-permute-start | bytes 2359304 | tf_op jit(solution)/shard_map/ppermute | solution.py:29
  41.8 35.1 %collective-permute-start.8 = (bf16[8,48,1024]{2,1,0:T(8,128)(2,1)S(1)}, bf16[8,48,1024]{2,1,0:T(8,128)(2,1)S(1)}, u32[]{:S(2)}, u32[]{:S(2)}) collective-permute-start(bf16[8,48,1024]{2,1,0:T(8,128)(2,1)S(1)} %get-tuple-element.35), channel_id=1, source_target_pairs={{0,8},{8,16},{16,24},{24,0},{1,9},{9,17},{17,25},{25,1},{2,10},{10... | collective-permute-start | bytes 2359304 | tf_op jit(solution)/shard_map/ppermute | solution.py:29
  46.6 30.3 %collective-permute-start.9 = (bf16[8,48,1024]{2,1,0:T(8,128)(2,1)S(1)}, bf16[8,48,1024]{2,1,0:T(8,128)(2,1)S(1)}, u32[]{:S(2)}, u32[]{:S(2)}) collective-permute-start(bf16[8,48,1024]{2,1,0:T(8,128)(2,1)S(1)} %get-tuple-element.36), channel_id=1, source_target_pairs={{0,24},{8,0},{16,8},{24,16},{1,25},{9,1},{17,9},{25,17},{2,26},{10... | collective-permute-start | bytes 2359304 | tf_op jit(solution)/shard_map/ppermute | solution.py:29
  64.3 18.5 %collective-permute-start.4 = (bf16[8,48,256]{2,1,0:T(8,128)(2,1)S(1)}, bf16[8,48,256]{2,1,0:T(8,128)(2,1)S(1)}, u32[]{:S(2)}, u32[]{:S(2)}) collective-permute-start(bf16[8,48,256]{2,1,0:T(8,128)(2,1)S(1)} %get-tuple-element.31), channel_id=1, source_target_pairs={{0,8},{8,16},{16,24},{24,0},{1,9},{9,17},{17,25},{25,1},{2,10},{10... | collective-permute-start | bytes 589832 | tf_op jit(solution)/shard_map/ppermute | solution.py:29
  65.5 17.3 %collective-permute-start.5 = (bf16[8,48,256]{2,1,0:T(8,128)(2,1)S(1)}, bf16[8,48,256]{2,1,0:T(8,128)(2,1)S(1)}, u32[]{:S(2)}, u32[]{:S(2)}) collective-permute-start(bf16[8,48,256]{2,1,0:T(8,128)(2,1)S(1)} %get-tuple-element.32), channel_id=1, source_target_pairs={{0,24},{8,0},{16,8},{24,16},{1,25},{9,1},{17,9},{25,17},{2,26},{10... | collective-permute-start | bytes 589832 | tf_op jit(solution)/shard_map/ppermute | solution.py:29
  67.0 16.6 %collective-permute-start.6 = (bf16[8,48,256]{2,1,0:T(8,128)(2,1)S(1)}, bf16[8,48,256]{2,1,0:T(8,128)(2,1)S(1)}, u32[]{:S(2)}, u32[]{:S(2)}) collective-permute-start(bf16[8,48,256]{2,1,0:T(8,128)(2,1)S(1)} %get-tuple-element.33), channel_id=1, source_target_pairs={{0,16},{8,24},{16,0},{24,8},{1,17},{9,25},{17,1},{25,9},{2,18},{10... | collective-permute-start | bytes 589832 | tf_op jit(solution)/shard_map/ppermute | solution.py:29
  85.2 15.0 %collective-permute-start.11 = (bf16[48,1280]{1,0:T(8,128)(2,1)S(1)}, bf16[48,1280]{1,0:T(8,128)(2,1)S(1)}, u32[]{:S(2)}, u32[]{:S(2)}) collective-permute-start(bf16[48,1280]{1,0:T(8,128)(2,1)S(1)} %get-tuple-element.39), channel_id=1, source_target_pairs={{0,128},{32,160},{64,192},{96,224},{128,0},{160,32},{192,64},{224,... | collective-permute-start | bytes 368648 | tf_op jit(solution)/shard_map/ppermute | solution.py:29
  92.1 17.0 %collective-permute-start.12 = (bf16[48,1280]{1,0:T(8,128)(2,1)S(1)}, bf16[48,1280]{1,0:T(8,128)(2,1)S(1)}, u32[]{:S(2)}, u32[]{:S(2)}) collective-permute-start(bf16[48,1280]{1,0:T(8,128)(2,1)S(1)} %get-tuple-element.40), channel_id=1, source_target_pairs={{0,96},{32,128},{64,160},{96,192},{128,224},{160,0},{192,32},{224,... | collective-permute-start | bytes 368648 | tf_op jit(solution)/shard_map/ppermute | solution.py:29
  93.8 15.3 %collective-permute-start.13 = (bf16[48,1280]{1,0:T(8,128)(2,1)S(1)}, bf16[48,1280]{1,0:T(8,128)(2,1)S(1)}, u32[]{:S(2)}, u32[]{:S(2)}) collective-permute-start(bf16[48,1280]{1,0:T(8,128)(2,1)S(1)} %get-tuple-element.41), channel_id=1, source_target_pairs={{0,160},{32,192},{64,224},{96,0},{128,32},{160,64},{192,96},{224,1... | collective-permute-start | bytes 368648 | tf_op jit(solution)/shard_map/ppermute | solution.py:29
  96.6 12.5 %collective-permute-start.14 = (bf16[48,1280]{1,0:T(8,128)(2,1)S(1)}, bf16[48,1280]{1,0:T(8,128)(2,1)S(1)}, u32[]{:S(2)}, u32[]{:S(2)}) collective-permute-start(bf16[48,1280]{1,0:T(8,128)(2,1)S(1)} %get-tuple-element.42), channel_id=1, source_target_pairs={{0,64},{32,96},{64,128},{96,160},{128,192},{160,224},{192,0},{224,... | collective-permute-start | bytes 368648 | tf_op jit(solution)/shard_map/ppermute | solution.py:29
  97.8 12.0 %collective-permute-start.15 = (bf16[48,1280]{1,0:T(8,128)(2,1)S(1)}, bf16[48,1280]{1,0:T(8,128)(2,1)S(1)}, u32[]{:S(2)}, u32[]{:S(2)}) collective-permute-start(bf16[48,1280]{1,0:T(8,128)(2,1)S(1)} %get-tuple-element.43), channel_id=1, source_target_pairs={{0,192},{32,224},{64,0},{96,32},{128,64},{160,96},{192,128},{224,1... | collective-permute-start | bytes 368648 | tf_op jit(solution)/shard_map/ppermute | solution.py:29
  100.2 13.0 %collective-permute-start.16 = (bf16[48,1280]{1,0:T(8,128)(2,1)S(1)}, bf16[48,1280]{1,0:T(8,128)(2,1)S(1)}, u32[]{:S(2)}, u32[]{:S(2)}) collective-permute-start(bf16[48,1280]{1,0:T(8,128)(2,1)S(1)} %get-tuple-element.44), channel_id=1, source_target_pairs={{0,32},{32,64},{64,96},{96,128},{128,160},{160,192},{192,224},{224... | collective-permute-start | bytes 368648 | tf_op jit(solution)/shard_map/ppermute | solution.py:29
  109.1 5.6 %collective-permute-start.17 = (bf16[48,1280]{1,0:T(8,128)(2,1)S(1)}, bf16[48,1280]{1,0:T(8,128)(2,1)S(1)}, u32[]{:S(2)}, u32[]{:S(2)}) collective-permute-start(bf16[48,1280]{1,0:T(8,128)(2,1)S(1)} %get-tuple-element.45), channel_id=1, source_target_pairs={{0,224},{32,0},{64,32},{96,64},{128,96},{160,128},{192,160},{224,1... | collective-permute-start | bytes 368648 | tf_op jit(solution)/shard_map/ppermute | solution.py:29
  117.9 4.1 %collective-permute-start.19 = (bf16[2,6,1280]{2,1,0:T(8,128)(2,1)S(1)}, bf16[2,6,1280]{2,1,0:T(8,128)(2,1)S(1)}, u32[]{:S(2)}, u32[]{:S(2)}) collective-permute-start(bf16[2,6,1280]{2,1,0:T(8,128)(2,1)S(1)} %get-tuple-element.63), channel_id=1, source_target_pairs={{0,1},{1,2},{2,3},{3,0},{4,5},{5,6},{6,7},{7,4},{8,9},{9,10},{10,1... | collective-permute-start | bytes 92168 | tf_op jit(solution)/shard_map/ppermute | solution.py:29
  118.4 4.4 %collective-permute-start.20 = (bf16[2,6,1280]{2,1,0:T(8,128)(2,1)S(1)}, bf16[2,6,1280]{2,1,0:T(8,128)(2,1)S(1)}, u32[]{:S(2)}, u32[]{:S(2)}) collective-permute-start(bf16[2,6,1280]{2,1,0:T(8,128)(2,1)S(1)} %get-tuple-element.64), channel_id=1, source_target_pairs={{0,2},{1,3},{2,0},{3,1},{4,6},{5,7},{6,4},{7,5},{8,10},{9,11},{10,... | collective-permute-start | bytes 92168 | tf_op jit(solution)/shard_map/ppermute | solution.py:29
  120.0 3.4 %collective-permute-start.21 = (bf16[2,6,1280]{2,1,0:T(8,128)(2,1)S(1)}, bf16[2,6,1280]{2,1,0:T(8,128)(2,1)S(1)}, u32[]{:S(2)}, u32[]{:S(2)}) collective-permute-start(bf16[2,6,1280]{2,1,0:T(8,128)(2,1)S(1)} %get-tuple-element.65), channel_id=1, source_target_pairs={{0,3},{1,0},{2,1},{3,2},{4,7},{5,4},{6,5},{7,6},{8,11},{9,8},{10,9... | collective-permute-start | bytes 92168 | tf_op jit(solution)/shard_map/ppermute | solution.py:29
  124.3 4.7 %collective-permute-start.22 = (bf16[6,4096]{1,0:T(8,128)(2,1)S(1)}, bf16[6,4096]{1,0:T(8,128)(2,1)S(1)}, u32[]{:S(2)}, u32[]{:S(2)}) collective-permute-start(bf16[6,4096]{1,0:T(8,128)(2,1)S(1)} %get-tuple-element.48), channel_id=1, source_target_pairs={{0,1},{1,2},{2,3},{3,0},{4,5},{5,6},{6,7},{7,4},{8,9},{9,10},{10,1... | collective-permute-start | bytes 147464 | tf_op jit(solution)/shard_map/ppermute | solution.py:29
  125.1 5.9 %collective-permute-start.23 = (bf16[6,4096]{1,0:T(8,128)(2,1)S(1)}, bf16[6,4096]{1,0:T(8,128)(2,1)S(1)}, u32[]{:S(2)}, u32[]{:S(2)}) collective-permute-start(bf16[6,4096]{1,0:T(8,128)(2,1)S(1)} %get-tuple-element.48), channel_id=1, source_target_pairs={{0,2},{1,3},{2,0},{3,1},{4,6},{5,7},{6,4},{7,5},{8,10},{9,11},{10,... | collective-permute-start | bytes 147464 | tf_op jit(solution)/shard_map/ppermute | solution.py:29
  128.6 4.0 %collective-permute-start.24 = (bf16[6,4096]{1,0:T(8,128)(2,1)S(1)}, bf16[6,4096]{1,0:T(8,128)(2,1)S(1)}, u32[]{:S(2)}, u32[]{:S(2)}) collective-permute-start(bf16[6,4096]{1,0:T(8,128)(2,1)S(1)} %get-tuple-element.48), channel_id=1, source_target_pairs={{0,3},{1,0},{2,1},{3,2},{4,7},{5,4},{6,5},{7,6},{8,11},{9,8},{10,9... | collective-permute-start | bytes 147464 | tf_op jit(solution)/shard_map/ppermute | solution.py:29
  (5 other events, 181.7 us)

commit v2 on v1

--- a/solution.py
+++ b/solution.py
@@ -11,10 +11,10 @@
 TN = 256
 BLK = D // (NZ * NX)
 FLOW_C = 1024
-FLOW_B = 1024
+FLOW_A = 1024
 T = 1024
 F32, BF16 = jnp.float32, jnp.bfloat16
-VMEM_LIMIT = 48 * 1024 * 1024
+VMEM_LIMIT = 62 * 1024 * 1024
 DN = (((0,), (0,)), ((), ()))
 
 
@@ -30,6 +30,8 @@
 
 
 def product(acts, cot, idx, base, ncols):
+    tn = 2 * TN
+
     def kernel(idx_ref, a, c, o):
         o[...] = lax.dot_general(a[...], c[...], DN, preferred_element_type=F32).astype(BF16)
 
@@ -37,17 +39,42 @@
         kernel,
         grid_spec=pltpu.PrefetchScalarGridSpec(
             num_scalar_prefetch=1,
-            grid=(ncols // TN,),
+            grid=(ncols // tn,),
             in_specs=[
                 pl.BlockSpec((T, D), lambda j, s: (0, 0)),
-                pl.BlockSpec((T, TN), lambda j, s: (0, (1 - s[0]) * (HALF // TN) + base // TN + j)),
+                pl.BlockSpec((T, tn), lambda j, s: (0, (1 - s[0]) * (HALF // tn) + base // tn + j)),
             ],
-            out_specs=pl.BlockSpec((D, TN), lambda j, s: (0, j)),
+            out_specs=pl.BlockSpec((D, tn), lambda j, s: (0, j)),
         ),
         out_shape=jax.ShapeDtypeStruct((D, ncols), BF16),
         name="product_theirs",
         **params_of(2 * T * D * ncols, 2 * (T * D + T * ncols + D * ncols)),
     )(idx, acts, cot)
+
+
+def product_for_z(acts, cot, got, idx, base, ncols):
+    tn = 2 * TN
+
+    def kernel(idx_ref, a, c, r, o):
+        acc = lax.dot_general(a[...], c[...], DN, preferred_element_type=F32) + r[...].astype(F32)
+        o[...] = acc.astype(BF16)
+
+    return pl.pallas_call(
+        kernel,
+        grid_spec=pltpu.PrefetchScalarGridSpec(
+            num_scalar_prefetch=1,
+            grid=(ncols // tn,),
+            in_specs=[
+                pl.BlockSpec((T, D), lambda j, s: (0, 0)),
+                pl.BlockSpec((T, tn), lambda j, s: (0, s[0] * (HALF // tn) + base // tn + j)),
+                pl.BlockSpec((D, tn), lambda j, s: (0, j)),
+            ],
+            out_specs=pl.BlockSpec((D, tn), lambda j, s: (0, j)),
+        ),
+        out_shape=jax.ShapeDtypeStruct((D, ncols), BF16),
+        name="product_for_z",
+        **params_of(2 * T * D * ncols, 2 * (T * D + T * ncols + 2 * D * ncols)),
+    )(idx, acts, cot, got)
 
 
 def product_for_y(acts, cot, got, idx, base):
@@ -77,35 +104,6 @@
     )(idx, acts, cot, got)
 
 
-def product_for_x(acts, cot, got, idx, base, ncols):
-    def kernel(idx_ref, a, c, r, *rest):
-        outs, acc = rest[:NX], rest[NX]
-        acc[...] = lax.dot_general(a[...], c[...], DN, preferred_element_type=F32) + r[...].astype(F32)
-        for o in range(NX):
-            target = lax.rem(idx_ref[1] + o, NX)
-            for z in range(NZ):
-                rows = pl.ds(pl.multiple_of((z * NX + target) * BLK, BLK), BLK)
-                outs[o][z] = acc[rows, :].astype(BF16)
-
-    return pl.pallas_call(
-        kernel,
-        grid_spec=pltpu.PrefetchScalarGridSpec(
-            num_scalar_prefetch=1,
-            grid=(ncols // TN,),
-            in_specs=[
-                pl.BlockSpec((T, D), lambda j, s: (0, 0)),
-                pl.BlockSpec((T, TN), lambda j, s: (0, s[0] * (HALF // TN) + base // TN + j)),
-                pl.BlockSpec((D, TN), lambda j, s: (0, j)),
-            ],
-            out_specs=[pl.BlockSpec((NZ, BLK, TN), lambda j, s: (0, 0, j))] * NX,
-            scratch_shapes=[pltpu.VMEM((D, TN), F32)],
-        ),
-        out_shape=[jax.ShapeDtypeStruct((NZ, BLK, ncols), BF16)] * NX,
-        name="product_for_x",
-        **params_of(2 * T * D * ncols, 2 * (T * D + T * ncols + 2 * D * ncols)),
-    )(idx, acts, cot, got)
-
-
 def sum_for_x(parts, idx):
     width = parts[0].shape[-1]
 
@@ -134,85 +132,83 @@
     )(idx, *[p.reshape(NZ, NX, BLK, width) for p in parts])
 
 
-def sum_for_z(first, second, idx):
+def sum_for_z(parts, idx):
+    width = parts[0].shape[-1]
+
+    def kernel(idx_ref, *refs):
+        ins, outs = refs[:NX], refs[NX:]
+        for o in range(NZ):
+            z = lax.rem(idx_ref[3] + o, NZ)
+            total = ins[0][z].astype(F32)
+            for r in ins[1:]:
+                total = total + r[z].astype(F32)
+            outs[o][...] = total.astype(BF16)
+
+    return pl.pallas_call(
+        kernel,
+        grid_spec=pltpu.PrefetchScalarGridSpec(
+            num_scalar_prefetch=1,
+            grid=(1,),
+            in_specs=[pl.BlockSpec((NZ, BLK, width), lambda j, s: (0, 0, 0))] * NX,
+            out_specs=[pl.BlockSpec((BLK, width), lambda j, s: (0, 0))] * NZ,
+        ),
+        out_shape=[jax.ShapeDtypeStruct((BLK, width), BF16)] * NZ,
+        name="sum_for_z",
+        **params_of(4 * NZ * BLK * width, 10 * NZ * BLK * width),
+    )(idx, *parts)
+
+
+def sum_for_core(first, second, idx):
     wa, wb = first[0].shape[-1], second[0].shape[-1]
+    width = wa + wb
+    count = len(first) + len(second)
+    rows = BLK // NC
 
     def kernel(idx_ref, *refs):
-        ins, outs = refs[: 2 * NX], refs[2 * NX :]
-        sums = []
-        for group in (ins[:NX], ins[NX:]):
-            total = group[0][0].astype(F32)
+        mine, theirs, acc = refs[count:]
+        for group, columns in ((refs[: len(first)], slice(0, wa)), (refs[len(first) : count], slice(wa, width))):
+            total = group[0][...].astype(F32)
             for r in group[1:]:
-                total = total + r[0].astype(F32)
-            sums.append(total.astype(BF16))
-        for o in range(NZ):
-
-            @pl.when(pl.program_id(0) == o)
-            def _():
-                outs[o][:, :wa] = sums[0]
-                outs[o][:, wa:] = sums[1]
-
-    spec = lambda w: pl.BlockSpec((1, BLK, w), lambda j, s: (lax.rem(s[3] + j, NZ), 0, 0))
-    return pl.pallas_call(
-        kernel,
-        grid_spec=pltpu.PrefetchScalarGridSpec(
-            num_scalar_prefetch=1,
-            grid=(NZ,),
-            in_specs=[spec(wa)] * NX + [spec(wb)] * NX,
-            out_specs=[pl.BlockSpec((BLK, wa + wb), lambda j, s: (0, 0))] * NZ,
-        ),
-        out_shape=[jax.ShapeDtypeStruct((BLK, wa + wb), BF16)] * NZ,
-        name="sum_for_z",
-        **params_of(4 * NZ * BLK * (wa + wb), 2 * 5 * NZ * BLK * (wa + wb)),
-    )(idx, *first, *second)
-
-
-def sum_for_core(parts, idx):
-    width = parts[0].shape[-1]
-    rows = BLK // NC
-
-    def kernel(idx_ref, *refs):
-        ins, mine, theirs, acc = refs[:NZ], refs[NZ], refs[NZ + 1], refs[NZ + 2]
-        total = ins[0][...].astype(F32)
-        for r in ins[1:]:
-            total = total + r[...].astype(F32)
-        acc[...] = total
+                total = total + r[...].astype(F32)
+            acc[:, columns] = total
         c = idx_ref[0]
         mine[...] = acc[pl.ds(pl.multiple_of(c * rows, rows), rows), :].astype(BF16)
         theirs[...] = acc[pl.ds(pl.multiple_of((1 - c) * rows, rows), rows), :].astype(BF16)
 
-    whole = lambda h: pl.BlockSpec((h, width), lambda j, s: (0, 0))
+    whole = lambda h, w: pl.BlockSpec((h, w), lambda j, s: (0, 0))
     return pl.pallas_call(
         kernel,
         grid_spec=pltpu.PrefetchScalarGridSpec(
             num_scalar_prefetch=1,
             grid=(1,),
-            in_specs=[whole(BLK)] * NZ,
-            out_specs=[whole(rows)] * NC,
+            in_specs=[whole(BLK, wa)] * len(first) + [whole(BLK, wb)] * len(second),
+            out_specs=[whole(rows, width)] * NC,
             scratch_shapes=[pltpu.VMEM((BLK, width), F32)],
         ),
         out_shape=[jax.ShapeDtypeStruct((rows, width), BF16)] * NC,
         name="sum_for_core",
         **params_of(NZ * BLK * width, 2 * 9 * BLK * width),
-    )(idx, *parts)
+    )(idx, *first, *second)
 
 
 def body(acts, cotangent, master, moment, second):
     z, x, c, y = (lax.axis_index(a) for a in ("z", "x", "c", "y"))
     idx = jnp.stack([c, x, y, z]).astype(jnp.int32)
+    theirs_a = product(acts, cotangent, idx, FLOW_C, FLOW_A)
+    got_a = shift(theirs_a, "c", NC, 1)
     theirs_c = product(acts, cotangent, idx, 0, FLOW_C)
     got_c = shift(theirs_c, "c", NC, 1)
-    theirs_b = product(acts, cotangent, idx, FLOW_C, FLOW_B)
-    got_b = shift(theirs_b, "c", NC, 1)
+    part_a = product_for_z(acts, cotangent, got_a, idx, FLOW_C, FLOW_A)
+    part_a = lax.psum_scatter(part_a, "z", scatter_dimension=0, tiled=True).reshape(NX, BLK, FLOW_A)
     pieces_c = product_for_y(acts, cotangent, got_c, idx, 0)
     over_y = [pieces_c[0]] + [shift(pieces_c[s], "y", NY, s) for s in (1, 3, 2)]
-    pieces_b = product_for_x(acts, cotangent, got_b, idx, FLOW_C, FLOW_B)
-    over_x = [pieces_b[0]] + [shift(pieces_b[s], "x", NX, s) for s in (1, 3, 2)]
     pieces_cx = sum_for_x(over_y, idx)
     over_cx = [pieces_cx[0]] + [shift(pieces_cx[s], "x", NX, s) for s in (1, 3, 2)]
-    pieces_z = sum_for_z(over_cx, over_x, idx)
+    pieces_z = sum_for_z(over_cx, idx)
     over_z = [pieces_z[0]] + [shift(pieces_z[s], "z", NZ, s) for s in (4, 3, 5, 2, 6, 1, 7)]
-    mine, theirs = sum_for_core(over_z, idx)
+    piece_a = lambda s: lax.dynamic_index_in_dim(part_a, lax.rem(x + s, NX), 0, keepdims=False)
+    over_ax = [piece_a(0)] + [shift(piece_a(s), "x", NX, s) for s in (1, 3, 2)]
+    mine, theirs = sum_for_core(over_z, over_ax, idx)
     got = shift(theirs, "c", NC, 1)
     pair = jnp.stack([jnp.where(c == 0, mine, got), jnp.where(c == 0, got, mine)])
     rows = BLK // NC // NY

time: 134 us -> 175 us (1.31); the launches traced: 133 us -> 172 us
  between operations: 0.83 us -> 14.2 us
  Pallas kernels: 34.4 us -> 43.5 us
  waiting for transfers between devices: 55.4 us -> 64.2 us
  starting transfers between devices: 39.2 us -> 44.2 us
    ppermute x25, waiting for transfers between devices: 55.4 us -> 64.2 us  [shift(): return lax.ppermute(v, axis, [(i, (i + s) % n) for i in range(n)])]
    ppermute x25, starting transfers between devices: 39.2 us -> 44.1 us  [shift(): return lax.ppermute(v, axis, [(i, (i + s) % n) for i in range(n)])]
    pallas_call x1, Pallas kernels: 1.71 us -> 4.79 us  [sum_for_x(): pl.pallas_call(kernel, grid_spec=pltpu.PrefetchScalarGridSpec(num_scalar_...]
    pallas_call x1, Pallas kernels: 7.63 us -> 9.47 us  [product_for_y(): pl.pallas_call(kernel, grid_spec=pltpu.PrefetchScalarGridSpec(num_scalar_...]
    pallas_call x1, Pallas kernels: 0.73 us -> 2.57 us  [sum_for_core(): pl.pallas_call(kernel, grid_spec=pltpu.PrefetchScalarGridSpec(num_scalar_...]
  transfers between devices with their start and end apart: 25 -> 26, of which waited for: 16 -> 18; matrix products, arithmetic and copies ran while one was open for 0% -> 1% of each run, Pallas kernels for 19% -> 14%
where the time goes in v2:
time: 175 us; the launch traced here: 172 us
  waiting for transfers between devices  64.2 us (37%)
  starting transfers between devices  44.2 us (25%)
  Pallas kernels  43.5 us (25%)
  between operations  14.2 us (8%)
  other arithmetic  3.24 us (2%)
  local copies, waits for them, and re-layouts  3.04 us (2%)
    ppermute x25, waiting for transfers between devices, shift(): return lax.ppermute(v, axis, [(i, (i + s) % n) for i in range(n)])  64.2 us
    ppermute x25, starting transfers between devices, shift(): return lax.ppermute(v, axis, [(i, (i + s) % n) for i in range(n)])  44.1 us
    pallas_call x2, Pallas kernels, product(): pl.pallas_call(kernel, grid_spec=pltpu.PrefetchScalarGridSpec(num_scalar_...  15.7 us
    pallas_call x1, Pallas kernels, product_for_y(): pl.pallas_call(kernel, grid_spec=pltpu.PrefetchScalarGridSpec(num_scalar_...  9.47 us
    pallas_call x1, Pallas kernels, product_for_z(): pl.pallas_call(kernel, grid_spec=pltpu.PrefetchScalarGridSpec(num_scalar_...  8.35 us
    pallas_call x1, Pallas kernels, sum_for_x(): pl.pallas_call(kernel, grid_spec=pltpu.PrefetchScalarGridSpec(num_scalar_...  4.79 us
  transfers between devices with their start and end apart: 26, of which 18 were waited for; matrix products, arithmetic and copies ran while one was open for 1% of the time, Pallas kernels for 14%

profile of v2, /device:TPU:1, one launch (start us, length us, event | category | flops | bytes accessed | tf_op | source)
XLA Modules:
  0.0 172.4 jit_solution(10932599994967767016)
XLA Ops:
  7.8 7.9 %product_theirs.3 = bf16[1536,1024]{1,0:T(8,128)(2,1)} custom-call(s32[4]{0:T(128)} %pad_add_fusion.idx_ref, bf16[1024,1536]{1,0:T(8,128)(2,1)} %a.7, bf16[1024,4096]{1,0:T(8,128)(2,1)} %c.7), custom_call_target="tpu_custom_call" | custom-call | flops 3221225472 | bytes 8388608 | tf_op jit(solution)/shard_map/product_theirs/pallas_call | solution.py:38
  15.7 3.2 %collective-permute-start.14 = (bf16[1536,1024]{1,0:T(8,128)(2,1)}, bf16[1536,1024]{1,0:T(8,128)(2,1)}, u32[]{:S(2)}, u32[]{:S(2)}) collective-permute-start(bf16[1536,1024]{1,0:T(8,128)(2,1)} %product_theirs.3), channel_id=1, source_target_pairs={{0,4},{4,0},{1,5},{5,1},{2,6},{6,2},{3,7},{7,3},{8,12},{12,8},{9,1... | collective-permute-start | bytes 9437192 | tf_op jit(solution)/shard_map/ppermute | solution.py:29
  18.9 5.6 %collective-permute-done.14.r = bf16[1536,1024]{1,0:T(8,128)(2,1)} collective-permute-done((bf16[1536,1024]{1,0:T(8,128)(2,1)}, bf16[1536,1024]{1,0:T(8,128)(2,1)}, u32[]{:S(2)}, u32[]{:S(2)}) %collective-permute-start.14) | collective-permute-done | bytes 3145760 | tf_op jit(solution)/shard_map/ppermute | solution.py:29
  24.6 8.3 %product_for_z.1 = bf16[1536,1024]{1,0:T(8,128)(2,1)} custom-call(s32[4]{0:T(128)} %pad_add_fusion.idx_ref, bf16[1024,1536]{1,0:T(8,128)(2,1)} %a.7, bf16[1024,4096]{1,0:T(8,128)(2,1)} %c.7, bf16[1536,1024]{1,0:T(8,128)(2,1)} %collective-permute-done.14.r), custom_call_target="tpu_custom_call" | custom-call | flops 3221225472 | bytes 11534336 | tf_op jit(solution)/shard_map/product_for_z/pallas_call | solution.py:62
  32.9 7.9 %product_theirs.2 = bf16[1536,1024]{1,0:T(8,128)(2,1)} custom-call(s32[4]{0:T(128)} %pad_add_fusion.idx_ref, bf16[1024,1536]{1,0:T(8,128)(2,1)} %a.7, bf16[1024,4096]{1,0:T(8,128)(2,1)} %c.7), custom_call_target="tpu_custom_call" | custom-call | flops 3221225472 | bytes 8388608 | tf_op jit(solution)/shard_map/product_theirs/pallas_call | solution.py:38
  41.2 5.6 %collective-permute-done.r = bf16[1536,1024]{1,0:T(8,128)(2,1)} collective-permute-done((bf16[1536,1024]{1,0:T(8,128)(2,1)}, bf16[1536,1024]{1,0:T(8,128)(2,1)}, u32[]{:S(2)}, u32[]{:S(2)}) %collective-permute-start) | collective-permute-done | bytes 3145760 | tf_op jit(solution)/shard_map/ppermute | solution.py:29
  46.8 9.5 %product_for_y.1 = (bf16[1536,256]{1,0:T(8,128)(2,1)}, bf16[1536,256]{1,0:T(8,128)(2,1)}, bf16[1536,256]{1,0:T(8,128)(2,1)}, bf16[1536,256]{1,0:T(8,128)(2,1)}) custom-call(s32[4]{0:T(128)} %pad_add_fusion.idx_ref, bf16[1024,1536]{1,0:T(8,128)(2,1)} %a.7, bf16[1024,4096]{1,0:T(8,128)(2,1)} %c.7, bf16[1536,1024]{1,0:T(8,128)(2,1)} %collective-permute-done.r), custom_call_target="tpu_custom_call" | custom-call | flops 3221225472 | bytes 11534336 | tf_op jit(solution)/shard_map/product_for_y/pallas_call | solution.py:89
  56.3 2.7 %collective-permute-start.2 = (bf16[1536,256]{1,0:T(8,128)(2,1)}, bf16[1536,256]{1,0:T(8,128)(2,1)S(1)}, u32[]{:S(2)}, u32[]{:S(2)}) collective-permute-start(bf16[1536,256]{1,0:T(8,128)(2,1)} %get-tuple-element.24), channel_id=1, source_target_pairs={{0,3},{1,0},{2,1},{3,2},{4,7},{5,4},{6,5},{7,6},{8,11},{9,8},{10,9... | collective-permute-start | bytes 2359304 | tf_op jit(solution)/shard_map/ppermute | solution.py:29
  58.9 18.0 %collective-permute-done.1 = bf16[1536,256]{1,0:T(8,128)(2,1)S(1)} collective-permute-done((bf16[1536,256]{1,0:T(8,128)(2,1)}, bf16[1536,256]{1,0:T(8,128)(2,1)S(1)}, u32[]{:S(2)}, u32[]{:S(2)}) %collective-permute-start.1) | collective-permute-done | bytes 786464 | tf_op jit(solution)/shard_map/ppermute | solution.py:29
  77.0 16.0 %collective-permute-done.3 = bf16[1536,256]{1,0:T(8,128)(2,1)} collective-permute-done((bf16[1536,256]{1,0:T(8,128)(2,1)}, bf16[1536,256]{1,0:T(8,128)(2,1)}, u32[]{:S(2)}, u32[]{:S(2)}) %collective-permute-start.3) | collective-permute-done | bytes 786464 | tf_op jit(solution)/shard_map/ppermute | solution.py:29
  93.0 4.8 %sum_for_x.1 = (bf16[8,48,256]{2,1,0:T(8,128)(2,1)}, bf16[8,48,256]{2,1,0:T(8,128)(2,1)}, bf16[8,48,256]{2,1,0:T(8,128)(2,1)}, bf16[8,48,256]{2,1,0:T(8,128)(2,1)}) custom-call(s32[4]{0:T(128)} %pad_add_fusion.idx_ref, bf16[8,4,48,256]{3,2,1,0:T(8,128)(2,1)} %bitcast.25, bf16[8,4,48,256]{3,2,1,0:T(8,128)(2,1)} %bitcast.26, bf16[8,4,48,256]{3,2,1,0:T(8,128)(2,1)} %bitcast.27, ...), custom_call_target="tpu_custom_call" | custom-call | flops 1572864 | bytes 3932160 | tf_op jit(solution)/shard_map/sum_for_x/pallas_call | solution.py:121
  102.0 1.8 %collective-permute-done.4.refs_1_ = bf16[8,48,256]{2,1,0:T(8,128)(2,1)S(1)} collective-permute-done((bf16[8,48,256]{2,1,0:T(8,128)(2,1)}, bf16[8,48,256]{2,1,0:T(8,128)(2,1)S(1)}, u32[]{:S(2)}, u32[]{:S(2)}) %collective-permute-start.4) | collective-permute-done | bytes 196640 | tf_op jit(solution)/shard_map/ppermute | solution.py:29
  104.0 5.6 %collective-permute-done.6.refs_3_ = bf16[8,48,256]{2,1,0:T(8,128)(2,1)S(1)} collective-permute-done((bf16[8,48,256]{2,1,0:T(8,128)(2,1)}, bf16[8,48,256]{2,1,0:T(8,128)(2,1)S(1)}, u32[]{:S(2)}, u32[]{:S(2)}) %collective-permute-start.6) | collective-permute-done | bytes 196640 | tf_op jit(solution)/shard_map/ppermute | solution.py:29
  110.3 2.6 %sum_for_z.1 = (bf16[48,256]{1,0:T(8,128)(2,1)}, bf16[48,256]{1,0:T(8,128)(2,1)}, bf16[48,256]{1,0:T(8,128)(2,1)}, bf16[48,256]{1,0:T(8,128)(2,1)}, bf16[48,256]...) custom-call(s32[4]{0:T(128)} %pad_add_fusion.idx_ref, ...), custom_call_target="tpu_custom_call" | custom-call | flops 393216 | bytes 983040 | tf_op jit(solution)/shard_map/sum_for_z/pallas_call | solution.py:147
  112.9 3.1 %collective-permute-start.10 = (bf16[48,256]{1,0:T(8,128)(2,1)}, bf16[48,256]{1,0:T(8,128)(2,1)S(1)}, u32[]{:S(2)}, u32[]{:S(2)}) collective-permute-start(bf16[48,256]{1,0:T(8,128)(2,1)} %get-tuple-element.34), channel_id=1, source_target_pairs={{0,64},{32,96},{64,128},{96,160},{128,192},{160,224},{192,0},{224,... | collective-permute-start | bytes 73736 | tf_op jit(solution)/shard_map/ppermute | solution.py:29
  116.0 1.7 dynamic-slice_bitcast_fusion
  118.3 2.1 %collective-permute-start.16 = (bf16[48,1024]{1,0:T(8,128)(2,1)S(1)}, bf16[48,1024]{1,0:T(8,128)(2,1)S(1)}, u32[]{:S(2)}, u32[]{:S(2)}) collective-permute-start(bf16[48,1024]{1,0:T(8,128)(2,1)S(1)} %get-tuple-element.45), channel_id=1, source_target_pairs={{0,24},{8,0},{16,8},{24,16},{1,25},{9,1},{17,9},{25,17},{2,26},{10... | collective-permute-start | bytes 294920 | tf_op jit(solution)/shard_map/ppermute | solution.py:29
  120.4 3.2 %collective-permute-start.11 = (bf16[48,256]{1,0:T(8,128)(2,1)}, bf16[48,256]{1,0:T(8,128)(2,1)S(1)}, u32[]{:S(2)}, u32[]{:S(2)}) collective-permute-start(bf16[48,256]{1,0:T(8,128)(2,1)} %get-tuple-element.35), channel_id=1, source_target_pairs={{0,192},{32,224},{64,0},{96,32},{128,64},{160,96},{192,128},{224,1... | collective-permute-start | bytes 73736 | tf_op jit(solution)/shard_map/ppermute | solution.py:29
  124.3 2.2 %collective-permute-done.11.refs_5_ = bf16[48,256]{1,0:T(8,128)(2,1)S(1)} collective-permute-done((bf16[48,256]{1,0:T(8,128)(2,1)}, bf16[48,256]{1,0:T(8,128)(2,1)S(1)}, u32[]{:S(2)}, u32[]{:S(2)}) %collective-permute-start.11) | collective-permute-done | bytes 24608 | tf_op jit(solution)/shard_map/ppermute | solution.py:29
  128.1 4.4 %collective-permute-start.7 = (bf16[48,256]{1,0:T(8,128)(2,1)}, bf16[48,256]{1,0:T(8,128)(2,1)S(1)}, u32[]{:S(2)}, u32[]{:S(2)}) collective-permute-start(bf16[48,256]{1,0:T(8,128)(2,1)} %get-tuple-element.31), channel_id=1, source_target_pairs={{0,128},{32,160},{64,192},{96,224},{128,0},{160,32},{192,64},{224,... | collective-permute-start | bytes 73736 | tf_op jit(solution)/shard_map/ppermute | solution.py:29
  134.9 3.0 %collective-permute-start.9 = (bf16[48,256]{1,0:T(8,128)(2,1)}, bf16[48,256]{1,0:T(8,128)(2,1)S(1)}, u32[]{:S(2)}, u32[]{:S(2)}) collective-permute-start(bf16[48,256]{1,0:T(8,128)(2,1)} %get-tuple-element.33), channel_id=1, source_target_pairs={{0,160},{32,192},{64,224},{96,0},{128,32},{160,64},{192,96},{224,1... | collective-permute-start | bytes 73736 | tf_op jit(solution)/shard_map/ppermute | solution.py:29
  140.6 2.6 %sum_for_core.1 = (bf16[24,1280]{1,0:T(8,128)(2,1)}, bf16[24,1280]{1,0:T(8,128)(2,1)}) custom-call(s32[4]{0:T(128)} %pad_add_fusion.idx_ref, bf16[48,256]{1,0:T(8,128)(2,1)} %get-tuple-element.30.refs_0_, bf16[48,256]{1,0:T(8,128)(2,1)} %copy-done.15, bf16[48,256]{1,0:T(8,128)(2,1)} %copy-done.16, bf16[48,256]{1,0:T(8,128)(2,1)} %copy-done.17, ...), custom_call_target="tpu_custom_call" | custom-call | flops 491520 | bytes 1105920 | tf_op jit(solution)/shard_map/sum_for_core/pallas_call | solution.py:179
  143.2 6.4 %collective-permute-start.18 = (bf16[24,1280]{1,0:T(8,128)(2,1)}, bf16[24,1280]{1,0:T(8,128)(2,1)S(1)}, u32[]{:S(2)}, u32[]{:S(2)}) collective-permute-start(bf16[24,1280]{1,0:T(8,128)(2,1)} %get-tuple-element.39), channel_id=1, source_target_pairs={{0,4},{4,0},{1,5},{5,1},{2,6},{6,2},{3,7},{7,3},{8,12},{12,8},{9,1... | collective-permute-start | bytes 184328 | tf_op jit(solution)/shard_map/ppermute | solution.py:29
  159.3 2.0 %collective-permute-start.23 = (bf16[6,4096]{1,0:T(8,128)(2,1)S(1)}, bf16[6,4096]{1,0:T(8,128)(2,1)S(1)}, u32[]{:S(2)}, u32[]{:S(2)}) collective-permute-start(bf16[6,4096]{1,0:T(8,128)(2,1)S(1)} %get-tuple-element.40), channel_id=1, source_target_pairs={{0,2},{1,3},{2,0},{3,1},{4,6},{5,7},{6,4},{7,5},{8,10},{9,11},{10,... | collective-permute-start | bytes 147464 | tf_op jit(solution)/shard_map/ppermute | solution.py:29
  (84 shorter events, 28.0 us)
Async XLA Ops:
  7.2 108.8 %reduce-scatter.2.cloned.1.call-start = ((), (), s32[]{:S(2)}) async-start(), calls=%async_computation.1 | async-start | bytes 3538944 | tf_op jit(solution)/shard_map/reduce_scatter | solution.py:202
  15.7 8.9 %collective-permute-start.14 = (bf16[1536,1024]{1,0:T(8,128)(2,1)}, bf16[1536,1024]{1,0:T(8,128)(2,1)}, u32[]{:S(2)}, u32[]{:S(2)}) collective-permute-start(bf16[1536,1024]{1,0:T(8,128)(2,1)} %product_theirs.3), channel_id=1, source_target_pairs={{0,4},{4,0},{1,5},{5,1},{2,6},{6,2},{3,7},{7,3},{8,12},{12,8},{9,1... | collective-permute-start | bytes 9437192 | tf_op jit(solution)/shard_map/ppermute | solution.py:29
  40.8 6.0 %collective-permute-start = (bf16[1536,1024]{1,0:T(8,128)(2,1)}, bf16[1536,1024]{1,0:T(8,128)(2,1)}, u32[]{:S(2)}, u32[]{:S(2)}) collective-permute-start(bf16[1536,1024]{1,0:T(8,128)(2,1)} %product_theirs.2), channel_id=1, source_target_pairs={{0,4},{4,0},{1,5},{5,1},{2,6},{6,2},{3,7},{7,3},{8,12},{12,8},{9,1... | collective-permute-start | bytes 9437192 | tf_op jit(solution)/shard_map/ppermute | solution.py:29
  56.3 20.7 %collective-permute-start.1 = (bf16[1536,256]{1,0:T(8,128)(2,1)}, bf16[1536,256]{1,0:T(8,128)(2,1)S(1)}, u32[]{:S(2)}, u32[]{:S(2)}) collective-permute-start(bf16[1536,256]{1,0:T(8,128)(2,1)} %get-tuple-element.23), channel_id=1, source_target_pairs={{0,1},{1,2},{2,3},{3,0},{4,5},{5,6},{6,7},{7,4},{8,9},{9,10},{10,1... | collective-permute-start | bytes 2359304 | tf_op jit(solution)/shard_map/ppermute | solution.py:29
  56.3 20.7 %collective-permute-start.2 = (bf16[1536,256]{1,0:T(8,128)(2,1)}, bf16[1536,256]{1,0:T(8,128)(2,1)S(1)}, u32[]{:S(2)}, u32[]{:S(2)}) collective-permute-start(bf16[1536,256]{1,0:T(8,128)(2,1)} %get-tuple-element.24), channel_id=1, source_target_pairs={{0,3},{1,0},{2,1},{3,2},{4,7},{5,4},{6,5},{7,6},{8,11},{9,8},{10,9... | collective-permute-start | bytes 2359304 | tf_op jit(solution)/shard_map/ppermute | solution.py:29
  58.9 34.0 %collective-permute-start.3 = (bf16[1536,256]{1,0:T(8,128)(2,1)}, bf16[1536,256]{1,0:T(8,128)(2,1)}, u32[]{:S(2)}, u32[]{:S(2)}) collective-permute-start(bf16[1536,256]{1,0:T(8,128)(2,1)} %get-tuple-element.25), channel_id=1, source_target_pairs={{0,2},{1,3},{2,0},{3,1},{4,6},{5,7},{6,4},{7,5},{8,10},{9,11},{10,... | collective-permute-start | bytes 2359304 | tf_op jit(solution)/shard_map/ppermute | solution.py:29
  97.8 5.9 %collective-permute-start.4 = (bf16[8,48,256]{2,1,0:T(8,128)(2,1)}, bf16[8,48,256]{2,1,0:T(8,128)(2,1)S(1)}, u32[]{:S(2)}, u32[]{:S(2)}) collective-permute-start(bf16[8,48,256]{2,1,0:T(8,128)(2,1)} %get-tuple-element.27), channel_id=1, source_target_pairs={{0,8},{8,16},{16,24},{24,0},{1,9},{9,17},{17,25},{25,1},{2,10},{10... | collective-permute-start | bytes 589832 | tf_op jit(solution)/shard_map/ppermute | solution.py:29
  99.0 5.1 %collective-permute-start.5 = (bf16[8,48,256]{2,1,0:T(8,128)(2,1)}, bf16[8,48,256]{2,1,0:T(8,128)(2,1)S(1)}, u32[]{:S(2)}, u32[]{:S(2)}) collective-permute-start(bf16[8,48,256]{2,1,0:T(8,128)(2,1)} %get-tuple-element.28), channel_id=1, source_target_pairs={{0,24},{8,0},{16,8},{24,16},{1,25},{9,1},{17,9},{25,17},{2,26},{10... | collective-permute-start | bytes 589832 | tf_op jit(solution)/shard_map/ppermute | solution.py:29
  100.5 9.1 %collective-permute-start.6 = (bf16[8,48,256]{2,1,0:T(8,128)(2,1)}, bf16[8,48,256]{2,1,0:T(8,128)(2,1)S(1)}, u32[]{:S(2)}, u32[]{:S(2)}) collective-permute-start(bf16[8,48,256]{2,1,0:T(8,128)(2,1)} %get-tuple-element.29), channel_id=1, source_target_pairs={{0,16},{8,24},{16,0},{24,8},{1,17},{9,25},{17,1},{25,9},{2,18},{10... | collective-permute-start | bytes 589832 | tf_op jit(solution)/shard_map/ppermute | solution.py:29
  112.9 10.7 %collective-permute-start.10 = (bf16[48,256]{1,0:T(8,128)(2,1)}, bf16[48,256]{1,0:T(8,128)(2,1)S(1)}, u32[]{:S(2)}, u32[]{:S(2)}) collective-permute-start(bf16[48,256]{1,0:T(8,128)(2,1)} %get-tuple-element.34), channel_id=1, source_target_pairs={{0,64},{32,96},{64,128},{96,160},{128,192},{160,224},{192,0},{224,... | collective-permute-start | bytes 73736 | tf_op jit(solution)/shard_map/ppermute | solution.py:29
  117.7 22.2 %collective-permute-start.15 = (bf16[48,1024]{1,0:T(8,128)(2,1)S(1)}, bf16[48,1024]{1,0:T(8,128)(2,1)S(1)}, u32[]{:S(2)}, u32[]{:S(2)}) collective-permute-start(bf16[48,1024]{1,0:T(8,128)(2,1)S(1)} %get-tuple-element.46), channel_id=1, source_target_pairs={{0,8},{8,16},{16,24},{24,0},{1,9},{9,17},{17,25},{25,1},{2,10},{10... | collective-permute-start | bytes 294920 | tf_op jit(solution)/shard_map/ppermute | solution.py:29
  118.3 21.6 %collective-permute-start.16 = (bf16[48,1024]{1,0:T(8,128)(2,1)S(1)}, bf16[48,1024]{1,0:T(8,128)(2,1)S(1)}, u32[]{:S(2)}, u32[]{:S(2)}) collective-permute-start(bf16[48,1024]{1,0:T(8,128)(2,1)S(1)} %get-tuple-element.45), channel_id=1, source_target_pairs={{0,24},{8,0},{16,8},{24,16},{1,25},{9,1},{17,9},{25,17},{2,26},{10... | collective-permute-start | bytes 294920 | tf_op jit(solution)/shard_map/ppermute | solution.py:29
  120.4 19.6 %collective-permute-start.17 = (bf16[48,1024]{1,0:T(8,128)(2,1)S(1)}, bf16[48,1024]{1,0:T(8,128)(2,1)S(1)}, u32[]{:S(2)}, u32[]{:S(2)}) collective-permute-start(bf16[48,1024]{1,0:T(8,128)(2,1)S(1)} %get-tuple-element.44), channel_id=1, source_target_pairs={{0,16},{8,24},{16,0},{24,8},{1,17},{9,25},{17,1},{25,9},{2,18},{10... | collective-permute-start | bytes 294920 | tf_op jit(solution)/shard_map/ppermute | solution.py:29
  120.4 6.1 %collective-permute-start.11 = (bf16[48,256]{1,0:T(8,128)(2,1)}, bf16[48,256]{1,0:T(8,128)(2,1)S(1)}, u32[]{:S(2)}, u32[]{:S(2)}) collective-permute-start(bf16[48,256]{1,0:T(8,128)(2,1)} %get-tuple-element.35), channel_id=1, source_target_pairs={{0,192},{32,224},{64,0},{96,32},{128,64},{160,96},{192,128},{224,1... | collective-permute-start | bytes 73736 | tf_op jit(solution)/shard_map/ppermute | solution.py:29
  123.6 4.5 %collective-permute-start.12 = (bf16[48,256]{1,0:T(8,128)(2,1)}, bf16[48,256]{1,0:T(8,128)(2,1)S(1)}, u32[]{:S(2)}, u32[]{:S(2)}) collective-permute-start(bf16[48,256]{1,0:T(8,128)(2,1)} %get-tuple-element.36), channel_id=1, source_target_pairs={{0,32},{32,64},{64,96},{96,128},{128,160},{160,192},{192,224},{224... | collective-permute-start | bytes 73736 | tf_op jit(solution)/shard_map/ppermute | solution.py:29
  126.5 6.1 %collective-permute-start.13 = (bf16[48,256]{1,0:T(8,128)(2,1)}, bf16[48,256]{1,0:T(8,128)(2,1)S(1)}, u32[]{:S(2)}, u32[]{:S(2)}) collective-permute-start(bf16[48,256]{1,0:T(8,128)(2,1)} %get-tuple-element.37), channel_id=1, source_target_pairs={{0,224},{32,0},{64,32},{96,64},{128,96},{160,128},{192,160},{224,1... | collective-permute-start | bytes 73736 | tf_op jit(solution)/shard_map/ppermute | solution.py:29
  128.1 6.8 %collective-permute-start.7 = (bf16[48,256]{1,0:T(8,128)(2,1)}, bf16[48,256]{1,0:T(8,128)(2,1)S(1)}, u32[]{:S(2)}, u32[]{:S(2)}) collective-permute-start(bf16[48,256]{1,0:T(8,128)(2,1)} %get-tuple-element.31), channel_id=1, source_target_pairs={{0,128},{32,160},{64,192},{96,224},{128,0},{160,32},{192,64},{224,... | collective-permute-start | bytes 73736 | tf_op jit(solution)/shard_map/ppermute | solution.py:29
  132.5 5.9 %collective-permute-start.8 = (bf16[48,256]{1,0:T(8,128)(2,1)}, bf16[48,256]{1,0:T(8,128)(2,1)S(1)}, u32[]{:S(2)}, u32[]{:S(2)}) collective-permute-start(bf16[48,256]{1,0:T(8,128)(2,1)} %get-tuple-element.32), channel_id=1, source_target_pairs={{0,96},{32,128},{64,160},{96,192},{128,224},{160,0},{192,32},{224,... | collective-permute-start | bytes 73736 | tf_op jit(solution)/shard_map/ppermute | solution.py:29
  134.9 5.0 %collective-permute-start.9 = (bf16[48,256]{1,0:T(8,128)(2,1)}, bf16[48,256]{1,0:T(8,128)(2,1)S(1)}, u32[]{:S(2)}, u32[]{:S(2)}) collective-permute-start(bf16[48,256]{1,0:T(8,128)(2,1)} %get-tuple-element.33), channel_id=1, source_target_pairs={{0,160},{32,192},{64,224},{96,0},{128,32},{160,64},{192,96},{224,1... | collective-permute-start | bytes 73736 | tf_op jit(solution)/shard_map/ppermute | solution.py:29
  143.2 7.5 %collective-permute-start.18 = (bf16[24,1280]{1,0:T(8,128)(2,1)}, bf16[24,1280]{1,0:T(8,128)(2,1)S(1)}, u32[]{:S(2)}, u32[]{:S(2)}) collective-permute-start(bf16[24,1280]{1,0:T(8,128)(2,1)} %get-tuple-element.39), channel_id=1, source_target_pairs={{0,4},{4,0},{1,5},{5,1},{2,6},{6,2},{3,7},{7,3},{8,12},{12,8},{9,1... | collective-permute-start | bytes 184328 | tf_op jit(solution)/shard_map/ppermute | solution.py:29
  151.6 4.1 %collective-permute-start.19 = (bf16[2,6,1280]{2,1,0:T(8,128)(2,1)S(1)}, bf16[2,6,1280]{2,1,0:T(8,128)(2,1)S(1)}, u32[]{:S(2)}, u32[]{:S(2)}) collective-permute-start(bf16[2,6,1280]{2,1,0:T(8,128)(2,1)S(1)} %get-tuple-element.59), channel_id=1, source_target_pairs={{0,1},{1,2},{2,3},{3,0},{4,5},{5,6},{6,7},{7,4},{8,9},{9,10},{10,1... | collective-permute-start | bytes 92168 | tf_op jit(solution)/shard_map/ppermute | solution.py:29
  152.4 4.5 %collective-permute-start.20 = (bf16[2,6,1280]{2,1,0:T(8,128)(2,1)S(1)}, bf16[2,6,1280]{2,1,0:T(8,128)(2,1)S(1)}, u32[]{:S(2)}, u32[]{:S(2)}) collective-permute-start(bf16[2,6,1280]{2,1,0:T(8,128)(2,1)S(1)} %get-tuple-element.60), channel_id=1, source_target_pairs={{0,2},{1,3},{2,0},{3,1},{4,6},{5,7},{6,4},{7,5},{8,10},{9,11},{10,... | collective-permute-start | bytes 92168 | tf_op jit(solution)/shard_map/ppermute | solution.py:29
  158.2 4.3 %collective-permute-start.22 = (bf16[6,4096]{1,0:T(8,128)(2,1)S(1)}, bf16[6,4096]{1,0:T(8,128)(2,1)S(1)}, u32[]{:S(2)}, u32[]{:S(2)}) collective-permute-start(bf16[6,4096]{1,0:T(8,128)(2,1)S(1)} %get-tuple-element.40), channel_id=1, source_target_pairs={{0,1},{1,2},{2,3},{3,0},{4,5},{5,6},{6,7},{7,4},{8,9},{9,10},{10,1... | collective-permute-start | bytes 147464 | tf_op jit(solution)/shard_map/ppermute | solution.py:29
  159.3 4.6 %collective-permute-start.23 = (bf16[6,4096]{1,0:T(8,128)(2,1)S(1)}, bf16[6,4096]{1,0:T(8,128)(2,1)S(1)}, u32[]{:S(2)}, u32[]{:S(2)}) collective-permute-start(bf16[6,4096]{1,0:T(8,128)(2,1)S(1)} %get-tuple-element.40), channel_id=1, source_target_pairs={{0,2},{1,3},{2,0},{3,1},{4,6},{5,7},{6,4},{7,5},{8,10},{9,11},{10,... | collective-permute-start | bytes 147464 | tf_op jit(solution)/shard_map/ppermute | solution.py:29
  (20 other events, 302.1 us)
Sparse Core Ops, SparseCore 0:
  33.1 45.0 reduce-scatter.1

commit v3 on v2

v3 whole, which is shorter than its diff:
```python
import jax
import jax.numpy as jnp
from jax import lax
from jax.experimental import pallas as pl
from jax.experimental.pallas import tpu as pltpu
from jax.sharding import Mesh, PartitionSpec as P

NZ, NX, NC, NY = 8, 4, 2, 4
D, FFW = 1536, 4096
HALF = FFW // 2
TN = 256
BLK = D // (NZ * NX)
FLOW_C = 1024
FLOW_A = 1024
T = 1024
F32, BF16 = jnp.float32, jnp.bfloat16
VMEM_LIMIT = 40 * 1024 * 1024
DN = (((0,), (0,)), ((), ()))


def params_of(flops, nbytes):
    return dict(
        compiler_params=pltpu.CompilerParams(vmem_limit_bytes=VMEM_LIMIT),
        cost_estimate=pl.CostEstimate(flops=flops, bytes_accessed=nbytes, transcendentals=0),
    )


def shift(v, axis, n, s):
    return lax.ppermute(v, axis, [(i, (i + s) % n) for i in range(n)])


def swap(v, axes):
    return lax.all_to_all(v, axes, 0, 0, tiled=True)


def product(acts, cot, idx, base, ncols):
    tn = 2 * TN

    def kernel(idx_ref, a, c, o):
        o[...] = lax.dot_general(a[...], c[...], DN, preferred_element_type=F32).astype(BF16)

    return pl.pallas_call(
        kernel,
        grid_spec=pltpu.PrefetchScalarGridSpec(
            num_scalar_prefetch=1,
            grid=(ncols // tn,),
            in_specs=[
                pl.BlockSpec((T, D), lambda j, s: (0, 0)),
                pl.BlockSpec((T, tn), lambda j, s: (0, (1 - s[0]) * (HALF // tn) + base // tn + j)),
            ],
            out_specs=pl.BlockSpec((D, tn), lambda j, s: (0, j)),
        ),
        out_shape=jax.ShapeDtypeStruct((D, ncols), BF16),
        name="product_theirs",
        **params_of(2 * T * D * ncols, 2 * (T * D + T * ncols + D * ncols)),
    )(idx, acts, cot)


def product_for_z(acts, cot, got, idx, base, ncols, after):
    tn = 2 * TN

    def kernel(idx_ref, a, c, r, _, o):
        acc = lax.dot_general(a[...], c[...], DN, preferred_element_type=F32) + r[...].astype(F32)
        o[...] = acc.astype(BF16)

    return pl.pallas_call(
        kernel,
        grid_spec=pltpu.PrefetchScalarGridSpec(
            num_scalar_prefetch=1,
            grid=(ncols // tn,),
            in_specs=[
                pl.BlockSpec((T, D), lambda j, s: (0, 0)),
                pl.BlockSpec((T, tn), lambda j, s: (0, s[0] * (HALF // tn) + base // tn + j)),
                pl.BlockSpec((D, tn), lambda j, s: (0, j)),
                pl.BlockSpec(memory_space=pl.ANY),
            ],
            out_specs=pl.BlockSpec((D, tn), lambda j, s: (0, j)),
        ),
        out_shape=jax.ShapeDtypeStruct((D, ncols), BF16),
        name="product_for_z",
        **params_of(2 * T * D * ncols, 2 * (T * D + T * ncols + 2 * D * ncols)),
    )(idx, acts, cot, got, after)


def product_for_y(acts, cot, got, idx, base):
    def kernel(idx_ref, a, c, r, o):
        acc = lax.dot_general(a[...], c[...], DN, preferred_element_type=F32) + r[...].astype(F32)
        o[0] = acc.astype(BF16)

    return pl.pallas_call(
        kernel,
        grid_spec=pltpu.PrefetchScalarGridSpec(
            num_scalar_prefetch=1,
            grid=(NY,),
            in_specs=[
                pl.BlockSpec((T, D), lambda j, s: (0, 0)),
                pl.BlockSpec((T, TN), lambda j, s: (0, s[0] * (HALF // TN) + base // TN + j)),
                pl.BlockSpec((D, TN), lambda j, s: (0, j)),
            ],
            out_specs=pl.BlockSpec((1, D, TN), lambda j, s: (j, 0, 0)),
        ),
        out_shape=jax.ShapeDtypeStruct((NY, D, TN), BF16),
        name="product_for_y",
        **params_of(2 * T * D * TN * NY, 2 * (T * D + T * TN * NY + 2 * D * TN * NY)),
    )(idx, acts, cot, got)


def sum_for_x(over_y, part_a):
    upper, parts = NZ * BLK, FLOW_A // TN
    height = upper + parts * BLK

    def kernel(c, a, o):
        total = c[0].astype(F32)
        for k in range(1, NY):
            total = total + c[k].astype(F32)
        o[0, :upper, :] = total.reshape(upper, TN).astype(BF16)
        for q in range(parts):
            o[0, upper + q * BLK : upper + (q + 1) * BLK, :] = a[0, :, q * TN : (q + 1) * TN]

    return pl.pallas_call(
        kernel,
        grid=(NX,),
        in_specs=[
            pl.BlockSpec((NY, NZ, 1, BLK, TN), lambda j: (0, 0, j, 0, 0)),
            pl.BlockSpec((1, BLK, FLOW_A), lambda j: (j, 0, 0)),
        ],
        out_specs=pl.BlockSpec((1, height, TN), lambda j: (j, 0, 0)),
        out_shape=jax.ShapeDtypeStruct((NX, height, TN), BF16),
        name="sum_for_x",
        **params_of(4 * D * TN, 10 * D * TN),
    )(over_y.reshape(NY, NZ, NX, BLK, TN), part_a.reshape(NX, BLK, FLOW_A))


def sum_for_z(over_x):
    upper, parts = NZ * BLK, FLOW_A // TN

    def kernel(r, c, a):
        for z in range(NZ + parts):
            rows = slice(z * BLK, (z + 1) * BLK)
            total = r[0, rows, :].astype(F32)
            for k in range(1, NX):
                total = total + r[k, rows, :].astype(F32)
            if z < NZ:
                c[z] = total.astype(BF16)
            else:
                a[:, (z - NZ) * TN : (z - NZ + 1) * TN] = total.astype(BF16)

    whole = lambda *shape: pl.BlockSpec(shape, lambda j: (0,) * len(shape))
    return pl.pallas_call(
        kernel,
        grid=(1,),
        in_specs=[whole(*over_x.shape)],
        out_specs=[whole(NZ, BLK, TN), whole(BLK, FLOW_A)],
        out_shape=[jax.ShapeDtypeStruct((NZ, BLK, TN), BF16), jax.ShapeDtypeStruct((BLK, FLOW_A), BF16)],
        name="sum_for_z",
        **params_of(5 * D * TN, 10 * D * TN),
    )(over_x)


def body(acts, cotangent, master, moment, second):
    y, c = lax.axis_index("y"), lax.axis_index("c")
    idx = jnp.stack([c, y]).astype(jnp.int32)
    theirs_a = product(acts, cotangent, idx, FLOW_C, FLOW_A)
    got_a = shift(theirs_a, "c", NC, 1)
    theirs_c = product(acts, cotangent, idx, 0, FLOW_C)
    got_c = shift(theirs_c, "c", NC, 1)
    part_a = product_for_z(acts, cotangent, got_a, idx, FLOW_C, FLOW_A, theirs_c)
    part_a = lax.psum_scatter(part_a, "z", scatter_dimension=0, tiled=True)
    over_y = swap(product_for_y(acts, cotangent, got_c, idx, 0), "y")
    part_c, part_a = sum_for_z(swap(sum_for_x(over_y, part_a), "x"))
    part_c = jnp.sum(swap(part_c, "z").astype(F32), axis=0).astype(BF16)
    rows = jnp.concatenate([part_c, part_a], axis=-1).reshape(NC * NY, BLK // NC // NY, TN + FLOW_A)
    pieces = swap(rows, ("c", "y"))
    columns = []
    for h in range(NC):
        of_core = [pieces[h * NY + k] for k in range(NY)]
        columns += [p[:, :TN].astype(F32) for p in of_core]
        columns.append(sum(p[:, TN:].astype(F32) for p in of_core))
    grad = jnp.concatenate(columns, axis=-1)
    new_moment = 0.9 * moment + 0.1 * grad
    new_second = 0.95 * second + 0.05 * grad * grad
    corr_one = 1.0 - 0.9**10
    corr_two = 1.0 - 0.95**10
    update = new_moment / corr_one / (jnp.sqrt(new_second / corr_two) + 1e-08)
    new_master = master - 0.02 * (update + 0.1 * master)
    rounded = new_master.astype(BF16)
    every = [rounded] + [shift(rounded, "y", NY, s) for s in (1, 2, 3)]
    params = jnp.concatenate([lax.select_n(lax.rem(y - k + NY, NY), *every) for k in range(NY)], axis=0)
    return (new_master, new_moment, new_second, params)


def solution(mesh):
    fine = Mesh(mesh.devices.reshape(NZ, NX, NC, NY), ("z", "x", "c", "y"))
    split = P(("z", "x", "c", "y"), None)
    return jax.shard_map(
        body,
        mesh=fine,
        in_specs=(split,) * 5,
        out_specs=(split, split, split, P(("z", "x", "c"), None)),
        check_vma=False,
    )
```

time: 175 us -> 149 us (0.85); the launches traced: 172 us -> 149 us
  blocking collectives: 0 us -> 86.8 us
  waiting for transfers between devices: 64.2 us -> 9.1 us
  starting transfers between devices: 44.2 us -> 6.5 us
  Pallas kernels: 43.5 us -> 23.9 us
  local copies, waits for them, and re-layouts: 3.04 us -> 6.26 us
    all_to_all x0 -> x4, blocking collectives: none -> 86.8 us  [swap(): return lax.all_to_all(v, axes, 0, 0, tiled=True)]
    ppermute x25 -> x5, waiting for transfers between devices: 64.2 us -> 9.08 us  [shift(): return lax.ppermute(v, axis, [(i, (i + s) % n) for i in range(n)])]
    ppermute x25 -> x5, starting transfers between devices: 44.1 us -> 6.46 us  [shift(): return lax.ppermute(v, axis, [(i, (i + s) % n) for i in range(n)])]
    pallas_call x3 -> x2, Pallas kernels: 9.94 us -> 0.83 us  [the longest x1 0.68 us: sum_for_x(): pl.pallas_call(kernel, grid=(NX,), in_specs=[pl.BlockSpec((NY, NZ, 1, BLK...]
    unnamed x36 -> x16, local copies, waits for them, and re-layouts: 1.34 us -> 6.2 us
    pallas_call x2, Pallas kernels: 15.7 us -> 11.4 us  [product(): pl.pallas_call(kernel, grid_spec=pltpu.PrefetchScalarGridSpec(num_scalar_...]
    pallas_call x1, Pallas kernels: 9.47 us -> 5.95 us  [product_for_y(): pl.pallas_call(kernel, grid_spec=pltpu.PrefetchScalarGridSpec(num_scalar_...]
    pallas_call x1, Pallas kernels: 8.35 us -> 5.72 us  [product_for_z(): pl.pallas_call(kernel, grid_spec=pltpu.PrefetchScalarGridSpec(num_scalar_...]
  transfers between devices with their start and end apart: 26 -> 6, of which waited for: 18 -> 3; matrix products, arithmetic and copies ran while one was open for 1% -> 0% of each run, Pallas kernels for 14% -> 8%
where the time goes in v3:
time: 149 us
  blocking collectives  86.8 us (58%)
  Pallas kernels  23.9 us (16%)
  between operations  14.3 us (10%)
  waiting for transfers between devices  9.1 us (6%)
  starting transfers between devices  6.5 us (4%)
  local copies, waits for them, and re-layouts  6.26 us (4%)
  other arithmetic  1.8 us (1%)
    all_to_all x4, blocking collectives, swap(): return lax.all_to_all(v, axes, 0, 0, tiled=True)  86.8 us
    pallas_call x2, Pallas kernels, product(): pl.pallas_call(kernel, grid_spec=pltpu.PrefetchScalarGridSpec(num_scalar_...  11.4 us
    ppermute x5, waiting for transfers between devices, shift(): return lax.ppermute(v, axis, [(i, (i + s) % n) for i in range(n)])  9.08 us
    ppermute x5, starting transfers between devices, shift(): return lax.ppermute(v, axis, [(i, (i + s) % n) for i in range(n)])  6.46 us
    unnamed x16, local copies, waits for them, and re-layouts  6.2 us
    pallas_call x1, Pallas kernels, product_for_y(): pl.pallas_call(kernel, grid_spec=pltpu.PrefetchScalarGridSpec(num_scalar_...  5.95 us
    pallas_call x1, Pallas kernels, product_for_z(): pl.pallas_call(kernel, grid_spec=pltpu.PrefetchScalarGridSpec(num_scalar_...  5.72 us
  transfers between devices with their start and end apart: 6, of which 3 were waited for; matrix products, arithmetic and copies ran while one was open for 0% of the time, Pallas kernels for 8%

profile of v3, /device:TPU:1, one launch (start us, length us, event | category | flops | bytes accessed | tf_op | source)
XLA Modules:
  0.0 148.7 jit_solution(1041450909708804076)
XLA Ops:
  7.3 1.9 %copy-done = bf16[1024,1536]{1,0:T(8,128)(2,1)S(1)} copy-done((bf16[1024,1536]{1,0:T(8,128)(2,1)S(1)}, bf16[1024,1536]{1,0:T(8,128)(2,1)}, u32[]{:S(2)}) %copy-start) | copy-done | bytes 3145752
  9.2 5.7 %product_theirs.3 = bf16[1536,1024]{1,0:T(8,128)(2,1)S(1)} custom-call(s32[2]{0:T(128)S(1)} %pad_add_fusion.idx_ref, bf16[1024,1536]{1,0:T(8,128)(2,1)S(1)} %copy-done, bf16[1024,4096]{1,0:T(8,128)(2,1)} %c.7), custom_call_target="tpu_custom_call" | custom-call | flops 3221225472 | bytes 8388608 | tf_op jit(solution)/shard_map/product_theirs/pallas_call | solution.py:42
  14.9 3.3 %collective-permute-start.1 = (bf16[1536,1024]{1,0:T(8,128)(2,1)S(1)}, bf16[1536,1024]{1,0:T(8,128)(2,1)S(1)}, u32[]{:S(2)}, u32[]{:S(2)}) collective-permute-start(bf16[1536,1024]{1,0:T(8,128)(2,1)S(1)} %product_theirs.3), channel_id=1, source_target_pairs={{0,4},{4,0},{1,5},{5,1},{2,6},{6,2},{3,7},{7,3},{8,12},{12,8},{9,1... | collective-permute-start | bytes 9437192 | tf_op jit(solution)/shard_map/ppermute | solution.py:29
  18.2 5.7 %product_theirs.2._ = bf16[1536,1024]{1,0:T(8,128)(2,1)S(1)} custom-call(s32[2]{0:T(128)S(1)} %pad_add_fusion.idx_ref, bf16[1024,1536]{1,0:T(8,128)(2,1)S(1)} %copy-done, bf16[1024,4096]{1,0:T(8,128)(2,1)} %c.7), custom_call_target="tpu_custom_call" | custom-call | flops 3221225472 | bytes 8388608 | tf_op jit(solution)/shard_map/product_theirs/pallas_call | solution.py:42
  24.0 5.7 %product_for_z.1 = bf16[1536,1024]{1,0:T(8,128)(2,1)S(1)} custom-call(s32[2]{0:T(128)S(1)} %pad_add_fusion.idx_ref, bf16[1024,1536]{1,0:T(8,128)(2,1)S(1)} %copy-done, bf16[1024,4096]{1,0:T(8,128)(2,1)} %c.7, bf16[1536,1024]{1,0:T(8,128)(2,1)S(1)} %collective-permute-done.1.r, bf16[1536,1024]{1,0:T(8,128)(2,1)S(1)} %product_theirs.2._), custom_call_target="tpu_custom_call" | custom-call | flops 3221225472 | bytes 11534336 | tf_op jit(solution)/shard_map/product_for_z/pallas_call | solution.py:66
  29.7 1.6 %copy-done.2 = bf16[1536,1024]{1,0:T(8,128)(2,1)} copy-done((bf16[1536,1024]{1,0:T(8,128)(2,1)}, bf16[1536,1024]{1,0:T(8,128)(2,1)S(1)}, u32[]{:S(2)}) %copy-start.2) | copy-done | bytes 3145752
  31.3 1.7 %copy-done.3 = bf16[1536,1024]{1,0:T(8,128)(2,1)} copy-done((bf16[1536,1024]{1,0:T(8,128)(2,1)}, bf16[1536,1024]{1,0:T(8,128)(2,1)S(1)}, u32[]{:S(2)}) %copy-start.3) | copy-done | bytes 3145752
  33.0 0.1 collective-permute-start
  33.1 5.9 %collective-permute-done.r = bf16[1536,1024]{1,0:T(8,128)(2,1)S(1)} collective-permute-done((bf16[1536,1024]{1,0:T(8,128)(2,1)}, bf16[1536,1024]{1,0:T(8,128)(2,1)S(1)}, u32[]{:S(2)}, u32[]{:S(2)}) %collective-permute-start) | collective-permute-done | bytes 3145760 | tf_op jit(solution)/shard_map/ppermute | solution.py:29
  39.0 6.0 %product_for_y.1 = bf16[4,1536,256]{2,1,0:T(8,128)(2,1)S(1)} custom-call(s32[2]{0:T(128)S(1)} %pad_add_fusion.idx_ref, bf16[1024,1536]{1,0:T(8,128)(2,1)S(1)} %copy-done.1, bf16[1024,4096]{1,0:T(8,128)(2,1)} %c.7, bf16[1536,1024]{1,0:T(8,128)(2,1)S(1)} %collective-permute-done.r), custom_call_target="tpu_custom_call" | custom-call | flops 3221225472 | bytes 11534336 | tf_op jit(solution)/shard_map/product_for_y/pallas_call | solution.py:90
  44.9 39.8 %all_to_all.20 = bf16[4,1536,256]{2,1,0:T(8,128)(2,1)S(1)} all-to-all(bf16[4,1536,256]{2,1,0:T(8,128)(2,1)S(1)} %product_for_y.1), channel_id=1, replica_groups=mesh['z'=8,'x'=4,'c'=2,'y'=4] {'y'}, dimensions={0} | all-to-all | bytes 6291456 | tf_op jit(solution)/shard_map/all_to_all | solution.py:33
  84.8 1.0 copy-done.4
  85.7 0.7 sum_for_x.1
  86.5 18.6 %all_to_all.21.r = bf16[4,576,256]{2,1,0:T(8,128)(2,1)S(1)} all-to-all(bf16[4,576,256]{2,1,0:T(8,128)(2,1)S(1)} %sum_for_x.1), channel_id=1, replica_groups=mesh['z'=8,'x'=4,'c'=2,'y'=4] {'x'}, dimensions={0} | all-to-all | bytes 2359296 | tf_op jit(solution)/shard_map/all_to_all | solution.py:33
  105.0 0.1 sum_for_z.1
  105.2 16.7 %all_to_all.22 = bf16[8,48,256]{2,1,0:T(8,128)(2,1)S(1)} all-to-all(bf16[8,48,256]{2,1,0:T(8,128)(2,1)S(1)} %get-tuple-element.6), channel_id=1, replica_groups=mesh['z'=8,'x'=4,'c'=2,'y'=4] {'z'}, dimensions={0} | all-to-all | bytes 393216 | tf_op jit(solution)/shard_map/all_to_all | solution.py:33
  122.0 11.8 %all_to_all.23 = bf16[8,6,1280]{2,1,0:T(8,128)(2,1)S(1)} all-to-all(bf16[8,6,1280]{2,1,0:T(8,128)(2,1)S(1)} %reshape.19), channel_id=1, replica_groups=mesh['z'=8,'x'=4,'c'=2,'y'=4] {'c','y'}, dimensions={0} | all-to-all | bytes 245760 | tf_op jit(solution)/shard_map/all_to_all | solution.py:33
  133.9 0.8 fusion.1
  134.7 0.7 collective-permute-start.2
  135.4 1.5 %collective-permute-start.3 = (bf16[6,4096]{1,0:T(8,128)(2,1)S(1)}, bf16[6,4096]{1,0:T(8,128)(2,1)S(1)}, u32[]{:S(2)}, u32[]{:S(2)}) collective-permute-start(bf16[6,4096]{1,0:T(8,128)(2,1)S(1)} %get-tuple-element.8), channel_id=1, source_target_pairs={{0,2},{1,3},{2,0},{3,1},{4,6},{5,7},{6,4},{7,5},{8,10},{9,11},{10,... | collective-permute-start | bytes 147464 | tf_op jit(solution)/shard_map/ppermute | solution.py:29
  136.9 0.9 collective-permute-start.4
  137.8 1.3 collective-permute-done.2
  139.1 1.9 %collective-permute-done.3 = bf16[6,4096]{1,0:T(8,128)(2,1)S(1)} collective-permute-done((bf16[6,4096]{1,0:T(8,128)(2,1)S(1)}, bf16[6,4096]{1,0:T(8,128)(2,1)S(1)}, u32[]{:S(2)}, u32[]{:S(2)}) %collective-permute-start.3) | collective-permute-done | bytes 49184 | tf_op jit(solution)/shard_map/ppermute | solution.py:29
  141.1 0.8 pad_maximum_fusion
  (33 shorter events, 0.4 us)
Async XLA Ops:
  7.2 77.6 %reduce-scatter.2.cloned.1.call-start = ((), (), s32[]{:S(2)}) async-start(), calls=%async_computation.5 | async-start | bytes 3538944 | tf_op jit(solution)/shard_map/reduce_scatter | solution.py:168
  7.3 1.9 %copy-start = (bf16[1024,1536]{1,0:T(8,128)(2,1)S(1)}, bf16[1024,1536]{1,0:T(8,128)(2,1)}, u32[]{:S(2)}) copy-start(bf16[1024,1536]{1,0:T(8,128)(2,1)} %a.7) | copy-start | bytes 9437188
  14.9 9.0 %collective-permute-start.1 = (bf16[1536,1024]{1,0:T(8,128)(2,1)S(1)}, bf16[1536,1024]{1,0:T(8,128)(2,1)S(1)}, u32[]{:S(2)}, u32[]{:S(2)}) collective-permute-start(bf16[1536,1024]{1,0:T(8,128)(2,1)S(1)} %product_theirs.3), channel_id=1, source_target_pairs={{0,4},{4,0},{1,5},{5,1},{2,6},{6,2},{3,7},{7,3},{8,12},{12,8},{9,1... | collective-permute-start | bytes 9437192 | tf_op jit(solution)/shard_map/ppermute | solution.py:29
  29.7 1.6 %copy-start.2 = (bf16[1536,1024]{1,0:T(8,128)(2,1)}, bf16[1536,1024]{1,0:T(8,128)(2,1)S(1)}, u32[]{:S(2)}) copy-start(bf16[1536,1024]{1,0:T(8,128)(2,1)S(1)} %product_for_z.1) | copy-start | bytes 9437188
  31.3 1.7 %copy-start.3 = (bf16[1536,1024]{1,0:T(8,128)(2,1)}, bf16[1536,1024]{1,0:T(8,128)(2,1)S(1)}, u32[]{:S(2)}) copy-start(bf16[1536,1024]{1,0:T(8,128)(2,1)S(1)} %product_theirs.2._) | copy-start | bytes 9437188
  33.0 6.0 %copy-start.1 = (bf16[1024,1536]{1,0:T(8,128)(2,1)S(1)}, bf16[1024,1536]{1,0:T(8,128)(2,1)}, u32[]{:S(2)}) copy-start(bf16[1024,1536]{1,0:T(8,128)(2,1)} %a.7) | copy-start | bytes 9437188
  33.0 6.0 %collective-permute-start = (bf16[1536,1024]{1,0:T(8,128)(2,1)}, bf16[1536,1024]{1,0:T(8,128)(2,1)S(1)}, u32[]{:S(2)}, u32[]{:S(2)}) collective-permute-start(bf16[1536,1024]{1,0:T(8,128)(2,1)} %copy-done.3), channel_id=1, source_target_pairs={{0,4},{4,0},{1,5},{5,1},{2,6},{6,2},{3,7},{7,3},{8,12},{12,8},{9,1... | collective-permute-start | bytes 9437192 | tf_op jit(solution)/shard_map/ppermute | solution.py:29
  84.7 1.0 copy-start.4
  86.4 47.5 %copy-start.5 = (f32[6,4096]{1,0:T(8,128)S(1)}, f32[6,4096]{1,0:T(8,128)}, u32[]{:S(2)}) copy-start(f32[6,4096]{1,0:T(8,128)} %param.7) | copy-start | bytes 294916
  86.4 47.5 %copy-start.6 = (f32[6,4096]{1,0:T(8,128)S(1)}, f32[6,4096]{1,0:T(8,128)}, u32[]{:S(2)}) copy-start(f32[6,4096]{1,0:T(8,128)} %param.8) | copy-start | bytes 294916
  86.5 47.5 %copy-start.7 = (f32[6,4096]{1,0:T(8,128)S(1)}, f32[6,4096]{1,0:T(8,128)}, u32[]{:S(2)}) copy-start(f32[6,4096]{1,0:T(8,128)} %param.9) | copy-start | bytes 294916
  134.7 4.3 %collective-permute-start.2 = (bf16[6,4096]{1,0:T(8,128)(2,1)S(1)}, bf16[6,4096]{1,0:T(8,128)(2,1)S(1)}, u32[]{:S(2)}, u32[]{:S(2)}) collective-permute-start(bf16[6,4096]{1,0:T(8,128)(2,1)S(1)} %get-tuple-element.8), channel_id=1, source_target_pairs={{0,1},{1,2},{2,3},{3,0},{4,5},{5,6},{6,7},{7,4},{8,9},{9,10},{10,1... | collective-permute-start | bytes 147464 | tf_op jit(solution)/shard_map/ppermute | solution.py:29
  135.4 5.6 %collective-permute-start.3 = (bf16[6,4096]{1,0:T(8,128)(2,1)S(1)}, bf16[6,4096]{1,0:T(8,128)(2,1)S(1)}, u32[]{:S(2)}, u32[]{:S(2)}) collective-permute-start(bf16[6,4096]{1,0:T(8,128)(2,1)S(1)} %get-tuple-element.8), channel_id=1, source_target_pairs={{0,2},{1,3},{2,0},{3,1},{4,6},{5,7},{6,4},{7,5},{8,10},{9,11},{10,... | collective-permute-start | bytes 147464 | tf_op jit(solution)/shard_map/ppermute | solution.py:29
  136.9 4.1 %collective-permute-start.4 = (bf16[6,4096]{1,0:T(8,128)(2,1)S(1)}, bf16[6,4096]{1,0:T(8,128)(2,1)S(1)}, u32[]{:S(2)}, u32[]{:S(2)}) collective-permute-start(bf16[6,4096]{1,0:T(8,128)(2,1)S(1)} %get-tuple-element.8), channel_id=1, source_target_pairs={{0,3},{1,0},{2,1},{3,2},{4,7},{5,4},{6,5},{7,6},{8,11},{9,8},{10,9... | collective-permute-start | bytes 147464 | tf_op jit(solution)/shard_map/ppermute | solution.py:29
Sparse Core Ops, SparseCore 0:
  33.1 44.8 reduce-scatter.1

commit v4 on v1

v4 whole, which is shorter than its diff:
```python
import jax
import jax.numpy as jnp
from jax import lax
from jax.experimental import pallas as pl
from jax.experimental.pallas import tpu as pltpu
from jax.sharding import Mesh, PartitionSpec as P

NZ, NX, NC, NY = 8, 4, 2, 4
D, FFW = 1536, 4096
HALF = FFW // 2
TN = 256
BLK = D // (NZ * NX)
FLOW_C = 1024
FLOW_B = 1024
T = 1024
F32, BF16 = jnp.float32, jnp.bfloat16
VMEM_LIMIT = 40 * 1024 * 1024
DN = (((0,), (0,)), ((), ()))


def params_of(flops, nbytes):
    return dict(
        compiler_params=pltpu.CompilerParams(vmem_limit_bytes=VMEM_LIMIT),
        cost_estimate=pl.CostEstimate(flops=flops, bytes_accessed=nbytes, transcendentals=0),
    )


def shift(v, axis, n, s):
    return lax.ppermute(v, axis, [(i, (i + s) % n) for i in range(n)])


def exchange(pieces, axis, n, order):
    return [pieces[0]] + [shift(pieces[s], axis, n, s) for s in order]


def swap(v, axes):
    return lax.all_to_all(v, axes, 0, 0, tiled=True)


def product(acts, cot, idx, base, ncols):
    tn = 2 * TN

    def kernel(idx_ref, a, c, o):
        o[...] = lax.dot_general(a[...], c[...], DN, preferred_element_type=F32).astype(BF16)

    return pl.pallas_call(
        kernel,
        grid_spec=pltpu.PrefetchScalarGridSpec(
            num_scalar_prefetch=1,
            grid=(ncols // tn,),
            in_specs=[
                pl.BlockSpec((T, D), lambda j, s: (0, 0)),
                pl.BlockSpec((T, tn), lambda j, s: (0, (1 - s[0]) * (HALF // tn) + base // tn + j)),
            ],
            out_specs=pl.BlockSpec((D, tn), lambda j, s: (0, j)),
        ),
        out_shape=jax.ShapeDtypeStruct((D, ncols), BF16),
        name="product_theirs",
        **params_of(2 * T * D * ncols, 2 * (T * D + T * ncols + D * ncols)),
    )(idx, acts, cot)


def product_for_y(acts, cot, got, idx, base):
    def kernel(idx_ref, a, c, r, *outs):
        acc = lax.dot_general(a[...], c[...], DN, preferred_element_type=F32) + r[...].astype(F32)
        for o in range(NY):

            @pl.when(pl.program_id(0) == o)
            def _():
                outs[o][...] = acc.astype(BF16)

    return pl.pallas_call(
        kernel,
        grid_spec=pltpu.PrefetchScalarGridSpec(
            num_scalar_prefetch=1,
            grid=(NY,),
            in_specs=[
                pl.BlockSpec((T, D), lambda j, s: (0, 0)),
                pl.BlockSpec((T, TN), lambda j, s: (0, s[0] * (HALF // TN) + base // TN + lax.rem(s[2] + j, NY))),
                pl.BlockSpec((D, TN), lambda j, s: (0, lax.rem(s[2] + j, NY))),
            ],
            out_specs=[pl.BlockSpec((D, TN), lambda j, s: (0, 0))] * NY,
        ),
        out_shape=[jax.ShapeDtypeStruct((D, TN), BF16)] * NY,
        name="product_for_y",
        **params_of(2 * T * D * TN * NY, 2 * (T * D + T * TN * NY + 2 * D * TN * NY)),
    )(idx, acts, cot, got)


def product_for_x(acts, cot, got, idx, base, ncols):
    def kernel(idx_ref, a, c, r, o):
        acc = lax.dot_general(a[...], c[...], DN, preferred_element_type=F32) + r[...].astype(F32)
        acc = acc.astype(BF16).reshape(NZ, NX, BLK, TN)
        for x in range(NX):
            o[x] = acc[:, x]

    return pl.pallas_call(
        kernel,
        grid_spec=pltpu.PrefetchScalarGridSpec(
            num_scalar_prefetch=1,
            grid=(ncols // TN,),
            in_specs=[
                pl.BlockSpec((T, D), lambda j, s: (0, 0)),
                pl.BlockSpec((T, TN), lambda j, s: (0, s[0] * (HALF // TN) + base // TN + j)),
                pl.BlockSpec((D, TN), lambda j, s: (0, j)),
            ],
            out_specs=pl.BlockSpec((NX, NZ, BLK, TN), lambda j, s: (0, 0, 0, j)),
        ),
        out_shape=jax.ShapeDtypeStruct((NX, NZ, BLK, ncols), BF16),
        name="product_for_x",
        **params_of(2 * T * D * ncols, 2 * (T * D + T * ncols + 2 * D * ncols)),
    )(idx, acts, cot, got)


def sum_for_x(parts, idx):
    width = parts[0].shape[-1]

    def kernel(idx_ref, *refs):
        ins, outs = refs[:NY], refs[NY:]
        for o in range(NX):
            x = lax.rem(idx_ref[1] + o, NX)
            for z in range(NZ):
                total = ins[0][z, x].astype(F32)
                for r in ins[1:]:
                    total = total + r[z, x].astype(F32)
                outs[o][z] = total.astype(BF16)

    return pl.pallas_call(
        kernel,
        grid_spec=pltpu.PrefetchScalarGridSpec(
            num_scalar_prefetch=1,
            grid=(1,),
            in_specs=[pl.BlockSpec((NZ, NX, BLK, width), lambda j, s: (0, 0, 0, 0))] * NY,
            out_specs=[pl.BlockSpec((NZ, BLK, width), lambda j, s: (0, 0, 0))] * NX,
        ),
        out_shape=[jax.ShapeDtypeStruct((NZ, BLK, width), BF16)] * NX,
        name="sum_for_x",
        **params_of(4 * D * width, 2 * 5 * D * width),
    )(idx, *[p.reshape(NZ, NX, BLK, width) for p in parts])


def sum_for_y(over_x):
    width = over_x.shape[-1] // NY

    def kernel(r, o):
        total = r[0].astype(F32)
        for k in range(1, NX):
            total = total + r[k].astype(F32)
        o[0] = total.astype(BF16)

    return pl.pallas_call(
        kernel,
        grid=(NY,),
        in_specs=[pl.BlockSpec((NX, NZ, BLK, width), lambda j: (0, 0, 0, j))],
        out_specs=pl.BlockSpec((1, NZ, BLK, width), lambda j: (j, 0, 0, 0)),
        out_shape=jax.ShapeDtypeStruct((NY, NZ, BLK, width), BF16),
        name="sum_for_y",
        **params_of(4 * D * width, 2 * 5 * D * width),
    )(over_x)


def sum_for_z(over_x, over_y):
    width = over_y.shape[-1]

    def kernel(*refs):
        ins, r, o = refs[:NX], refs[NX], refs[NX + 1]
        total = ins[0][...].astype(F32)
        for p in ins[1:]:
            total = total + p[...].astype(F32)
        o[:, :, :width] = total.astype(BF16)
        total = r[0].astype(F32)
        for k in range(1, NY):
            total = total + r[k].astype(F32)
        o[:, :, width:] = total.astype(BF16)

    spec = pl.BlockSpec((NZ // 2, BLK, width), lambda j: (j, 0, 0))
    return pl.pallas_call(
        kernel,
        grid=(2,),
        in_specs=[spec] * NX + [pl.BlockSpec((NY, NZ // 2, BLK, width), lambda j: (0, j, 0, 0))],
        out_specs=pl.BlockSpec((NZ // 2, BLK, 2 * width), lambda j: (j, 0, 0)),
        out_shape=jax.ShapeDtypeStruct((NZ, BLK, 2 * width), BF16),
        name="sum_for_z",
        **params_of(8 * NZ * BLK * width, 20 * NZ * BLK * width),
    )(*over_x, over_y)


def body(acts, cotangent, master, moment, second):
    x, c, y = (lax.axis_index(a) for a in ("x", "c", "y"))
    idx = jnp.stack([c, x, y]).astype(jnp.int32)
    theirs_c = product(acts, cotangent, idx, 0, FLOW_C)
    got_c = shift(theirs_c, "c", NC, 1)
    theirs_b = product(acts, cotangent, idx, FLOW_C, FLOW_B)
    got_b = shift(theirs_b, "c", NC, 1)
    over_y = exchange(product_for_y(acts, cotangent, got_c, idx, 0), "y", NY, (1, 3, 2))
    over_x = swap(product_for_x(acts, cotangent, got_b, idx, FLOW_C, FLOW_B), "x")
    over_yx = exchange(sum_for_x(over_y, idx), "x", NX, (1, 3, 2))
    over_xy = swap(sum_for_y(over_x), "y")
    rows = sum_for_z(over_yx, over_xy).reshape(NZ * NC * NY, BLK // NC // NY, 2 * TN)
    pieces = swap(rows, ("z", "c", "y")).reshape(NZ, NC * NY, BLK // NC // NY, 2 * TN)
    pieces = jnp.sum(pieces.astype(F32), axis=0)
    grad = jnp.concatenate(
        [pieces[h * NY + k, :, f * TN : (f + 1) * TN] for h in range(NC) for f in range(2) for k in range(NY)], axis=-1
    )
    new_moment = 0.9 * moment + 0.1 * grad
    new_second = 0.95 * second + 0.05 * grad * grad
    corr_one = 1.0 - 0.9**10
    corr_two = 1.0 - 0.95**10
    update = new_moment / corr_one / (jnp.sqrt(new_second / corr_two) + 1e-08)
    new_master = master - 0.02 * (update + 0.1 * master)
    every = exchange([new_master.astype(BF16)] * NY, "y", NY, (1, 2, 3))
    params = jnp.concatenate([lax.select_n(lax.rem(y - k + NY, NY), *every) for k in range(NY)], axis=0)
    return (new_master, new_moment, new_second, params)


def solution(mesh):
    fine = Mesh(mesh.devices.reshape(NZ, NX, NC, NY), ("z", "x", "c", "y"))
    split = P(("z", "x", "c", "y"), None)
    return jax.shard_map(
        body,
        mesh=fine,
        in_specs=(split,) * 5,
        out_specs=(split, split, split, P(("z", "x", "c"), None)),
        check_vma=False,
    )
```

time: 134 us -> 130 us (0.970)
  blocking collectives: 0 us -> 30.4 us
  waiting for transfers between devices: 55.4 us -> 36 us
  starting transfers between devices: 39.2 us -> 21.7 us
  local copies, waits for them, and re-layouts: 1.65 us -> 4.68 us
  Pallas kernels: 34.4 us -> 32.9 us
    ppermute x25 -> x11, waiting for transfers between devices: 55.4 us -> 10.4 us  [shift(): return lax.ppermute(v, axis, [(i, (i + s) % n) for i in range(n)])]
    all_to_all x0 -> x1, blocking collectives: none -> 30.4 us  [swap(): return lax.all_to_all(v, axes, 0, 0, tiled=True)]
    ppermute x25 -> x11, starting transfers between devices: 39.2 us -> 13.3 us  [shift(): return lax.ppermute(v, axis, [(i, (i + s) % n) for i in range(n)])]
    all_to_all x0 -> x2, waiting for transfers between devices: none -> 25.6 us  [swap(): return lax.all_to_all(v, axes, 0, 0, tiled=True)]
    all_to_all x0 -> x2, starting transfers between devices: none -> 8.4 us  [swap(): return lax.all_to_all(v, axes, 0, 0, tiled=True)]
    unnamed x8 -> x31, local copies, waits for them, and re-layouts: 1.65 us -> 4.55 us
    pallas_call x1, Pallas kernels: 8.42 us -> 6.32 us  [product_for_x(): pl.pallas_call(kernel, grid_spec=pltpu.PrefetchScalarGridSpec(num_scalar_...]
    pallas_call x2, Pallas kernels: 14.4 us -> 12.3 us  [product(): pl.pallas_call(kernel, grid_spec=pltpu.PrefetchScalarGridSpec(num_scalar_...]
  transfers between devices with their start and end apart: 25 -> 13, of which waited for: 16 -> 6; matrix products, arithmetic and copies ran while one was open for 0% -> 0% of each run, Pallas kernels for 19% -> 21%
where the time goes in v4:
time: 130 us; the launch traced here: 128 us
  waiting for transfers between devices  36 us (28%)
  Pallas kernels  32.9 us (25%)
  blocking collectives  30.4 us (23%)
  starting transfers between devices  21.7 us (17%)
  local copies, waits for them, and re-layouts  4.68 us (4%)
  other arithmetic  1.8 us (1%)
    all_to_all x1, blocking collectives, swap(): return lax.all_to_all(v, axes, 0, 0, tiled=True)  30.4 us
    all_to_all x2, waiting for transfers between devices, swap(): return lax.all_to_all(v, axes, 0, 0, tiled=True)  25.6 us
    ppermute x11, starting transfers between devices, shift(): return lax.ppermute(v, axis, [(i, (i + s) % n) for i in range(n)])  13.3 us
    pallas_call x2, Pallas kernels, product(): pl.pallas_call(kernel, grid_spec=pltpu.PrefetchScalarGridSpec(num_scalar_...  12.3 us
    ppermute x11, waiting for transfers between devices, shift(): return lax.ppermute(v, axis, [(i, (i + s) % n) for i in range(n)])  10.4 us
    all_to_all x2, starting transfers between devices, swap(): return lax.all_to_all(v, axes, 0, 0, tiled=True)  8.4 us
    pallas_call x1, Pallas kernels, product_for_y(): pl.pallas_call(kernel, grid_spec=pltpu.PrefetchScalarGridSpec(num_scalar_...  7.98 us
    pallas_call x1, Pallas kernels, product_for_x(): pl.pallas_call(kernel, grid_spec=pltpu.PrefetchScalarGridSpec(num_scalar_...  6.32 us
  transfers between devices with their start and end apart: 13, of which 6 were waited for; matrix products, arithmetic and copies ran while one was open for 0% of the time, Pallas kernels for 21%

profile of v4, /device:TPU:1, one launch (start us, length us, event | category | flops | bytes accessed | tf_op | source)
XLA Modules:
  0.0 128.5 jit_solution(6257252863984745658)
XLA Ops:
  0.7 1.9 %copy-done = bf16[1024,1536]{1,0:T(8,128)(2,1)S(1)} copy-done((bf16[1024,1536]{1,0:T(8,128)(2,1)S(1)}, bf16[1024,1536]{1,0:T(8,128)(2,1)}, u32[]{:S(2)}) %copy-start) | copy-done | bytes 3145752
  2.6 5.7 %product_theirs.3 = bf16[1536,1024]{1,0:T(8,128)(2,1)S(1)} custom-call(s32[3]{0:T(128)S(1)} %pad_add_fusion.idx_ref, bf16[1024,1536]{1,0:T(8,128)(2,1)S(1)} %copy-done, bf16[1024,4096]{1,0:T(8,128)(2,1)} %c.7), custom_call_target="tpu_custom_call" | custom-call | flops 3221225472 | bytes 8388608 | tf_op jit(solution)/shard_map/product_theirs/pallas_call | solution.py:46
  8.3 3.3 %collective-permute-start.7 = (bf16[1536,1024]{1,0:T(8,128)(2,1)S(1)}, bf16[1536,1024]{1,0:T(8,128)(2,1)S(1)}, u32[]{:S(2)}, u32[]{:S(2)}) collective-permute-start(bf16[1536,1024]{1,0:T(8,128)(2,1)S(1)} %product_theirs.3), channel_id=1, source_target_pairs={{0,4},{4,0},{1,5},{5,1},{2,6},{6,2},{3,7},{7,3},{8,12},{12,8},{9,1... | collective-permute-start | bytes 9437192 | tf_op jit(solution)/shard_map/ppermute | solution.py:29
  11.7 6.6 %product_theirs.2 = bf16[1536,1024]{1,0:T(8,128)(2,1)} custom-call(s32[3]{0:T(128)S(1)} %pad_add_fusion.idx_ref, bf16[1024,1536]{1,0:T(8,128)(2,1)S(1)} %copy-done, bf16[1024,4096]{1,0:T(8,128)(2,1)} %c.7), custom_call_target="tpu_custom_call" | custom-call | flops 3221225472 | bytes 8388608 | tf_op jit(solution)/shard_map/product_theirs/pallas_call | solution.py:46
  18.3 6.3 %product_for_x.1 = bf16[4,8,48,1024]{3,2,1,0:T(8,128)(2,1)S(1)} custom-call(s32[3]{0:T(128)S(1)} %pad_add_fusion.idx_ref, bf16[1024,1536]{1,0:T(8,128)(2,1)S(1)} %copy-done, bf16[1024,4096]{1,0:T(8,128)(2,1)} %c.7, bf16[1536,1024]{1,0:T(8,128)(2,1)S(1)} %collective-permute-done.7.r), custom_call_target="tpu_custom_call" | custom-call | flops 3221225472 | bytes 11534336 | tf_op jit(solution)/shard_map/product_for_x/pallas_call | solution.py:97
  24.6 1.7 %copy-done.2 = bf16[4,8,48,1024]{3,2,1,0:T(8,128)(2,1)} copy-done((bf16[4,8,48,1024]{3,2,1,0:T(8,128)(2,1)}, bf16[4,8,48,1024]{3,2,1,0:T(8,128)(2,1)S(1)}, u32[]{:S(2)}) %copy-start.2) | copy-done | bytes 3145752
  26.3 4.9 %all-to-all-start = ((bf16[4,8,48,1024]{3,2,1,0:T(8,128)(2,1)}), bf16[4,8,48,1024]{3,2,1,0:T(8,128)(2,1)}, u32[]{:S(2)}, u32[]{:S(2)}) async-start(bf16[4,8,48,1024]{3,2,1,0:T(8,128)(2,1)} %copy-done.2), calls=%async_computation | async-start | bytes 6291456 | tf_op jit(solution)/shard_map/all_to_all | solution.py:37
  31.3 8.0 %product_for_y.1 = (bf16[1536,256]{1,0:T(8,128)(2,1)S(1)}, bf16[1536,256]{1,0:T(8,128)(2,1)}, bf16[1536,256]{1,0:T(8,128)(2,1)}, bf16[1536,256]{1,0:T(8,128)(2,1)}) custom-call(s32[3]{0:T(128)S(1)} %pad_add_fusion.idx_ref, bf16[1024,1536]{1,0:T(8,128)(2,1)S(1)} %copy-done.1, bf16[1024,4096]{1,0:T(8,128)(2,1)} %c.7, bf16[1536,1024]{1,0:T(8,128)(2,1)} %collective-permute-done.r), custom_call_target="tpu_custom_call" | custom-call | flops 3221225472 | bytes 11534336 | tf_op jit(solution)/shard_map/product_for_y/pallas_call | solution.py:72
  39.2 0.9 copy-done.3
  40.1 2.7 %collective-permute-start.2 = (bf16[1536,256]{1,0:T(8,128)(2,1)}, bf16[1536,256]{1,0:T(8,128)(2,1)S(1)}, u32[]{:S(2)}, u32[]{:S(2)}) collective-permute-start(bf16[1536,256]{1,0:T(8,128)(2,1)} %get-tuple-element.14), channel_id=1, source_target_pairs={{0,3},{1,0},{2,1},{3,2},{4,7},{5,4},{6,5},{7,6},{8,11},{9,8},{10,9... | collective-permute-start | bytes 2359304 | tf_op jit(solution)/shard_map/ppermute | solution.py:29
  42.8 25.6 %all-to-all-done.r = bf16[4,8,48,1024]{3,2,1,0:T(8,128)(2,1)} async-done(((bf16[4,8,48,1024]{3,2,1,0:T(8,128)(2,1)}), bf16[4,8,48,1024]{3,2,1,0:T(8,128)(2,1)}, u32[]{:S(2)}, u32[]{:S(2)}) %all-to-all-start) | async-done | bytes 3145760 | tf_op jit(solution)/shard_map/all_to_all | solution.py:37
  68.5 3.9 %sum_for_y.1 = bf16[4,8,48,256]{3,2,1,0:T(8,128)(2,1)} custom-call(bf16[4,8,48,1024]{3,2,1,0:T(8,128)(2,1)} %all-to-all-done.r), custom_call_target="tpu_custom_call" | custom-call | flops 1572864 | bytes 3932160 | tf_op jit(solution)/shard_map/sum_for_y/pallas_call | solution.py:151
  72.4 3.5 %all-to-all-start.1 = ((bf16[4,8,48,256]{3,2,1,0:T(8,128)(2,1)}), bf16[4,8,48,256]{3,2,1,0:T(8,128)(2,1)S(1)}, u32[]{:S(2)}, u32[]{:S(2)}) async-start(bf16[4,8,48,256]{3,2,1,0:T(8,128)(2,1)} %sum_for_y.1), calls=%async_computation.1 | async-start | bytes 1572864 | tf_op jit(solution)/shard_map/all_to_all | solution.py:37
  76.7 2.1 %sum_for_x.1 = (bf16[8,48,256]{2,1,0:T(8,128)(2,1)S(1)}, bf16[8,48,256]{2,1,0:T(8,128)(2,1)S(1)}, bf16[8,48,256]{2,1,0:T(8,128)(2,1)S(1)}, bf16[8,48,256]{2,1,0:T(8,128)(2,1)S(1)}) custom-call(s32[3]{0:T(128)S(1)} %pad_add_fusion.idx_ref, bf16[8,4,48,256]{3,2,1,0:T(8,128)(2,1)S(1)} %bitcast.73, bf16[8,4,48,256]{3,2,1,0:T(8,128)(2,1)S(1)} %bitcast.74, ...), custom_call_target="tpu_custom_call" | custom-call | flops 1572864 | bytes 3932160 | tf_op jit(solution)/shard_map/sum_for_x/pallas_call | solution.py:128
  78.8 1.1 collective-permute-start.4
  79.9 1.6 %collective-permute-start.5 = (bf16[8,48,256]{2,1,0:T(8,128)(2,1)S(1)}, bf16[8,48,256]{2,1,0:T(8,128)(2,1)S(1)}, u32[]{:S(2)}, u32[]{:S(2)}) collective-permute-start(bf16[8,48,256]{2,1,0:T(8,128)(2,1)S(1)} %get-tuple-element.18), channel_id=1, source_target_pairs={{0,24},{8,0},{16,8},{24,16},{1,25},{9,1},{17,9},{25,17},{2,26},{10... | collective-permute-start | bytes 589832 | tf_op jit(solution)/shard_map/ppermute | solution.py:29
  81.5 1.4 %collective-permute-start.6 = (bf16[8,48,256]{2,1,0:T(8,128)(2,1)S(1)}, bf16[8,48,256]{2,1,0:T(8,128)(2,1)S(1)}, u32[]{:S(2)}, u32[]{:S(2)}) collective-permute-start(bf16[8,48,256]{2,1,0:T(8,128)(2,1)S(1)} %get-tuple-element.19), channel_id=1, source_target_pairs={{0,16},{8,24},{16,0},{24,8},{1,17},{9,25},{17,1},{25,9},{2,18},{10... | collective-permute-start | bytes 589832 | tf_op jit(solution)/shard_map/ppermute | solution.py:29
  82.9 2.0 %collective-permute-done.4.refs_1_ = bf16[8,48,256]{2,1,0:T(8,128)(2,1)S(1)} collective-permute-done((bf16[8,48,256]{2,1,0:T(8,128)(2,1)S(1)}, bf16[8,48,256]{2,1,0:T(8,128)(2,1)S(1)}, u32[]{:S(2)}, u32[]{:S(2)}) %collective-permute-start.4) | collective-permute-done | bytes 196640 | tf_op jit(solution)/shard_map/ppermute | solution.py:29
  84.9 1.0 collective-permute-done.5.refs_2_
  85.9 2.8 %collective-permute-done.6.refs_3_ = bf16[8,48,256]{2,1,0:T(8,128)(2,1)S(1)} collective-permute-done((bf16[8,48,256]{2,1,0:T(8,128)(2,1)S(1)}, bf16[8,48,256]{2,1,0:T(8,128)(2,1)S(1)}, u32[]{:S(2)}, u32[]{:S(2)}) %collective-permute-start.6) | collective-permute-done | bytes 196640 | tf_op jit(solution)/shard_map/ppermute | solution.py:29
  89.2 30.4 %all_to_all.15 = bf16[64,6,512]{2,1,0:T(8,128)(2,1)S(1)} all-to-all(bf16[64,6,512]{2,1,0:T(8,128)(2,1)S(1)} %reshape.30), channel_id=1, replica_groups=mesh['z'=8,'x'=4,'c'=2,'y'=4] {'z','c','y'}, dimensions={0} | all-to-all | bytes 786432 | tf_op jit(solution)/shard_map/all_to_all | solution.py:37
  120.8 1.9 %collective-permute-start.10 = (bf16[6,4096]{1,0:T(8,128)(2,1)S(1)}, bf16[6,4096]{1,0:T(8,128)(2,1)S(1)}, u32[]{:S(2)}, u32[]{:S(2)}) collective-permute-start(bf16[6,4096]{1,0:T(8,128)(2,1)S(1)} %get-tuple-element.20), channel_id=1, source_target_pairs={{0,3},{1,0},{2,1},{3,2},{4,7},{5,4},{6,5},{7,6},{8,11},{9,8},{10,9... | collective-permute-start | bytes 147464 | tf_op jit(solution)/shard_map/ppermute | solution.py:29
  122.6 1.3 %collective-permute-start.9 = (bf16[6,4096]{1,0:T(8,128)(2,1)S(1)}, bf16[6,4096]{1,0:T(8,128)(2,1)S(1)}, u32[]{:S(2)}, u32[]{:S(2)}) collective-permute-start(bf16[6,4096]{1,0:T(8,128)(2,1)S(1)} %get-tuple-element.20), channel_id=1, source_target_pairs={{0,2},{1,3},{2,0},{3,1},{4,6},{5,7},{6,4},{7,5},{8,10},{9,11},{10,... | collective-permute-start | bytes 147464 | tf_op jit(solution)/shard_map/ppermute | solution.py:29
  124.0 3.7 %collective-permute-done.8 = bf16[6,4096]{1,0:T(8,128)(2,1)S(1)} collective-permute-done((bf16[6,4096]{1,0:T(8,128)(2,1)S(1)}, bf16[6,4096]{1,0:T(8,128)(2,1)S(1)}, u32[]{:S(2)}, u32[]{:S(2)}) %collective-permute-start.8) | collective-permute-done | bytes 49184 | tf_op jit(solution)/shard_map/ppermute | solution.py:29
  (48 shorter events, 3.2 us)
Async XLA Ops:
  0.7 1.9 %copy-start = (bf16[1024,1536]{1,0:T(8,128)(2,1)S(1)}, bf16[1024,1536]{1,0:T(8,128)(2,1)}, u32[]{:S(2)}) copy-start(bf16[1024,1536]{1,0:T(8,128)(2,1)} %a.7) | copy-start | bytes 9437188
  8.3 10.0 %collective-permute-start.7 = (bf16[1536,1024]{1,0:T(8,128)(2,1)S(1)}, bf16[1536,1024]{1,0:T(8,128)(2,1)S(1)}, u32[]{:S(2)}, u32[]{:S(2)}) collective-permute-start(bf16[1536,1024]{1,0:T(8,128)(2,1)S(1)} %product_theirs.3), channel_id=1, source_target_pairs={{0,4},{4,0},{1,5},{5,1},{2,6},{6,2},{3,7},{7,3},{8,12},{12,8},{9,1... | collective-permute-start | bytes 9437192 | tf_op jit(solution)/shard_map/ppermute | solution.py:29
  18.3 12.9 %collective-permute-start = (bf16[1536,1024]{1,0:T(8,128)(2,1)}, bf16[1536,1024]{1,0:T(8,128)(2,1)}, u32[]{:S(2)}, u32[]{:S(2)}) collective-permute-start(bf16[1536,1024]{1,0:T(8,128)(2,1)} %product_theirs.2), channel_id=1, source_target_pairs={{0,4},{4,0},{1,5},{5,1},{2,6},{6,2},{3,7},{7,3},{8,12},{12,8},{9,1... | collective-permute-start | bytes 9437192 | tf_op jit(solution)/shard_map/ppermute | solution.py:29
  24.6 1.7 %copy-start.2 = (bf16[4,8,48,1024]{3,2,1,0:T(8,128)(2,1)}, bf16[4,8,48,1024]{3,2,1,0:T(8,128)(2,1)S(1)}, u32[]{:S(2)}) copy-start(bf16[4,8,48,1024]{3,2,1,0:T(8,128)(2,1)S(1)} %product_for_x.1) | copy-start | bytes 9437188
  26.3 4.9 %copy-start.1 = (bf16[1024,1536]{1,0:T(8,128)(2,1)S(1)}, bf16[1024,1536]{1,0:T(8,128)(2,1)}, u32[]{:S(2)}) copy-start(bf16[1024,1536]{1,0:T(8,128)(2,1)} %a.7) | copy-start | bytes 9437188
  26.3 42.1 %all-to-all-start = ((bf16[4,8,48,1024]{3,2,1,0:T(8,128)(2,1)}), bf16[4,8,48,1024]{3,2,1,0:T(8,128)(2,1)}, u32[]{:S(2)}, u32[]{:S(2)}) async-start(bf16[4,8,48,1024]{3,2,1,0:T(8,128)(2,1)} %copy-done.2), calls=%async_computation | async-start | bytes 6291456 | tf_op jit(solution)/shard_map/all_to_all | solution.py:37
  39.2 0.9 copy-start.3
  40.1 36.6 %copy-start.4 = (bf16[1536,256]{1,0:T(8,128)(2,1)S(1)}, bf16[1536,256]{1,0:T(8,128)(2,1)}, u32[]{:S(2)}) copy-start(bf16[1536,256]{1,0:T(8,128)(2,1)} %copy-done.3) | copy-start | bytes 2359300
  40.1 35.8 %collective-permute-start.1 = (bf16[1536,256]{1,0:T(8,128)(2,1)}, bf16[1536,256]{1,0:T(8,128)(2,1)S(1)}, u32[]{:S(2)}, u32[]{:S(2)}) collective-permute-start(bf16[1536,256]{1,0:T(8,128)(2,1)} %get-tuple-element.13), channel_id=1, source_target_pairs={{0,1},{1,2},{2,3},{3,0},{4,5},{5,6},{6,7},{7,4},{8,9},{9,10},{10,1... | collective-permute-start | bytes 2359304 | tf_op jit(solution)/shard_map/ppermute | solution.py:29
  40.1 35.8 %collective-permute-start.2 = (bf16[1536,256]{1,0:T(8,128)(2,1)}, bf16[1536,256]{1,0:T(8,128)(2,1)S(1)}, u32[]{:S(2)}, u32[]{:S(2)}) collective-permute-start(bf16[1536,256]{1,0:T(8,128)(2,1)} %get-tuple-element.14), channel_id=1, source_target_pairs={{0,3},{1,0},{2,1},{3,2},{4,7},{5,4},{6,5},{7,6},{8,11},{9,8},{10,9... | collective-permute-start | bytes 2359304 | tf_op jit(solution)/shard_map/ppermute | solution.py:29
  42.8 33.9 %collective-permute-start.3 = (bf16[1536,256]{1,0:T(8,128)(2,1)}, bf16[1536,256]{1,0:T(8,128)(2,1)}, u32[]{:S(2)}, u32[]{:S(2)}) collective-permute-start(bf16[1536,256]{1,0:T(8,128)(2,1)} %get-tuple-element.15), channel_id=1, source_target_pairs={{0,2},{1,3},{2,0},{3,1},{4,6},{5,7},{6,4},{7,5},{8,10},{9,11},{10,... | collective-permute-start | bytes 2359304 | tf_op jit(solution)/shard_map/ppermute | solution.py:29
  72.4 16.4 %all-to-all-start.1 = ((bf16[4,8,48,256]{3,2,1,0:T(8,128)(2,1)}), bf16[4,8,48,256]{3,2,1,0:T(8,128)(2,1)S(1)}, u32[]{:S(2)}, u32[]{:S(2)}) async-start(bf16[4,8,48,256]{3,2,1,0:T(8,128)(2,1)} %sum_for_y.1), calls=%async_computation.1 | async-start | bytes 1572864 | tf_op jit(solution)/shard_map/all_to_all | solution.py:37
  78.8 41.2 %copy-start.5 = (f32[6,4096]{1,0:T(8,128)S(1)}, f32[6,4096]{1,0:T(8,128)}, u32[]{:S(2)}) copy-start(f32[6,4096]{1,0:T(8,128)} %param.7) | copy-start | bytes 294916
  78.8 41.2 %copy-start.6 = (f32[6,4096]{1,0:T(8,128)S(1)}, f32[6,4096]{1,0:T(8,128)}, u32[]{:S(2)}) copy-start(f32[6,4096]{1,0:T(8,128)} %param.8) | copy-start | bytes 294916
  78.8 41.2 %copy-start.7 = (f32[6,4096]{1,0:T(8,128)S(1)}, f32[6,4096]{1,0:T(8,128)}, u32[]{:S(2)}) copy-start(f32[6,4096]{1,0:T(8,128)} %param.9) | copy-start | bytes 294916
  78.8 6.1 %collective-permute-start.4 = (bf16[8,48,256]{2,1,0:T(8,128)(2,1)S(1)}, bf16[8,48,256]{2,1,0:T(8,128)(2,1)S(1)}, u32[]{:S(2)}, u32[]{:S(2)}) collective-permute-start(bf16[8,48,256]{2,1,0:T(8,128)(2,1)S(1)} %get-tuple-element.17), channel_id=1, source_target_pairs={{0,8},{8,16},{16,24},{24,0},{1,9},{9,17},{17,25},{25,1},{2,10},{10... | collective-permute-start | bytes 589832 | tf_op jit(solution)/shard_map/ppermute | solution.py:29
  79.9 6.0 %collective-permute-start.5 = (bf16[8,48,256]{2,1,0:T(8,128)(2,1)S(1)}, bf16[8,48,256]{2,1,0:T(8,128)(2,1)S(1)}, u32[]{:S(2)}, u32[]{:S(2)}) collective-permute-start(bf16[8,48,256]{2,1,0:T(8,128)(2,1)S(1)} %get-tuple-element.18), channel_id=1, source_target_pairs={{0,24},{8,0},{16,8},{24,16},{1,25},{9,1},{17,9},{25,17},{2,26},{10... | collective-permute-start | bytes 589832 | tf_op jit(solution)/shard_map/ppermute | solution.py:29
  81.5 7.2 %collective-permute-start.6 = (bf16[8,48,256]{2,1,0:T(8,128)(2,1)S(1)}, bf16[8,48,256]{2,1,0:T(8,128)(2,1)S(1)}, u32[]{:S(2)}, u32[]{:S(2)}) collective-permute-start(bf16[8,48,256]{2,1,0:T(8,128)(2,1)S(1)} %get-tuple-element.19), channel_id=1, source_target_pairs={{0,16},{8,24},{16,0},{24,8},{1,17},{9,25},{17,1},{25,9},{2,18},{10... | collective-permute-start | bytes 589832 | tf_op jit(solution)/shard_map/ppermute | solution.py:29
  120.8 3.2 %collective-permute-start.10 = (bf16[6,4096]{1,0:T(8,128)(2,1)S(1)}, bf16[6,4096]{1,0:T(8,128)(2,1)S(1)}, u32[]{:S(2)}, u32[]{:S(2)}) collective-permute-start(bf16[6,4096]{1,0:T(8,128)(2,1)S(1)} %get-tuple-element.20), channel_id=1, source_target_pairs={{0,3},{1,0},{2,1},{3,2},{4,7},{5,4},{6,5},{7,6},{8,11},{9,8},{10,9... | collective-permute-start | bytes 147464 | tf_op jit(solution)/shard_map/ppermute | solution.py:29
  122.6 5.0 %collective-permute-start.8 = (bf16[6,4096]{1,0:T(8,128)(2,1)S(1)}, bf16[6,4096]{1,0:T(8,128)(2,1)S(1)}, u32[]{:S(2)}, u32[]{:S(2)}) collective-permute-start(bf16[6,4096]{1,0:T(8,128)(2,1)S(1)} %get-tuple-element.20), channel_id=1, source_target_pairs={{0,1},{1,2},{2,3},{3,0},{4,5},{5,6},{6,7},{7,4},{8,9},{9,10},{10,1... | collective-permute-start | bytes 147464 | tf_op jit(solution)/shard_map/ppermute | solution.py:29
  122.6 5.0 %collective-permute-start.9 = (bf16[6,4096]{1,0:T(8,128)(2,1)S(1)}, bf16[6,4096]{1,0:T(8,128)(2,1)S(1)}, u32[]{:S(2)}, u32[]{:S(2)}) collective-permute-start(bf16[6,4096]{1,0:T(8,128)(2,1)S(1)} %get-tuple-element.20), channel_id=1, source_target_pairs={{0,2},{1,3},{2,0},{3,1},{4,6},{5,7},{6,4},{7,5},{8,10},{9,11},{10,... | collective-permute-start | bytes 147464 | tf_op jit(solution)/shard_map/ppermute | solution.py:29

commit v5 on v4

--- a/solution.py
+++ b/solution.py
@@ -37,7 +37,7 @@
     return lax.all_to_all(v, axes, 0, 0, tiled=True)
 
 
-def product(acts, cot, idx, base, ncols):
+def product_mine(acts, cot, idx, base, ncols):
     tn = 2 * TN
 
     def kernel(idx_ref, a, c, o):
@@ -50,19 +50,42 @@
             grid=(ncols // tn,),
             in_specs=[
                 pl.BlockSpec((T, D), lambda j, s: (0, 0)),
-                pl.BlockSpec((T, tn), lambda j, s: (0, (1 - s[0]) * (HALF // tn) + base // tn + j)),
+                pl.BlockSpec((T, tn), lambda j, s: (0, s[0] * (HALF // tn) + base // tn + j)),
             ],
             out_specs=pl.BlockSpec((D, tn), lambda j, s: (0, j)),
         ),
         out_shape=jax.ShapeDtypeStruct((D, ncols), BF16),
-        name="product_theirs",
+        name="product_mine",
         **params_of(2 * T * D * ncols, 2 * (T * D + T * ncols + D * ncols)),
     )(idx, acts, cot)
 
 
-def product_for_y(acts, cot, got, idx, base):
-    def kernel(idx_ref, a, c, r, *outs):
-        acc = lax.dot_general(a[...], c[...], DN, preferred_element_type=F32) + r[...].astype(F32)
+def product_for_x(acts, cot, mine, ncols):
+    def kernel(a, c, m, o):
+        acc = lax.dot_general(a[...], c[...], DN, preferred_element_type=F32) + m[...].astype(F32)
+        acc = acc.astype(BF16).reshape(NZ, NX, BLK, TN)
+        for x in range(NX):
+            o[x] = acc[:, x]
+
+    return pl.pallas_call(
+        kernel,
+        grid=(ncols // TN,),
+        in_specs=[
+            pl.BlockSpec((T, D), lambda j: (0, 0)),
+            pl.BlockSpec((T, TN), lambda j: (0, j)),
+            pl.BlockSpec((D, TN), lambda j: (0, j)),
+        ],
+        out_specs=pl.BlockSpec((NX, NZ, BLK, TN), lambda j: (0, 0, 0, j)),
+        out_shape=jax.ShapeDtypeStruct((NX, NZ, BLK, ncols), BF16),
+        name="product_for_x",
+        **params_of(2 * T * D * ncols, 2 * (T * D + T * ncols + 2 * D * ncols)),
+    )(acts, cot, mine)
+
+
+def product_for_y(acts, cot, acts_other, cot_other, idx, base):
+    def kernel(idx_ref, a, c, a2, c2, *outs):
+        acc = lax.dot_general(a[...], c[...], DN, preferred_element_type=F32)
+        acc = acc + lax.dot_general(a2[...], c2[...], DN, preferred_element_type=F32)
         for o in range(NY):
 
             @pl.when(pl.program_id(0) == o)
@@ -77,39 +100,15 @@
             in_specs=[
                 pl.BlockSpec((T, D), lambda j, s: (0, 0)),
                 pl.BlockSpec((T, TN), lambda j, s: (0, s[0] * (HALF // TN) + base // TN + lax.rem(s[2] + j, NY))),
-                pl.BlockSpec((D, TN), lambda j, s: (0, lax.rem(s[2] + j, NY))),
+                pl.BlockSpec((T, D), lambda j, s: (0, 0)),
+                pl.BlockSpec((T, TN), lambda j, s: (0, lax.rem(s[2] + j, NY))),
             ],
             out_specs=[pl.BlockSpec((D, TN), lambda j, s: (0, 0))] * NY,
         ),
         out_shape=[jax.ShapeDtypeStruct((D, TN), BF16)] * NY,
         name="product_for_y",
-        **params_of(2 * T * D * TN * NY, 2 * (T * D + T * TN * NY + 2 * D * TN * NY)),
-    )(idx, acts, cot, got)
-
-
-def product_for_x(acts, cot, got, idx, base, ncols):
-    def kernel(idx_ref, a, c, r, o):
-        acc = lax.dot_general(a[...], c[...], DN, preferred_element_type=F32) + r[...].astype(F32)
-        acc = acc.astype(BF16).reshape(NZ, NX, BLK, TN)
-        for x in range(NX):
-            o[x] = acc[:, x]
-
-    return pl.pallas_call(
-        kernel,
-        grid_spec=pltpu.PrefetchScalarGridSpec(
-            num_scalar_prefetch=1,
-            grid=(ncols // TN,),
-            in_specs=[
-                pl.BlockSpec((T, D), lambda j, s: (0, 0)),
-                pl.BlockSpec((T, TN), lambda j, s: (0, s[0] * (HALF // TN) + base // TN + j)),
-                pl.BlockSpec((D, TN), lambda j, s: (0, j)),
-            ],
-            out_specs=pl.BlockSpec((NX, NZ, BLK, TN), lambda j, s: (0, 0, 0, j)),
-        ),
-        out_shape=jax.ShapeDtypeStruct((NX, NZ, BLK, ncols), BF16),
-        name="product_for_x",
-        **params_of(2 * T * D * ncols, 2 * (T * D + T * ncols + 2 * D * ncols)),
-    )(idx, acts, cot, got)
+        **params_of(4 * T * D * TN * NY, 2 * (2 * T * D + 2 * T * TN * NY + D * TN * NY)),
+    )(idx, acts, cot, acts_other, cot_other)
 
 
 def sum_for_x(parts, idx):
@@ -188,12 +187,13 @@
 def body(acts, cotangent, master, moment, second):
     x, c, y = (lax.axis_index(a) for a in ("x", "c", "y"))
     idx = jnp.stack([c, x, y]).astype(jnp.int32)
-    theirs_c = product(acts, cotangent, idx, 0, FLOW_C)
-    got_c = shift(theirs_c, "c", NC, 1)
-    theirs_b = product(acts, cotangent, idx, FLOW_C, FLOW_B)
-    got_b = shift(theirs_b, "c", NC, 1)
-    over_y = exchange(product_for_y(acts, cotangent, got_c, idx, 0), "y", NY, (1, 3, 2))
-    over_x = swap(product_for_x(acts, cotangent, got_b, idx, FLOW_C, FLOW_B), "x")
+    acts_other = shift(acts, "c", NC, 1)
+    columns = lambda base, n: lax.dynamic_slice_in_dim(cotangent, (1 - c) * HALF + base, n, 1)
+    other_b = shift(columns(FLOW_C, FLOW_B), "c", NC, 1)
+    other_c = shift(columns(0, FLOW_C), "c", NC, 1)
+    mine_b = product_mine(acts, cotangent, idx, FLOW_C, FLOW_B)
+    over_x = swap(product_for_x(acts_other, other_b, mine_b, FLOW_B), "x")
+    over_y = exchange(product_for_y(acts, cotangent, acts_other, other_c, idx, 0), "y", NY, (1, 3, 2))
     over_yx = exchange(sum_for_x(over_y, idx), "x", NX, (1, 3, 2))
     over_xy = swap(sum_for_y(over_x), "y")
     rows = sum_for_z(over_yx, over_xy).reshape(NZ * NC * NY, BLK // NC // NY, 2 * TN)

time: 130 us -> 135 us (1.038)
  local copies, waits for them, and re-layouts: 4.68 us -> 11.6 us
  Pallas kernels: 32.9 us -> 28.4 us
  waiting for transfers between devices: 36 us -> 39 us
    ppermute x11 -> x12, waiting for transfers between devices: 10.4 us -> 19 us  [shift(): return lax.ppermute(v, axis, [(i, (i + s) % n) for i in range(n)])]
    pallas_call x3 -> x2, Pallas kernels: 18.7 us -> 12.6 us  [the longest x1 6.8 us: product_for_x(): pl.pallas_call(kernel, grid=(ncols // TN,), in_specs=[pl.BlockSpec((T, D)...]
    all_to_all x2, waiting for transfers between devices: 25.6 us -> 20 us  [swap(): return lax.all_to_all(v, axes, 0, 0, tiled=True)]
    dynamic_slice x0 -> x1, local copies, waits for them, and re-layouts: none -> 4.97 us  [body(): lax.dynamic_slice_in_dim(cotangent, (1 - c) * HALF + base, n, 1)]
    pallas_call x1, Pallas kernels: 7.98 us -> 12.1 us  [product_for_y(): pl.pallas_call(kernel, grid_spec=pltpu.PrefetchScalarGridSpec(num_scalar_...]
    pallas_call x1, Pallas kernels: 3.93 us -> 0.88 us  [sum_for_y(): pl.pallas_call(kernel, grid=(NY,), in_specs=[pl.BlockSpec((NX, NZ, BLK, w...]
    unnamed x31 -> x33, local copies, waits for them, and re-layouts: 4.55 us -> 6.52 us
    ppermute x11 -> x12, starting transfers between devices: 13.3 us -> 14.1 us  [shift(): return lax.ppermute(v, axis, [(i, (i + s) % n) for i in range(n)])]
  transfers between devices with their start and end apart: 13 -> 14, of which waited for: 6 -> 9; matrix products, arithmetic and copies ran while one was open for 0% -> 4% of each run, Pallas kernels for 21% -> 21%
where the time goes in v5:
time: 135 us; the launch traced here: 134 us
  waiting for transfers between devices  39 us (29%)
  blocking collectives  30.4 us (23%)
  Pallas kernels  28.4 us (21%)
  starting transfers between devices  21.3 us (16%)
  local copies, waits for them, and re-layouts  11.6 us (9%)
  other arithmetic  1.8 us (1%)
    all_to_all x1, blocking collectives, swap(): return lax.all_to_all(v, axes, 0, 0, tiled=True)  30.4 us
    all_to_all x2, waiting for transfers between devices, swap(): return lax.all_to_all(v, axes, 0, 0, tiled=True)  20 us
    ppermute x12, waiting for transfers between devices, shift(): return lax.ppermute(v, axis, [(i, (i + s) % n) for i in range(n)])  19 us
    ppermute x12, starting transfers between devices, shift(): return lax.ppermute(v, axis, [(i, (i + s) % n) for i in range(n)])  14.1 us
    pallas_call x1, Pallas kernels, product_for_y(): pl.pallas_call(kernel, grid_spec=pltpu.PrefetchScalarGridSpec(num_scalar_...  12.1 us
    all_to_all x2, starting transfers between devices, swap(): return lax.all_to_all(v, axes, 0, 0, tiled=True)  7.19 us
    pallas_call x1, Pallas kernels, product_for_x(): pl.pallas_call(kernel, grid=(ncols // TN,), in_specs=[pl.BlockSpec((T, D)...  6.8 us
    unnamed x33, local copies, waits for them, and re-layouts  6.52 us
  transfers between devices with their start and end apart: 14, of which 9 were waited for; matrix products, arithmetic and copies ran while one was open for 4% of the time, Pallas kernels for 21%

profile of v5, /device:TPU:1, one launch (start us, length us, event | category | flops | bytes accessed | tf_op | source)
XLA Modules:
  0.0 133.5 jit_solution(5906600460981440774)
XLA Ops:
  0.6 3.3 %collective-permute-start = (bf16[1024,1536]{1,0:T(8,128)(2,1)}, bf16[1024,1536]{1,0:T(8,128)(2,1)}, u32[]{:S(2)}, u32[]{:S(2)}) collective-permute-start(bf16[1024,1536]{1,0:T(8,128)(2,1)} %a.3), channel_id=1, source_target_pairs={{0,4},{4,0},{1,5},{5,1},{2,6},{6,2},{3,7},{7,3},{8,12},{12,8},{9,1... | collective-permute-start | bytes 9437192 | tf_op jit(solution)/shard_map/ppermute | solution.py:29
  4.0 5.0 %constant_dynamic-slice_fusion = (bf16[1024,1024]{1,0:T(8,128)(2,1)}, bf16[1024,1024]{1,0:T(8,128)(2,1)}) fusion(bf16[1024,4096]{1,0:T(8,128)(2,1)} %c.3, s32[]{:T(128)S(6)} %select_n.115, s32[]{:T(128)S(6)} %select_n.114), kind=kLoop, calls=%fused_computation.43 | loop fusion | bytes 8388616 | tf_op jit(solution)/shard_map/dynamic_slice | solution.py:191
  9.5 5.8 %product_mine.1.m = bf16[1536,1024]{1,0:T(8,128)(2,1)S(1)} custom-call(s32[3]{0:T(128)S(1)} %pad_add_fusion.idx_ref, bf16[1024,1536]{1,0:T(8,128)(2,1)S(1)} %copy-done.1, bf16[1024,4096]{1,0:T(8,128)(2,1)} %c.3), custom_call_target="tpu_custom_call" | custom-call | flops 3221225472 | bytes 8388608 | tf_op jit(solution)/shard_map/product_mine/pallas_call | solution.py:46
  15.3 6.8 %product_for_x.1 = bf16[4,8,48,1024]{3,2,1,0:T(8,128)(2,1)S(1)} custom-call(bf16[1024,1536]{1,0:T(8,128)(2,1)} %collective-permute-done.a2.a, bf16[1024,1024]{1,0:T(8,128)(2,1)} %collective-permute-done.8.c, bf16[1536,1024]{1,0:T(8,128)(2,1)S(1)} %product_mine.1.m), custom_call_target="tpu_custom_call" | custom-call | flops 3221225472 | bytes 11534336 | tf_op jit(solution)/shard_map/product_for_x/pallas_call | solution.py:70
  22.2 1.7 %copy-done = bf16[4,8,48,1024]{3,2,1,0:T(8,128)(2,1)} copy-done((bf16[4,8,48,1024]{3,2,1,0:T(8,128)(2,1)}, bf16[4,8,48,1024]{3,2,1,0:T(8,128)(2,1)S(1)}, u32[]{:S(2)}) %copy-start) | copy-done | bytes 3145752
  23.8 3.7 %all-to-all-start = ((bf16[4,8,48,1024]{3,2,1,0:T(8,128)(2,1)}), bf16[4,8,48,1024]{3,2,1,0:T(8,128)(2,1)S(1)}, u32[]{:S(2)}, u32[]{:S(2)}) async-start(bf16[4,8,48,1024]{3,2,1,0:T(8,128)(2,1)} %copy-done), calls=%async_computation | async-start | bytes 6291456 | tf_op jit(solution)/shard_map/all_to_all | solution.py:37
  27.5 1.9 %copy-done.2 = bf16[1024,1536]{1,0:T(8,128)(2,1)S(1)} copy-done((bf16[1024,1536]{1,0:T(8,128)(2,1)S(1)}, bf16[1024,1536]{1,0:T(8,128)(2,1)}, u32[]{:S(2)}) %copy-start.2) | copy-done | bytes 3145752
  29.4 12.1 %product_for_y.1 = (bf16[1536,256]{1,0:T(8,128)(2,1)S(1)}, bf16[1536,256]{1,0:T(8,128)(2,1)}, bf16[1536,256]{1,0:T(8,128)(2,1)}, bf16[1536,256]{1,0:T(8,128)(2,1)}) custom-call(s32[3]{0:T(128)S(1)} %pad_add_fusion.idx_ref, bf16[1024,1536]{1,0:T(8,128)(2,1)S(1)} %copy-done.2, bf16[1024,4096]{1,0:T(8,128)(2,1)} %c.3, ...), custom_call_target="tpu_custom_call" | custom-call | flops 6442450944 | bytes 13631488 | tf_op jit(solution)/shard_map/product_for_y/pallas_call | solution.py:95
  42.4 2.7 %collective-permute-start.3 = (bf16[1536,256]{1,0:T(8,128)(2,1)}, bf16[1536,256]{1,0:T(8,128)(2,1)}, u32[]{:S(2)}, u32[]{:S(2)}) collective-permute-start(bf16[1536,256]{1,0:T(8,128)(2,1)} %get-tuple-element.14), channel_id=1, source_target_pairs={{0,3},{1,0},{2,1},{3,2},{4,7},{5,4},{6,5},{7,6},{8,11},{9,8},{10,9... | collective-permute-start | bytes 2359304 | tf_op jit(solution)/shard_map/ppermute | solution.py:29
  45.3 19.9 %all-to-all-done.r = bf16[4,8,48,1024]{3,2,1,0:T(8,128)(2,1)S(1)} async-done(((bf16[4,8,48,1024]{3,2,1,0:T(8,128)(2,1)}), bf16[4,8,48,1024]{3,2,1,0:T(8,128)(2,1)S(1)}, u32[]{:S(2)}, u32[]{:S(2)}) %all-to-all-start) | async-done | bytes 3145760 | tf_op jit(solution)/shard_map/all_to_all | solution.py:37
  67.1 3.5 %all-to-all-start.1 = ((bf16[4,8,48,256]{3,2,1,0:T(8,128)(2,1)}), bf16[4,8,48,256]{3,2,1,0:T(8,128)(2,1)S(1)}, u32[]{:S(2)}, u32[]{:S(2)}) async-start(bf16[4,8,48,256]{3,2,1,0:T(8,128)(2,1)} %copy-done.3), calls=%async_computation.1 | async-start | bytes 1572864 | tf_op jit(solution)/shard_map/all_to_all | solution.py:37
  70.6 7.6 %collective-permute-done.3 = bf16[1536,256]{1,0:T(8,128)(2,1)} collective-permute-done((bf16[1536,256]{1,0:T(8,128)(2,1)}, bf16[1536,256]{1,0:T(8,128)(2,1)}, u32[]{:S(2)}, u32[]{:S(2)}) %collective-permute-start.3) | collective-permute-done | bytes 786464 | tf_op jit(solution)/shard_map/ppermute | solution.py:29
  78.2 1.2 collective-permute-done.4
  80.6 2.5 %sum_for_x.1 = (bf16[8,48,256]{2,1,0:T(8,128)(2,1)S(1)}, bf16[8,48,256]{2,1,0:T(8,128)(2,1)S(1)}, bf16[8,48,256]{2,1,0:T(8,128)(2,1)S(1)}, bf16[8,48,256]{2,1,0:T(8,128)(2,1)S(1)}) custom-call(s32[3]{0:T(128)S(1)} %pad_add_fusion.idx_ref, bf16[8,4,48,256]{3,2,1,0:T(8,128)(2,1)S(1)} %bitcast.73, bf16[8,4,48,256]{3,2,1,0:T(8,128)(2,1)} %bitcast.4.refs_1_, ...), custom_call_target="tpu_custom_call" | custom-call | flops 1572864 | bytes 3932160 | tf_op jit(solution)/shard_map/sum_for_x/pallas_call | solution.py:127
  83.1 1.2 collective-permute-start.5
  84.4 1.5 %collective-permute-start.6 = (bf16[8,48,256]{2,1,0:T(8,128)(2,1)S(1)}, bf16[8,48,256]{2,1,0:T(8,128)(2,1)S(1)}, u32[]{:S(2)}, u32[]{:S(2)}) collective-permute-start(bf16[8,48,256]{2,1,0:T(8,128)(2,1)S(1)} %get-tuple-element.18), channel_id=1, source_target_pairs={{0,24},{8,0},{16,8},{24,16},{1,25},{9,1},{17,9},{25,17},{2,26},{10... | collective-permute-start | bytes 589832 | tf_op jit(solution)/shard_map/ppermute | solution.py:29
  85.9 1.4 %collective-permute-start.7 = (bf16[8,48,256]{2,1,0:T(8,128)(2,1)S(1)}, bf16[8,48,256]{2,1,0:T(8,128)(2,1)S(1)}, u32[]{:S(2)}, u32[]{:S(2)}) collective-permute-start(bf16[8,48,256]{2,1,0:T(8,128)(2,1)S(1)} %get-tuple-element.19), channel_id=1, source_target_pairs={{0,16},{8,24},{16,0},{24,8},{1,17},{9,25},{17,1},{25,9},{2,18},{10... | collective-permute-start | bytes 589832 | tf_op jit(solution)/shard_map/ppermute | solution.py:29
  87.3 1.6 %collective-permute-done.5.refs_1_ = bf16[8,48,256]{2,1,0:T(8,128)(2,1)S(1)} collective-permute-done((bf16[8,48,256]{2,1,0:T(8,128)(2,1)S(1)}, bf16[8,48,256]{2,1,0:T(8,128)(2,1)S(1)}, u32[]{:S(2)}, u32[]{:S(2)}) %collective-permute-start.5) | collective-permute-done | bytes 196640 | tf_op jit(solution)/shard_map/ppermute | solution.py:29
  89.9 3.2 %collective-permute-done.7.refs_3_ = bf16[8,48,256]{2,1,0:T(8,128)(2,1)S(1)} collective-permute-done((bf16[8,48,256]{2,1,0:T(8,128)(2,1)S(1)}, bf16[8,48,256]{2,1,0:T(8,128)(2,1)S(1)}, u32[]{:S(2)}, u32[]{:S(2)}) %collective-permute-start.7) | collective-permute-done | bytes 196640 | tf_op jit(solution)/shard_map/ppermute | solution.py:29
  93.6 30.4 %all_to_all.15 = bf16[64,6,512]{2,1,0:T(8,128)(2,1)S(1)} all-to-all(bf16[64,6,512]{2,1,0:T(8,128)(2,1)S(1)} %reshape.30), channel_id=1, replica_groups=mesh['z'=8,'x'=4,'c'=2,'y'=4] {'z','c','y'}, dimensions={0} | all-to-all | bytes 786432 | tf_op jit(solution)/shard_map/all_to_all | solution.py:37
  125.1 1.7 %collective-permute-start.10 = (bf16[6,4096]{1,0:T(8,128)(2,1)S(1)}, bf16[6,4096]{1,0:T(8,128)(2,1)S(1)}, u32[]{:S(2)}, u32[]{:S(2)}) collective-permute-start(bf16[6,4096]{1,0:T(8,128)(2,1)S(1)} %get-tuple-element.20), channel_id=1, source_target_pairs={{0,2},{1,3},{2,0},{3,1},{4,6},{5,7},{6,4},{7,5},{8,10},{9,11},{10,... | collective-permute-start | bytes 147464 | tf_op jit(solution)/shard_map/ppermute | solution.py:29
  126.8 1.3 collective-permute-start.11
  128.3 1.4 %collective-permute-done.10 = bf16[6,4096]{1,0:T(8,128)(2,1)S(1)} collective-permute-done((bf16[6,4096]{1,0:T(8,128)(2,1)S(1)}, bf16[6,4096]{1,0:T(8,128)(2,1)S(1)}, u32[]{:S(2)}, u32[]{:S(2)}) %collective-permute-start.10) | collective-permute-done | bytes 49184 | tf_op jit(solution)/shard_map/ppermute | solution.py:29
  129.9 2.8 %collective-permute-done.9 = bf16[6,4096]{1,0:T(8,128)(2,1)S(1)} collective-permute-done((bf16[6,4096]{1,0:T(8,128)(2,1)S(1)}, bf16[6,4096]{1,0:T(8,128)(2,1)S(1)}, u32[]{:S(2)}, u32[]{:S(2)}) %collective-permute-start.9) | collective-permute-done | bytes 49184 | tf_op jit(solution)/shard_map/ppermute | solution.py:29
  (52 shorter events, 8.2 us)
Async XLA Ops:
  0.6 14.7 %collective-permute-start = (bf16[1024,1536]{1,0:T(8,128)(2,1)}, bf16[1024,1536]{1,0:T(8,128)(2,1)}, u32[]{:S(2)}, u32[]{:S(2)}) collective-permute-start(bf16[1024,1536]{1,0:T(8,128)(2,1)} %a.3), channel_id=1, source_target_pairs={{0,4},{4,0},{1,5},{5,1},{2,6},{6,2},{3,7},{7,3},{8,12},{12,8},{9,1... | collective-permute-start | bytes 9437192 | tf_op jit(solution)/shard_map/ppermute | solution.py:29
  4.0 5.6 %copy-start.1 = (bf16[1024,1536]{1,0:T(8,128)(2,1)S(1)}, bf16[1024,1536]{1,0:T(8,128)(2,1)}, u32[]{:S(2)}) copy-start(bf16[1024,1536]{1,0:T(8,128)(2,1)} %a.3) | copy-start | bytes 9437188
  8.9 6.4 %collective-permute-start.8 = (bf16[1024,1024]{1,0:T(8,128)(2,1)}, bf16[1024,1024]{1,0:T(8,128)(2,1)}, u32[]{:S(2)}, u32[]{:S(2)}) collective-permute-start(bf16[1024,1024]{1,0:T(8,128)(2,1)} %get-tuple-element.24), channel_id=1, source_target_pairs={{0,4},{4,0},{1,5},{5,1},{2,6},{6,2},{3,7},{7,3},{8,12},{12,8},{9,1... | collective-permute-start | bytes 6291464 | tf_op jit(solution)/shard_map/ppermute | solution.py:29
  9.0 18.5 %collective-permute-start.1 = (bf16[1024,1024]{1,0:T(8,128)(2,1)}, bf16[1024,1024]{1,0:T(8,128)(2,1)}, u32[]{:S(2)}, u32[]{:S(2)}) collective-permute-start(bf16[1024,1024]{1,0:T(8,128)(2,1)} %get-tuple-element.25), channel_id=1, source_target_pairs={{0,4},{4,0},{1,5},{5,1},{2,6},{6,2},{3,7},{7,3},{8,12},{12,8},{9,1... | collective-permute-start | bytes 6291464 | tf_op jit(solution)/shard_map/ppermute | solution.py:29
  22.1 1.7 %copy-start = (bf16[4,8,48,1024]{3,2,1,0:T(8,128)(2,1)}, bf16[4,8,48,1024]{3,2,1,0:T(8,128)(2,1)S(1)}, u32[]{:S(2)}) copy-start(bf16[4,8,48,1024]{3,2,1,0:T(8,128)(2,1)S(1)} %product_for_x.1) | copy-start | bytes 9437188
  23.8 41.5 %all-to-all-start = ((bf16[4,8,48,1024]{3,2,1,0:T(8,128)(2,1)}), bf16[4,8,48,1024]{3,2,1,0:T(8,128)(2,1)S(1)}, u32[]{:S(2)}, u32[]{:S(2)}) async-start(bf16[4,8,48,1024]{3,2,1,0:T(8,128)(2,1)} %copy-done), calls=%async_computation | async-start | bytes 6291456 | tf_op jit(solution)/shard_map/all_to_all | solution.py:37
  27.5 1.9 %copy-start.2 = (bf16[1024,1536]{1,0:T(8,128)(2,1)S(1)}, bf16[1024,1536]{1,0:T(8,128)(2,1)}, u32[]{:S(2)}) copy-start(bf16[1024,1536]{1,0:T(8,128)(2,1)} %a.3) | copy-start | bytes 9437188
  41.5 0.9 copy-start.4
  42.4 28.2 %collective-permute-start.2 = (bf16[1536,256]{1,0:T(8,128)(2,1)}, bf16[1536,256]{1,0:T(8,128)(2,1)}, u32[]{:S(2)}, u32[]{:S(2)}) collective-permute-start(bf16[1536,256]{1,0:T(8,128)(2,1)} %get-tuple-element.13), channel_id=1, source_target_pairs={{0,1},{1,2},{2,3},{3,0},{4,5},{5,6},{6,7},{7,4},{8,9},{9,10},{10,1... | collective-permute-start | bytes 2359304 | tf_op jit(solution)/shard_map/ppermute | solution.py:29
  42.4 35.8 %collective-permute-start.3 = (bf16[1536,256]{1,0:T(8,128)(2,1)}, bf16[1536,256]{1,0:T(8,128)(2,1)}, u32[]{:S(2)}, u32[]{:S(2)}) collective-permute-start(bf16[1536,256]{1,0:T(8,128)(2,1)} %get-tuple-element.14), channel_id=1, source_target_pairs={{0,3},{1,0},{2,1},{3,2},{4,7},{5,4},{6,5},{7,6},{8,11},{9,8},{10,9... | collective-permute-start | bytes 2359304 | tf_op jit(solution)/shard_map/ppermute | solution.py:29
  45.1 34.3 %collective-permute-start.4 = (bf16[1536,256]{1,0:T(8,128)(2,1)}, bf16[1536,256]{1,0:T(8,128)(2,1)}, u32[]{:S(2)}, u32[]{:S(2)}) collective-permute-start(bf16[1536,256]{1,0:T(8,128)(2,1)} %get-tuple-element.15), channel_id=1, source_target_pairs={{0,2},{1,3},{2,0},{3,1},{4,6},{5,7},{6,4},{7,5},{8,10},{9,11},{10,... | collective-permute-start | bytes 2359304 | tf_op jit(solution)/shard_map/ppermute | solution.py:29
  66.2 0.9 copy-start.3
  67.1 26.0 %all-to-all-start.1 = ((bf16[4,8,48,256]{3,2,1,0:T(8,128)(2,1)}), bf16[4,8,48,256]{3,2,1,0:T(8,128)(2,1)S(1)}, u32[]{:S(2)}, u32[]{:S(2)}) async-start(bf16[4,8,48,256]{3,2,1,0:T(8,128)(2,1)} %copy-done.3), calls=%async_computation.1 | async-start | bytes 1572864 | tf_op jit(solution)/shard_map/all_to_all | solution.py:37
  79.4 1.1 copy-start.5
  83.1 41.2 %copy-start.6 = (f32[6,4096]{1,0:T(8,128)S(1)}, f32[6,4096]{1,0:T(8,128)}, u32[]{:S(2)}) copy-start(f32[6,4096]{1,0:T(8,128)} %param.7) | copy-start | bytes 294916
  83.1 41.2 %copy-start.7 = (f32[6,4096]{1,0:T(8,128)S(1)}, f32[6,4096]{1,0:T(8,128)}, u32[]{:S(2)}) copy-start(f32[6,4096]{1,0:T(8,128)} %param.8) | copy-start | bytes 294916
  83.1 41.2 %copy-start.8 = (f32[6,4096]{1,0:T(8,128)S(1)}, f32[6,4096]{1,0:T(8,128)}, u32[]{:S(2)}) copy-start(f32[6,4096]{1,0:T(8,128)} %param.9) | copy-start | bytes 294916
  83.1 5.8 %collective-permute-start.5 = (bf16[8,48,256]{2,1,0:T(8,128)(2,1)S(1)}, bf16[8,48,256]{2,1,0:T(8,128)(2,1)S(1)}, u32[]{:S(2)}, u32[]{:S(2)}) collective-permute-start(bf16[8,48,256]{2,1,0:T(8,128)(2,1)S(1)} %get-tuple-element.17), channel_id=1, source_target_pairs={{0,8},{8,16},{16,24},{24,0},{1,9},{9,17},{17,25},{25,1},{2,10},{10... | collective-permute-start | bytes 589832 | tf_op jit(solution)/shard_map/ppermute | solution.py:29
  84.4 5.5 %collective-permute-start.6 = (bf16[8,48,256]{2,1,0:T(8,128)(2,1)S(1)}, bf16[8,48,256]{2,1,0:T(8,128)(2,1)S(1)}, u32[]{:S(2)}, u32[]{:S(2)}) collective-permute-start(bf16[8,48,256]{2,1,0:T(8,128)(2,1)S(1)} %get-tuple-element.18), channel_id=1, source_target_pairs={{0,24},{8,0},{16,8},{24,16},{1,25},{9,1},{17,9},{25,17},{2,26},{10... | collective-permute-start | bytes 589832 | tf_op jit(solution)/shard_map/ppermute | solution.py:29
  85.9 7.2 %collective-permute-start.7 = (bf16[8,48,256]{2,1,0:T(8,128)(2,1)S(1)}, bf16[8,48,256]{2,1,0:T(8,128)(2,1)S(1)}, u32[]{:S(2)}, u32[]{:S(2)}) collective-permute-start(bf16[8,48,256]{2,1,0:T(8,128)(2,1)S(1)} %get-tuple-element.19), channel_id=1, source_target_pairs={{0,16},{8,24},{16,0},{24,8},{1,17},{9,25},{17,1},{25,9},{2,18},{10... | collective-permute-start | bytes 589832 | tf_op jit(solution)/shard_map/ppermute | solution.py:29
  125.1 4.6 %collective-permute-start.10 = (bf16[6,4096]{1,0:T(8,128)(2,1)S(1)}, bf16[6,4096]{1,0:T(8,128)(2,1)S(1)}, u32[]{:S(2)}, u32[]{:S(2)}) collective-permute-start(bf16[6,4096]{1,0:T(8,128)(2,1)S(1)} %get-tuple-element.20), channel_id=1, source_target_pairs={{0,2},{1,3},{2,0},{3,1},{4,6},{5,7},{6,4},{7,5},{8,10},{9,11},{10,... | collective-permute-start | bytes 147464 | tf_op jit(solution)/shard_map/ppermute | solution.py:29
  126.8 3.1 %collective-permute-start.11 = (bf16[6,4096]{1,0:T(8,128)(2,1)S(1)}, bf16[6,4096]{1,0:T(8,128)(2,1)S(1)}, u32[]{:S(2)}, u32[]{:S(2)}) collective-permute-start(bf16[6,4096]{1,0:T(8,128)(2,1)S(1)} %get-tuple-element.20), channel_id=1, source_target_pairs={{0,3},{1,0},{2,1},{3,2},{4,7},{5,4},{6,5},{7,6},{8,11},{9,8},{10,9... | collective-permute-start | bytes 147464 | tf_op jit(solution)/shard_map/ppermute | solution.py:29
  128.1 4.6 %collective-permute-start.9 = (bf16[6,4096]{1,0:T(8,128)(2,1)S(1)}, bf16[6,4096]{1,0:T(8,128)(2,1)S(1)}, u32[]{:S(2)}, u32[]{:S(2)}) collective-permute-start(bf16[6,4096]{1,0:T(8,128)(2,1)S(1)} %get-tuple-element.20), channel_id=1, source_target_pairs={{0,1},{1,2},{2,3},{3,0},{4,5},{5,6},{6,7},{7,4},{8,9},{9,10},{10,1... | collective-permute-start | bytes 147464 | tf_op jit(solution)/shard_map/ppermute | solution.py:29

commit v6 on v4

v6 whole, which is shorter than its diff:
```python
import jax
import jax.numpy as jnp
from jax import lax
from jax.experimental import pallas as pl
from jax.experimental.pallas import tpu as pltpu
from jax.sharding import Mesh, PartitionSpec as P

NZ, NX, NC, NY = 8, 4, 2, 4
D, FFW = 1536, 4096
HALF = FFW // 2
TN = 256
BLK = D // (NZ * NX)
OWN = BLK // NC // NY
FLOW_C = 1024
FLOW_B = 1024
T = 1024
F32, BF16 = jnp.float32, jnp.bfloat16
ORDER = (1, 3, 2)
VMEM_LIMIT = 40 * 1024 * 1024
DN = (((0,), (0,)), ((), ()))
WHOLE = pl.BlockSpec(memory_space=pltpu.VMEM)


def params_of(flops, nbytes):
    return dict(
        compiler_params=pltpu.CompilerParams(vmem_limit_bytes=VMEM_LIMIT),
        cost_estimate=pl.CostEstimate(flops=flops, bytes_accessed=nbytes, transcendentals=0),
    )


def shift(v, axis, n, s):
    return lax.ppermute(v, axis, [(i, (i + s) % n) for i in range(n)])


def exchange(pieces, axis, n, order):
    return [pieces[0]] + [shift(pieces[s], axis, n, s) for s in order]


def swap(v, axes):
    return lax.all_to_all(v, axes, 0, 0, tiled=True)


def product(acts, cot, idx, base, ncols):
    tn = 2 * TN

    def kernel(idx_ref, a, c, o):
        o[...] = lax.dot_general(a[...], c[...], DN, preferred_element_type=F32).astype(BF16)

    return pl.pallas_call(
        kernel,
        grid_spec=pltpu.PrefetchScalarGridSpec(
            num_scalar_prefetch=1,
            grid=(ncols // tn,),
            in_specs=[
                WHOLE,
                pl.BlockSpec((T, tn), lambda j, s: (0, (1 - s[0]) * (HALF // tn) + base // tn + j)),
            ],
            out_specs=pl.BlockSpec((D, tn), lambda j, s: (0, j)),
        ),
        out_shape=jax.ShapeDtypeStruct((D, ncols), BF16),
        name="product_theirs",
        **params_of(2 * T * D * ncols, 2 * (T * D + T * ncols + D * ncols)),
    )(idx, acts, cot)


def ahead(idx_ref, axis, o):
    return lax.rem(idx_ref["cxy".index(axis)] + o, 4)


def product_for_y(acts, cot, got, idx, base):
    def kernel(idx_ref, a, c, r, *outs):
        acc = lax.dot_general(a[...], c[...], DN, preferred_element_type=F32) + r[...].astype(F32)
        acc = acc.astype(BF16).reshape(NZ * NX, BLK, TN)
        for o in range(NY):

            @pl.when(pl.program_id(0) == o)
            def _():
                for out, here, there in parts_of(o, NZ * NX // 2):
                    outs[out][there] = acc[here]

    place = lambda j, s: lax.rem(s[2] + j, NY)
    shapes = ring_shapes(NZ * NX, TN)
    return pl.pallas_call(
        kernel,
        grid_spec=pltpu.PrefetchScalarGridSpec(
            num_scalar_prefetch=1,
            grid=(NY,),
            in_specs=[
                WHOLE,
                pl.BlockSpec((T, TN), lambda j, s: (0, s[0] * (HALF // TN) + base // TN + place(j, s))),
                pl.BlockSpec((D, TN), lambda j, s: (0, place(j, s))),
            ],
            out_specs=[pl.BlockSpec(o.shape, lambda j, s: (0, 0, 0)) for o in shapes],
        ),
        out_shape=shapes,
        name="product_for_y",
        **params_of(2 * T * D * TN * NY, 2 * (T * D + T * TN * NY + 2 * D * TN * NY)),
    )(idx, acts, cot, got)


def product_for_x(acts, cot, got, idx, base, ncols):
    tn = 2 * TN

    def kernel(idx_ref, a, c, r, *rest):
        outs, acc = rest[:-1], rest[-1]
        acc[...] = lax.dot_general(a[...], c[...], DN, preferred_element_type=F32) + r[...].astype(F32)
        for o in range(NX):
            x = ahead(idx_ref, "x", o)
            for out, here, there in parts_of(o, NZ // 2):
                for z in range(here.start, here.stop):
                    rows = pl.ds(pl.multiple_of((z * NX + x) * BLK, BLK), BLK)
                    outs[out][z - here.start + there.start] = acc[rows, :].astype(BF16)

    shapes = ring_shapes(NZ, ncols)
    return pl.pallas_call(
        kernel,
        grid_spec=pltpu.PrefetchScalarGridSpec(
            num_scalar_prefetch=1,
            grid=(ncols // tn,),
            in_specs=[
                WHOLE,
                pl.BlockSpec((T, tn), lambda j, s: (0, s[0] * (HALF // tn) + base // tn + j)),
                pl.BlockSpec((D, tn), lambda j, s: (0, j)),
            ],
            out_specs=[pl.BlockSpec(o.shape[:2] + (tn,), lambda j, s: (0, 0, j)) for o in shapes],
            scratch_shapes=[pltpu.VMEM((D, tn), F32)],
        ),
        out_shape=shapes,
        name="product_for_x",
        **params_of(2 * T * D * ncols, 2 * (T * D + T * ncols + 2 * D * ncols)),
    )(idx, acts, cot, got)


def ring_shapes(n, width):
    return [jax.ShapeDtypeStruct((k, BLK, width), BF16) for k in (n, n, n, n // 2, n // 2)]


def parts_of(o, half):
    upper, lower = slice(0, half), slice(half, 2 * half)
    return {
        0: ((0, upper, upper), (0, lower, lower)),
        1: ((3, upper, upper), (1, lower, lower)),
        2: ((1, upper, upper), (2, lower, lower)),
        3: ((2, upper, upper), (4, lower, upper)),
    }[o]


def pass_on(keep_up, keep_down, from_down, from_up):
    half = keep_up.shape[0]

    def kernel(ku, kd, fd, fu, up, down):
        for k in range(half):
            up[k] = (ku[k].astype(F32) + fd[k].astype(F32)).astype(BF16)
            down[k] = (kd[k].astype(F32) + fu[half + k].astype(F32)).astype(BF16)

    return pl.pallas_call(
        kernel,
        in_specs=[WHOLE] * 4,
        out_specs=[WHOLE] * 2,
        out_shape=[jax.ShapeDtypeStruct(keep_up.shape, BF16)] * 2,
        name="pass_on",
        **params_of(2 * keep_up.size, 12 * keep_up.size),
    )(keep_up, keep_down, from_down, from_up)


def ring(pieces, axis):
    own, up, down, keep_up, keep_down = pieces
    from_down, from_up = shift(up, axis, 4, 1), shift(down, axis, 4, 3)
    up, down = pass_on(keep_up, keep_down, from_down, from_up)
    return own, from_down, from_up, shift(up, axis, 4, 1), shift(down, axis, 4, 3)


def total_of(refs, z):
    total = refs[0][z].astype(F32)
    for r in refs[1:]:
        total = total + r[z].astype(F32)
    return total


def sum_and_cut(arrived, idx, axis):
    n = arrived[0].shape[0]

    def kernel(idx_ref, own, from_down, from_up, up, down, *outs):
        for o in range(4):
            t = ahead(idx_ref, axis, o)
            for z in range(NZ):
                if axis == "x":
                    place, rest = z * NX + t, slice(None)
                else:
                    place, rest = z, pl.ds(pl.multiple_of(t * TN, TN), TN)
                total = own[place, :, rest].astype(F32)
                if z < NZ // 2:
                    total = total + from_up[place, :, rest].astype(F32) + up[place, :, rest].astype(F32)
                else:
                    total = total + from_down[place, :, rest].astype(F32) + down[place - n // 2, :, rest].astype(F32)
                outs[o][z] = total.astype(BF16)

    return pl.pallas_call(
        kernel,
        grid_spec=pltpu.PrefetchScalarGridSpec(
            num_scalar_prefetch=1, grid=(1,), in_specs=[WHOLE] * 5, out_specs=[WHOLE] * 4
        ),
        out_shape=[jax.ShapeDtypeStruct((NZ, BLK, TN), BF16)] * 4,
        name="sum_for_" + axis,
        **params_of(4 * D * TN, 10 * D * TN),
    )(idx, *arrived)


def sum_for_z(flows):
    counts = [len(f) for f in flows]

    def kernel(*refs):
        ins, o = refs[:-1], refs[-1]
        for z in range(NZ):
            totals = [total_of(ins[: counts[0]], z), total_of(ins[counts[0] :], z)]
            for y in range(NY):
                rows = [t[h * NY * OWN + y * OWN : h * NY * OWN + (y + 1) * OWN] for t in totals for h in range(NC)]
                o[z * NY + y] = jnp.concatenate(rows, axis=0).astype(BF16)

    return pl.pallas_call(
        kernel,
        in_specs=[WHOLE] * sum(counts),
        out_specs=WHOLE,
        out_shape=jax.ShapeDtypeStruct((NZ * NY, 2 * NC * OWN, TN), BF16),
        name="sum_for_z",
        **params_of(8 * D * TN, 20 * D * TN),
    )(*flows[0], *flows[1])


def settle(flows, c):
    pieces = swap(sum_for_z(flows), ("z", "y")).astype(F32)
    pieces = jnp.sum(pieces.reshape(NZ, NY, 2, NC, OWN, TN), axis=0)
    mine, theirs = [
        lax.select_n(c == h, pieces[:, :, 1], pieces[:, :, 0]).astype(BF16) for h in (0, 1)
    ]
    got = shift(theirs, "c", NC, 1)
    halves = [lax.select_n(c == h, got, mine) for h in range(NC)]
    return jnp.concatenate([p[k, f] for p in halves for f in range(2) for k in range(NY)], axis=-1).astype(F32)


def body(acts, cotangent, master, moment, second):
    x, c, y = (lax.axis_index(a) for a in ("x", "c", "y"))
    idx = jnp.stack([c, x, y]).astype(jnp.int32)
    theirs_c = product(acts, cotangent, idx, 0, FLOW_C)
    got_c = shift(theirs_c, "c", NC, 1)
    theirs_b = product(acts, cotangent, idx, FLOW_C, FLOW_B)
    got_b = shift(theirs_b, "c", NC, 1)
    over_x = ring(product_for_x(acts, cotangent, got_b, idx, FLOW_C, FLOW_B), "x")
    over_y = ring(product_for_y(acts, cotangent, got_c, idx, 0), "y")
    over_xy = exchange(sum_and_cut(over_x, idx, "y"), "y", 4, ORDER)
    over_yx = exchange(sum_and_cut(over_y, idx, "x"), "x", 4, ORDER)
    grad = settle((over_yx, over_xy), c)
    new_moment = 0.9 * moment + 0.1 * grad
    new_second = 0.95 * second + 0.05 * grad * grad
    corr_one = 1.0 - 0.9**10
    corr_two = 1.0 - 0.95**10
    update = new_moment / corr_one / (jnp.sqrt(new_second / corr_two) + 1e-08)
    new_master = master - 0.02 * (update + 0.1 * master)
    every = exchange([new_master.astype(BF16)] * NY, "y", NY, (1, 2, 3))
    params = jnp.concatenate([lax.select_n(lax.rem(y - k + NY, NY), *every) for k in range(NY)], axis=0)
    return (new_master, new_moment, new_second, params)


def solution(mesh):
    fine = Mesh(mesh.devices.reshape(NZ, NX, NC, NY), ("z", "x", "c", "y"))
    split = P(("z", "x", "c", "y"), None)
    return jax.shard_map(
        body,
        mesh=fine,
        in_specs=(split,) * 5,
        out_specs=(split, split, split, P(("z", "x", "c"), None)),
        check_vma=False,
    )
```

time: 130 us -> 114 us (0.88)
  blocking collectives: 30.4 us -> 0 us
  starting transfers between devices: 21.7 us -> 44.5 us
  Pallas kernels: 32.9 us -> 27.8 us
  local copies, waits for them, and re-layouts: 4.68 us -> 2.09 us
    all_to_all x1 -> x0, blocking collectives: 30.4 us -> none  [swap(): return lax.all_to_all(v, axes, 0, 0, tiled=True)]
    ppermute x11 -> x20, starting transfers between devices: 13.3 us -> 34.4 us  [shift(): return lax.ppermute(v, axis, [(i, (i + s) % n) for i in range(n)])]
    ppermute x11 -> x20, waiting for transfers between devices: 10.4 us -> 24.7 us  [shift(): return lax.ppermute(v, axis, [(i, (i + s) % n) for i in range(n)])]
    all_to_all x2 -> x1, waiting for transfers between devices: 25.6 us -> 11.5 us  [swap(): return lax.all_to_all(v, axes, 0, 0, tiled=True)]
    pallas_call x3 -> x5, Pallas kernels: 6.29 us -> 3.06 us  [the longest x2 1.69 us: sum_and_cut(): pl.pallas_call(kernel, grid_spec=pltpu.PrefetchScalarGridSpec(num_scalar_...]
    unnamed x31 -> x24, local copies, waits for them, and re-layouts: 4.55 us -> 2 us
    all_to_all x2 -> x1, starting transfers between devices: 8.4 us -> 10.1 us  [swap(): return lax.all_to_all(v, axes, 0, 0, tiled=True)]
    pallas_call x1, Pallas kernels: 7.98 us -> 6.48 us  [product_for_y(): pl.pallas_call(kernel, grid_spec=pltpu.PrefetchScalarGridSpec(num_scalar_...]
  transfers between devices with their start and end apart: 13 -> 21, of which waited for: 6 -> 13; matrix products, arithmetic and copies ran while one was open for 0% -> 0% of each run, Pallas kernels for 21% -> 19%
where the time goes in v6:
time: 114 us; the launch traced here: 113 us
  starting transfers between devices  44.5 us (39%)
  waiting for transfers between devices  36.2 us (32%)
  Pallas kernels  27.8 us (24%)
  local copies, waits for them, and re-layouts  2.09 us (2%)
  other arithmetic  1.81 us (2%)
    ppermute x20, starting transfers between devices, shift(): return lax.ppermute(v, axis, [(i, (i + s) % n) for i in range(n)])  34.4 us
    ppermute x20, waiting for transfers between devices, shift(): return lax.ppermute(v, axis, [(i, (i + s) % n) for i in range(n)])  24.7 us
    pallas_call x2, Pallas kernels, product(): pl.pallas_call(kernel, grid_spec=pltpu.PrefetchScalarGridSpec(num_scalar_...  11.5 us
    all_to_all x1, waiting for transfers between devices, swap(): return lax.all_to_all(v, axes, 0, 0, tiled=True)  11.5 us
    all_to_all x1, starting transfers between devices, swap(): return lax.all_to_all(v, axes, 0, 0, tiled=True)  10.1 us
    pallas_call x1, Pallas kernels, product_for_x(): pl.pallas_call(kernel, grid_spec=pltpu.PrefetchScalarGridSpec(num_scalar_...  6.67 us
    pallas_call x1, Pallas kernels, product_for_y(): pl.pallas_call(kernel, grid_spec=pltpu.PrefetchScalarGridSpec(num_scalar_...  6.48 us
  transfers between devices with their start and end apart: 21, of which 13 were waited for; matrix products, arithmetic and copies ran while one was open for 0% of the time, Pallas kernels for 19%

profile of v6, /device:TPU:1, one launch (start us, length us, event | category | flops | bytes accessed | tf_op | source)
XLA Modules:
  0.0 113.3 jit_solution(16956200488358456274)
XLA Ops:
  0.7 1.9 %copy-done = bf16[1024,1536]{1,0:T(8,128)(2,1)S(1)} copy-done((bf16[1024,1536]{1,0:T(8,128)(2,1)S(1)}, bf16[1024,1536]{1,0:T(8,128)(2,1)}, u32[]{:S(2)}) %copy-start) | copy-done | bytes 3145752
  2.6 5.8 %product_theirs.3 = bf16[1536,1024]{1,0:T(8,128)(2,1)S(1)} custom-call(s32[3]{0:T(128)S(1)} %pad_add_fusion.idx_ref, bf16[1024,1536]{1,0:T(8,128)(2,1)S(1)} %copy-done, bf16[1024,4096]{1,0:T(8,128)(2,1)} %c.7), custom_call_target="tpu_custom_call" | custom-call | flops 3221225472 | bytes 8388608 | tf_op jit(solution)/shard_map/product_theirs/pallas_call | solution.py:49
  8.4 3.3 %collective-permute-start.8 = (bf16[1536,1024]{1,0:T(8,128)(2,1)S(1)}, bf16[1536,1024]{1,0:T(8,128)(2,1)S(1)}, u32[]{:S(2)}, u32[]{:S(2)}) collective-permute-start(bf16[1536,1024]{1,0:T(8,128)(2,1)S(1)} %product_theirs.3), channel_id=1, source_target_pairs={{0,4},{4,0},{1,5},{5,1},{2,6},{6,2},{3,7},{7,3},{8,12},{12,8},{9,1... | collective-permute-start | bytes 9437192 | tf_op jit(solution)/shard_map/ppermute | solution.py:32
  11.7 5.8 %product_theirs.2 = bf16[1536,1024]{1,0:T(8,128)(2,1)S(1)} custom-call(s32[3]{0:T(128)S(1)} %pad_add_fusion.idx_ref, bf16[1024,1536]{1,0:T(8,128)(2,1)S(1)} %copy-done, bf16[1024,4096]{1,0:T(8,128)(2,1)} %c.7), custom_call_target="tpu_custom_call" | custom-call | flops 3221225472 | bytes 8388608 | tf_op jit(solution)/shard_map/product_theirs/pallas_call | solution.py:49
  17.6 6.7 %product_for_x.1 = (bf16[8,48,1024]{2,1,0:T(8,128)(2,1)S(1)}, bf16[8,48,1024]{2,1,0:T(8,128)(2,1)S(1)}, bf16[8,48,1024]{2,1,0:T(8,128)(2,1)S(1)}, bf16[4,48,1024...) custom-call(s32[3]{0:T(128)S(1)} %pad_add_fusion.idx_ref, bf16[1024,1536]{1,0:T(8,128)(2,1)S(1)} %copy-done, ...), custom_call_target="tpu_custom_call" | custom-call | flops 3221225472 | bytes 11534336 | tf_op jit(solution)/shard_map/product_for_x/pallas_call | solution.py:115
  25.8 6.5 %product_for_y.1 = (bf16[32,48,256]{2,1,0:T(8,128)(2,1)S(1)}, bf16[32,48,256]{2,1,0:T(8,128)(2,1)S(1)}, bf16[32,48,256]{2,1,0:T(8,128)(2,1)S(1)}, bf16[16,48,256...) custom-call(s32[3]{0:T(128)S(1)} %pad_add_fusion.idx_ref, bf16[1024,1536]{1,0:T(8,128)(2,1)S(1)} %copy-done, ...), custom_call_target="tpu_custom_call" | custom-call | flops 3221225472 | bytes 11534336 | tf_op jit(solution)/shard_map/product_for_y/pallas_call | solution.py:83
  33.0 2.1 %collective-permute-start.2 = (bf16[32,48,256]{2,1,0:T(8,128)(2,1)S(1)}, bf16[32,48,256]{2,1,0:T(8,128)(2,1)S(1)}, u32[]{:S(2)}, u32[]{:S(2)}) collective-permute-start(bf16[32,48,256]{2,1,0:T(8,128)(2,1)S(1)} %get-tuple-element.28), channel_id=1, source_target_pairs={{0,3},{1,0},{2,1},{3,2},{4,7},{5,4},{6,5},{7,6},{8,11},{9,8},{10,9... | collective-permute-start | bytes 2359304 | tf_op jit(solution)/shard_map/ppermute | solution.py:32
  35.1 7.9 %collective-permute-done.10.fu.from_up = bf16[8,48,1024]{2,1,0:T(8,128)(2,1)S(1)} collective-permute-done((bf16[8,48,1024]{2,1,0:T(8,128)(2,1)S(1)}, bf16[8,48,1024]{2,1,0:T(8,128)(2,1)S(1)}, u32[]{:S(2)}, u32[]{:S(2)}) %collective-permute-start.10) | collective-permute-done | bytes 786464 | tf_op jit(solution)/shard_map/ppermute | solution.py:32
  43.0 1.6 %collective-permute-done.9.fd.from_down = bf16[8,48,1024]{2,1,0:T(8,128)(2,1)S(1)} collective-permute-done((bf16[8,48,1024]{2,1,0:T(8,128)(2,1)S(1)}, bf16[8,48,1024]{2,1,0:T(8,128)(2,1)S(1)}, u32[]{:S(2)}, u32[]{:S(2)}) %collective-permute-start.9) | collective-permute-done | bytes 786464 | tf_op jit(solution)/shard_map/ppermute | solution.py:32
  44.9 2.7 %collective-permute-start.12 = (bf16[4,48,1024]{2,1,0:T(8,128)(2,1)S(1)}, bf16[4,48,1024]{2,1,0:T(8,128)(2,1)S(1)}, u32[]{:S(2)}, u32[]{:S(2)}) collective-permute-start(bf16[4,48,1024]{2,1,0:T(8,128)(2,1)S(1)} %get-tuple-element.43), channel_id=1, source_target_pairs={{0,24},{8,0},{16,8},{24,16},{1,25},{9,1},{17,9},{25,17},{2,26},{10... | collective-permute-start | bytes 1179656 | tf_op jit(solution)/shard_map/ppermute | solution.py:32
  47.5 4.1 %collective-permute-done.1.fd.from_down = bf16[32,48,256]{2,1,0:T(8,128)(2,1)S(1)} collective-permute-done((bf16[32,48,256]{2,1,0:T(8,128)(2,1)S(1)}, bf16[32,48,256]{2,1,0:T(8,128)(2,1)S(1)}, u32[]{:S(2)}, u32[]{:S(2)}) %collective-permute-start.1) | collective-permute-done | bytes 786464 | tf_op jit(solution)/shard_map/ppermute | solution.py:32
  52.5 2.0 %collective-permute-start.4 = (bf16[16,48,256]{2,1,0:T(8,128)(2,1)S(1)}, bf16[16,48,256]{2,1,0:T(8,128)(2,1)S(1)}, u32[]{:S(2)}, u32[]{:S(2)}) collective-permute-start(bf16[16,48,256]{2,1,0:T(8,128)(2,1)S(1)} %get-tuple-element.32), channel_id=1, source_target_pairs={{0,3},{1,0},{2,1},{3,2},{4,7},{5,4},{6,5},{7,6},{8,11},{9,8},{10,9... | collective-permute-start | bytes 1179656 | tf_op jit(solution)/shard_map/ppermute | solution.py:32
  55.9 1.4 %collective-permute-start.13 = (bf16[8,48,256]{2,1,0:T(8,128)(2,1)S(1)}, bf16[8,48,256]{2,1,0:T(8,128)(2,1)S(1)}, u32[]{:S(2)}, u32[]{:S(2)}) collective-permute-start(bf16[8,48,256]{2,1,0:T(8,128)(2,1)S(1)} %get-tuple-element.45), channel_id=1, source_target_pairs={{0,1},{1,2},{2,3},{3,0},{4,5},{5,6},{6,7},{7,4},{8,9},{9,10},{10,1... | collective-permute-start | bytes 589832 | tf_op jit(solution)/shard_map/ppermute | solution.py:32
  57.3 1.5 %collective-permute-start.14 = (bf16[8,48,256]{2,1,0:T(8,128)(2,1)S(1)}, bf16[8,48,256]{2,1,0:T(8,128)(2,1)S(1)}, u32[]{:S(2)}, u32[]{:S(2)}) collective-permute-start(bf16[8,48,256]{2,1,0:T(8,128)(2,1)S(1)} %get-tuple-element.46), channel_id=1, source_target_pairs={{0,3},{1,0},{2,1},{3,2},{4,7},{5,4},{6,5},{7,6},{8,11},{9,8},{10,9... | collective-permute-start | bytes 589832 | tf_op jit(solution)/shard_map/ppermute | solution.py:32
  58.8 1.6 %collective-permute-start.15 = (bf16[8,48,256]{2,1,0:T(8,128)(2,1)S(1)}, bf16[8,48,256]{2,1,0:T(8,128)(2,1)S(1)}, u32[]{:S(2)}, u32[]{:S(2)}) collective-permute-start(bf16[8,48,256]{2,1,0:T(8,128)(2,1)S(1)} %get-tuple-element.47), channel_id=1, source_target_pairs={{0,2},{1,3},{2,0},{3,1},{4,6},{5,7},{6,4},{7,5},{8,10},{9,11},{10,... | collective-permute-start | bytes 589832 | tf_op jit(solution)/shard_map/ppermute | solution.py:32
  60.4 1.4 %collective-permute-done.3.up = bf16[16,48,256]{2,1,0:T(8,128)(2,1)S(1)} collective-permute-done((bf16[16,48,256]{2,1,0:T(8,128)(2,1)S(1)}, bf16[16,48,256]{2,1,0:T(8,128)(2,1)S(1)}, u32[]{:S(2)}, u32[]{:S(2)}) %collective-permute-start.3) | collective-permute-done | bytes 393248 | tf_op jit(solution)/shard_map/ppermute | solution.py:32
  63.3 2.0 %collective-permute-start.6 = (bf16[8,48,256]{2,1,0:T(8,128)(2,1)S(1)}, bf16[8,48,256]{2,1,0:T(8,128)(2,1)S(1)}, u32[]{:S(2)}, u32[]{:S(2)}) collective-permute-start(bf16[8,48,256]{2,1,0:T(8,128)(2,1)S(1)} %get-tuple-element.35), channel_id=1, source_target_pairs={{0,24},{8,0},{16,8},{24,16},{1,25},{9,1},{17,9},{25,17},{2,26},{10... | collective-permute-start | bytes 589832 | tf_op jit(solution)/shard_map/ppermute | solution.py:32
  67.1 3.4 %collective-permute-done.15.refs_7_ = bf16[8,48,256]{2,1,0:T(8,128)(2,1)S(1)} collective-permute-done((bf16[8,48,256]{2,1,0:T(8,128)(2,1)S(1)}, bf16[8,48,256]{2,1,0:T(8,128)(2,1)S(1)}, u32[]{:S(2)}, u32[]{:S(2)}) %collective-permute-start.15) | collective-permute-done | bytes 196640 | tf_op jit(solution)/shard_map/ppermute | solution.py:32
  70.5 1.8 %collective-permute-done.7.refs_3_ = bf16[8,48,256]{2,1,0:T(8,128)(2,1)S(1)} collective-permute-done((bf16[8,48,256]{2,1,0:T(8,128)(2,1)S(1)}, bf16[8,48,256]{2,1,0:T(8,128)(2,1)S(1)}, u32[]{:S(2)}, u32[]{:S(2)}) %collective-permute-start.7) | collective-permute-done | bytes 196640 | tf_op jit(solution)/shard_map/ppermute | solution.py:32
  73.3 10.1 %all-to-all-start = ((bf16[32,24,256]{2,1,0:T(8,128)(2,1)}), bf16[32,24,256]{2,1,0:T(8,128)(2,1)S(1)}, u32[]{:S(2)}, u32[]{:S(2)}) async-start(bf16[32,24,256]{2,1,0:T(8,128)(2,1)} %sum_for_z.1), calls=%async_computation | async-start | bytes 786432 | tf_op jit(solution)/shard_map/all_to_all | solution.py:40
  83.4 11.5 %all-to-all-done = bf16[32,24,256]{2,1,0:T(8,128)(2,1)S(1)} async-done(((bf16[32,24,256]{2,1,0:T(8,128)(2,1)}), bf16[32,24,256]{2,1,0:T(8,128)(2,1)S(1)}, u32[]{:S(2)}, u32[]{:S(2)}) %all-to-all-start) | async-done | bytes 393248 | tf_op jit(solution)/shard_map/all_to_all | solution.py:40
  95.0 9.1 %collective-permute-start.16 = (bf16[4,2,6,256]{3,0,2,1:T(4,128)(2,1)S(1)}, bf16[4,2,6,256]{3,0,2,1:T(4,128)(2,1)S(1)}, u32[]{:S(2)}, u32[]{:S(2)}) collective-permute-start(bf16[4,2,6,256]{3,0,2,1:T(4,128)(2,1)S(1)} %fusion.3), channel_id=1, source_target_pairs={{0,4},{4,0},{1,5},{5,1},{2,6},{6,2},{3,7},{7,3},{8,12},{12,8},{9,1... | collective-permute-start | bytes 73736 | tf_op jit(solution)/shard_map/ppermute | solution.py:32
  106.2 2.4 %collective-permute-start.18 = (bf16[6,4096]{1,0:T(8,128)(2,1)S(1)}, bf16[6,4096]{1,0:T(8,128)(2,1)S(1)}, u32[]{:S(2)}, u32[]{:S(2)}) collective-permute-start(bf16[6,4096]{1,0:T(8,128)(2,1)S(1)} %get-tuple-element.48), channel_id=1, source_target_pairs={{0,2},{1,3},{2,0},{3,1},{4,6},{5,7},{6,4},{7,5},{8,10},{9,11},{10,... | collective-permute-start | bytes 147464 | tf_op jit(solution)/shard_map/ppermute | solution.py:32
  109.8 1.3 %collective-permute-done.17 = bf16[6,4096]{1,0:T(8,128)(2,1)S(1)} collective-permute-done((bf16[6,4096]{1,0:T(8,128)(2,1)S(1)}, bf16[6,4096]{1,0:T(8,128)(2,1)S(1)}, u32[]{:S(2)}, u32[]{:S(2)}) %collective-permute-start.17) | collective-permute-done | bytes 49184 | tf_op jit(solution)/shard_map/ppermute | solution.py:32
  (62 shorter events, 14.7 us)
Async XLA Ops:
  8.4 9.2 %collective-permute-start.8 = (bf16[1536,1024]{1,0:T(8,128)(2,1)S(1)}, bf16[1536,1024]{1,0:T(8,128)(2,1)S(1)}, u32[]{:S(2)}, u32[]{:S(2)}) collective-permute-start(bf16[1536,1024]{1,0:T(8,128)(2,1)S(1)} %product_theirs.3), channel_id=1, source_target_pairs={{0,4},{4,0},{1,5},{5,1},{2,6},{6,2},{3,7},{7,3},{8,12},{12,8},{9,1... | collective-permute-start | bytes 9437192 | tf_op jit(solution)/shard_map/ppermute | solution.py:32
  17.5 8.3 %collective-permute-start = (bf16[1536,1024]{1,0:T(8,128)(2,1)S(1)}, bf16[1536,1024]{1,0:T(8,128)(2,1)S(1)}, u32[]{:S(2)}, u32[]{:S(2)}) collective-permute-start(bf16[1536,1024]{1,0:T(8,128)(2,1)S(1)} %product_theirs.2), channel_id=1, source_target_pairs={{0,4},{4,0},{1,5},{5,1},{2,6},{6,2},{3,7},{7,3},{8,12},{12,8},{9,1... | collective-permute-start | bytes 9437192 | tf_op jit(solution)/shard_map/ppermute | solution.py:32
  24.3 18.7 %collective-permute-start.10 = (bf16[8,48,1024]{2,1,0:T(8,128)(2,1)S(1)}, bf16[8,48,1024]{2,1,0:T(8,128)(2,1)S(1)}, u32[]{:S(2)}, u32[]{:S(2)}) collective-permute-start(bf16[8,48,1024]{2,1,0:T(8,128)(2,1)S(1)} %get-tuple-element.39), channel_id=1, source_target_pairs={{0,24},{8,0},{16,8},{24,16},{1,25},{9,1},{17,9},{25,17},{2,26},{10... | collective-permute-start | bytes 2359304 | tf_op jit(solution)/shard_map/ppermute | solution.py:32
  25.1 19.5 %collective-permute-start.9 = (bf16[8,48,1024]{2,1,0:T(8,128)(2,1)S(1)}, bf16[8,48,1024]{2,1,0:T(8,128)(2,1)S(1)}, u32[]{:S(2)}, u32[]{:S(2)}) collective-permute-start(bf16[8,48,1024]{2,1,0:T(8,128)(2,1)S(1)} %get-tuple-element.38), channel_id=1, source_target_pairs={{0,8},{8,16},{16,24},{24,0},{1,9},{9,17},{17,25},{25,1},{2,10},{10... | collective-permute-start | bytes 2359304 | tf_op jit(solution)/shard_map/ppermute | solution.py:32
  32.3 19.3 %collective-permute-start.1 = (bf16[32,48,256]{2,1,0:T(8,128)(2,1)S(1)}, bf16[32,48,256]{2,1,0:T(8,128)(2,1)S(1)}, u32[]{:S(2)}, u32[]{:S(2)}) collective-permute-start(bf16[32,48,256]{2,1,0:T(8,128)(2,1)S(1)} %get-tuple-element.27), channel_id=1, source_target_pairs={{0,1},{1,2},{2,3},{3,0},{4,5},{5,6},{6,7},{7,4},{8,9},{9,10},{10,1... | collective-permute-start | bytes 2359304 | tf_op jit(solution)/shard_map/ppermute | solution.py:32
  33.0 18.6 %collective-permute-start.2 = (bf16[32,48,256]{2,1,0:T(8,128)(2,1)S(1)}, bf16[32,48,256]{2,1,0:T(8,128)(2,1)S(1)}, u32[]{:S(2)}, u32[]{:S(2)}) collective-permute-start(bf16[32,48,256]{2,1,0:T(8,128)(2,1)S(1)} %get-tuple-element.28), channel_id=1, source_target_pairs={{0,3},{1,0},{2,1},{3,2},{4,7},{5,4},{6,5},{7,6},{8,11},{9,8},{10,9... | collective-permute-start | bytes 2359304 | tf_op jit(solution)/shard_map/ppermute | solution.py:32
  44.8 10.2 %collective-permute-start.11 = (bf16[4,48,1024]{2,1,0:T(8,128)(2,1)S(1)}, bf16[4,48,1024]{2,1,0:T(8,128)(2,1)S(1)}, u32[]{:S(2)}, u32[]{:S(2)}) collective-permute-start(bf16[4,48,1024]{2,1,0:T(8,128)(2,1)S(1)} %get-tuple-element.42), channel_id=1, source_target_pairs={{0,8},{8,16},{16,24},{24,0},{1,9},{9,17},{17,25},{25,1},{2,10},{10... | collective-permute-start | bytes 1179656 | tf_op jit(solution)/shard_map/ppermute | solution.py:32
  44.9 10.2 %collective-permute-start.12 = (bf16[4,48,1024]{2,1,0:T(8,128)(2,1)S(1)}, bf16[4,48,1024]{2,1,0:T(8,128)(2,1)S(1)}, u32[]{:S(2)}, u32[]{:S(2)}) collective-permute-start(bf16[4,48,1024]{2,1,0:T(8,128)(2,1)S(1)} %get-tuple-element.43), channel_id=1, source_target_pairs={{0,24},{8,0},{16,8},{24,16},{1,25},{9,1},{17,9},{25,17},{2,26},{10... | collective-permute-start | bytes 1179656 | tf_op jit(solution)/shard_map/ppermute | solution.py:32
  51.8 9.9 %collective-permute-start.3 = (bf16[16,48,256]{2,1,0:T(8,128)(2,1)S(1)}, bf16[16,48,256]{2,1,0:T(8,128)(2,1)S(1)}, u32[]{:S(2)}, u32[]{:S(2)}) collective-permute-start(bf16[16,48,256]{2,1,0:T(8,128)(2,1)S(1)} %get-tuple-element.31), channel_id=1, source_target_pairs={{0,1},{1,2},{2,3},{3,0},{4,5},{5,6},{6,7},{7,4},{8,9},{9,10},{10,1... | collective-permute-start | bytes 1179656 | tf_op jit(solution)/shard_map/ppermute | solution.py:32
  52.5 9.2 %collective-permute-start.4 = (bf16[16,48,256]{2,1,0:T(8,128)(2,1)S(1)}, bf16[16,48,256]{2,1,0:T(8,128)(2,1)S(1)}, u32[]{:S(2)}, u32[]{:S(2)}) collective-permute-start(bf16[16,48,256]{2,1,0:T(8,128)(2,1)S(1)} %get-tuple-element.32), channel_id=1, source_target_pairs={{0,3},{1,0},{2,1},{3,2},{4,7},{5,4},{6,5},{7,6},{8,11},{9,8},{10,9... | collective-permute-start | bytes 1179656 | tf_op jit(solution)/shard_map/ppermute | solution.py:32
  55.9 10.0 %collective-permute-start.13 = (bf16[8,48,256]{2,1,0:T(8,128)(2,1)S(1)}, bf16[8,48,256]{2,1,0:T(8,128)(2,1)S(1)}, u32[]{:S(2)}, u32[]{:S(2)}) collective-permute-start(bf16[8,48,256]{2,1,0:T(8,128)(2,1)S(1)} %get-tuple-element.45), channel_id=1, source_target_pairs={{0,1},{1,2},{2,3},{3,0},{4,5},{5,6},{6,7},{7,4},{8,9},{9,10},{10,1... | collective-permute-start | bytes 589832 | tf_op jit(solution)/shard_map/ppermute | solution.py:32
  57.3 9.8 %collective-permute-start.14 = (bf16[8,48,256]{2,1,0:T(8,128)(2,1)S(1)}, bf16[8,48,256]{2,1,0:T(8,128)(2,1)S(1)}, u32[]{:S(2)}, u32[]{:S(2)}) collective-permute-start(bf16[8,48,256]{2,1,0:T(8,128)(2,1)S(1)} %get-tuple-element.46), channel_id=1, source_target_pairs={{0,3},{1,0},{2,1},{3,2},{4,7},{5,4},{6,5},{7,6},{8,11},{9,8},{10,9... | collective-permute-start | bytes 589832 | tf_op jit(solution)/shard_map/ppermute | solution.py:32
  58.8 11.7 %collective-permute-start.15 = (bf16[8,48,256]{2,1,0:T(8,128)(2,1)S(1)}, bf16[8,48,256]{2,1,0:T(8,128)(2,1)S(1)}, u32[]{:S(2)}, u32[]{:S(2)}) collective-permute-start(bf16[8,48,256]{2,1,0:T(8,128)(2,1)S(1)} %get-tuple-element.47), channel_id=1, source_target_pairs={{0,2},{1,3},{2,0},{3,1},{4,6},{5,7},{6,4},{7,5},{8,10},{9,11},{10,... | collective-permute-start | bytes 589832 | tf_op jit(solution)/shard_map/ppermute | solution.py:32
  61.7 43.5 %copy-start.1 = (f32[6,4096]{1,0:T(8,128)S(1)}, f32[6,4096]{1,0:T(8,128)}, u32[]{:S(2)}) copy-start(f32[6,4096]{1,0:T(8,128)} %param.7) | copy-start | bytes 294916
  61.7 43.5 %copy-start.2 = (f32[6,4096]{1,0:T(8,128)S(1)}, f32[6,4096]{1,0:T(8,128)}, u32[]{:S(2)}) copy-start(f32[6,4096]{1,0:T(8,128)} %param.8) | copy-start | bytes 294916
  61.7 43.5 %copy-start.3 = (f32[6,4096]{1,0:T(8,128)S(1)}, f32[6,4096]{1,0:T(8,128)}, u32[]{:S(2)}) copy-start(f32[6,4096]{1,0:T(8,128)} %param.9) | copy-start | bytes 294916
  62.6 7.9 %collective-permute-start.5 = (bf16[8,48,256]{2,1,0:T(8,128)(2,1)S(1)}, bf16[8,48,256]{2,1,0:T(8,128)(2,1)S(1)}, u32[]{:S(2)}, u32[]{:S(2)}) collective-permute-start(bf16[8,48,256]{2,1,0:T(8,128)(2,1)S(1)} %get-tuple-element.34), channel_id=1, source_target_pairs={{0,8},{8,16},{16,24},{24,0},{1,9},{9,17},{17,25},{25,1},{2,10},{10... | collective-permute-start | bytes 589832 | tf_op jit(solution)/shard_map/ppermute | solution.py:32
  63.3 7.2 %collective-permute-start.6 = (bf16[8,48,256]{2,1,0:T(8,128)(2,1)S(1)}, bf16[8,48,256]{2,1,0:T(8,128)(2,1)S(1)}, u32[]{:S(2)}, u32[]{:S(2)}) collective-permute-start(bf16[8,48,256]{2,1,0:T(8,128)(2,1)S(1)} %get-tuple-element.35), channel_id=1, source_target_pairs={{0,24},{8,0},{16,8},{24,16},{1,25},{9,1},{17,9},{25,17},{2,26},{10... | collective-permute-start | bytes 589832 | tf_op jit(solution)/shard_map/ppermute | solution.py:32
  65.9 6.3 %collective-permute-start.7 = (bf16[8,48,256]{2,1,0:T(8,128)(2,1)S(1)}, bf16[8,48,256]{2,1,0:T(8,128)(2,1)S(1)}, u32[]{:S(2)}, u32[]{:S(2)}) collective-permute-start(bf16[8,48,256]{2,1,0:T(8,128)(2,1)S(1)} %get-tuple-element.36), channel_id=1, source_target_pairs={{0,16},{8,24},{16,0},{24,8},{1,17},{9,25},{17,1},{25,9},{2,18},{10... | collective-permute-start | bytes 589832 | tf_op jit(solution)/shard_map/ppermute | solution.py:32
  73.3 21.6 %all-to-all-start = ((bf16[32,24,256]{2,1,0:T(8,128)(2,1)}), bf16[32,24,256]{2,1,0:T(8,128)(2,1)S(1)}, u32[]{:S(2)}, u32[]{:S(2)}) async-start(bf16[32,24,256]{2,1,0:T(8,128)(2,1)} %sum_for_z.1), calls=%async_computation | async-start | bytes 786432 | tf_op jit(solution)/shard_map/all_to_all | solution.py:40
  95.0 9.9 %collective-permute-start.16 = (bf16[4,2,6,256]{3,0,2,1:T(4,128)(2,1)S(1)}, bf16[4,2,6,256]{3,0,2,1:T(4,128)(2,1)S(1)}, u32[]{:S(2)}, u32[]{:S(2)}) collective-permute-start(bf16[4,2,6,256]{3,0,2,1:T(4,128)(2,1)S(1)} %fusion.3), channel_id=1, source_target_pairs={{0,4},{4,0},{1,5},{5,1},{2,6},{6,2},{3,7},{7,3},{8,12},{12,8},{9,1... | collective-permute-start | bytes 73736 | tf_op jit(solution)/shard_map/ppermute | solution.py:32
  106.1 5.0 %collective-permute-start.17 = (bf16[6,4096]{1,0:T(8,128)(2,1)S(1)}, bf16[6,4096]{1,0:T(8,128)(2,1)S(1)}, u32[]{:S(2)}, u32[]{:S(2)}) collective-permute-start(bf16[6,4096]{1,0:T(8,128)(2,1)S(1)} %get-tuple-element.48), channel_id=1, source_target_pairs={{0,1},{1,2},{2,3},{3,0},{4,5},{5,6},{6,7},{7,4},{8,9},{9,10},{10,1... | collective-permute-start | bytes 147464 | tf_op jit(solution)/shard_map/ppermute | solution.py:32
  106.2 5.4 %collective-permute-start.18 = (bf16[6,4096]{1,0:T(8,128)(2,1)S(1)}, bf16[6,4096]{1,0:T(8,128)(2,1)S(1)}, u32[]{:S(2)}, u32[]{:S(2)}) collective-permute-start(bf16[6,4096]{1,0:T(8,128)(2,1)S(1)} %get-tuple-element.48), channel_id=1, source_target_pairs={{0,2},{1,3},{2,0},{3,1},{4,6},{5,7},{6,4},{7,5},{8,10},{9,11},{10,... | collective-permute-start | bytes 147464 | tf_op jit(solution)/shard_map/ppermute | solution.py:32
  108.6 3.9 %collective-permute-start.19 = (bf16[6,4096]{1,0:T(8,128)(2,1)S(1)}, bf16[6,4096]{1,0:T(8,128)(2,1)S(1)}, u32[]{:S(2)}, u32[]{:S(2)}) collective-permute-start(bf16[6,4096]{1,0:T(8,128)(2,1)S(1)} %get-tuple-element.48), channel_id=1, source_target_pairs={{0,3},{1,0},{2,1},{3,2},{4,7},{5,4},{6,5},{7,6},{8,11},{9,8},{10,9... | collective-permute-start | bytes 147464 | tf_op jit(solution)/shard_map/ppermute | solution.py:32
  (1 other events, 1.9 us)

commit v7 on v6

--- a/solution.py
+++ b/solution.py
@@ -40,11 +40,11 @@
     return lax.all_to_all(v, axes, 0, 0, tiled=True)
 
 
-def product(acts, cot, idx, base, ncols):
+def product(acts, cot, idx, base, ncols, after=()):
     tn = 2 * TN
 
-    def kernel(idx_ref, a, c, o):
-        o[...] = lax.dot_general(a[...], c[...], DN, preferred_element_type=F32).astype(BF16)
+    def kernel(idx_ref, a, c, *rest):
+        rest[-1][...] = lax.dot_general(a[...], c[...], DN, preferred_element_type=F32).astype(BF16)
 
     return pl.pallas_call(
         kernel,
@@ -54,64 +54,77 @@
             in_specs=[
                 WHOLE,
                 pl.BlockSpec((T, tn), lambda j, s: (0, (1 - s[0]) * (HALF // tn) + base // tn + j)),
-            ],
+            ]
+            + [pl.BlockSpec(memory_space=pl.ANY)] * len(after),
             out_specs=pl.BlockSpec((D, tn), lambda j, s: (0, j)),
         ),
         out_shape=jax.ShapeDtypeStruct((D, ncols), BF16),
         name="product_theirs",
         **params_of(2 * T * D * ncols, 2 * (T * D + T * ncols + D * ncols)),
-    )(idx, acts, cot)
+    )(idx, acts, cot, *after)
 
 
 def ahead(idx_ref, axis, o):
     return lax.rem(idx_ref["cxy".index(axis)] + o, 4)
 
 
-def product_for_y(acts, cot, got, idx, base):
-    def kernel(idx_ref, a, c, r, *outs):
-        acc = lax.dot_general(a[...], c[...], DN, preferred_element_type=F32) + r[...].astype(F32)
-        acc = acc.astype(BF16).reshape(NZ * NX, BLK, TN)
-        for o in range(NY):
-
-            @pl.when(pl.program_id(0) == o)
-            def _():
-                for out, here, there in parts_of(o, NZ * NX // 2):
-                    outs[out][there] = acc[here]
-
-    place = lambda j, s: lax.rem(s[2] + j, NY)
-    shapes = ring_shapes(NZ * NX, TN)
+def product_for_y(acts, cot, got, idx, base, part, after=()):
+    half = D // 2
+    upper, lower = slice(0, half), slice(half, D)
+    full, one_upper, one_lower = (2, 3, 1) if part == 0 else (0, 1, 3)
+    full_lower = 1 if part == 0 else 0
+    one_lower_out = 0 if part == 0 else 1
+
+    def kernel(idx_ref, a, c_full, c_upper, c_lower, r, *rest):
+        outs = rest[-2:]
+
+        def add(product, rows, o):
+            columns = pl.ds(pl.multiple_of(lax.rem(idx_ref[2] + o, NY) * TN, TN), TN)
+            return (product + r[rows, columns].astype(F32)).astype(BF16)
+
+        product = lax.dot_general(a[...], c_full[...], DN, preferred_element_type=F32)
+        outs[0][upper, :] = add(product[upper], upper, full)
+        outs[full_lower][lower, :] = add(product[lower], lower, full)
+        product = lax.dot_general(a[:, upper], c_upper[...], DN, preferred_element_type=F32)
+        outs[1][upper, :] = add(product, upper, one_upper)
+        product = lax.dot_general(a[:, lower], c_lower[...], DN, preferred_element_type=F32)
+        outs[one_lower_out][lower, :] = add(product, lower, one_lower)
+
+    def columns(o):
+        place = lambda j, s: (0, s[0] * (HALF // TN) + base // TN + lax.rem(s[2] + o, NY))
+        return pl.BlockSpec((T, TN), place)
+
     return pl.pallas_call(
         kernel,
         grid_spec=pltpu.PrefetchScalarGridSpec(
             num_scalar_prefetch=1,
-            grid=(NY,),
-            in_specs=[
-                WHOLE,
-                pl.BlockSpec((T, TN), lambda j, s: (0, s[0] * (HALF // TN) + base // TN + place(j, s))),
-                pl.BlockSpec((D, TN), lambda j, s: (0, place(j, s))),
-            ],
-            out_specs=[pl.BlockSpec(o.shape, lambda j, s: (0, 0, 0)) for o in shapes],
-        ),
-        out_shape=shapes,
+            grid=(1,),
+            in_specs=[WHOLE]
+            + [columns(o) for o in (full, one_upper, one_lower)]
+            + [WHOLE]
+            + [pl.BlockSpec(memory_space=pl.ANY)] * len(after),
+            out_specs=[WHOLE] * 2,
+        ),
+        out_shape=[jax.ShapeDtypeStruct((D, TN), BF16)] * 2,
         name="product_for_y",
-        **params_of(2 * T * D * TN * NY, 2 * (T * D + T * TN * NY + 2 * D * TN * NY)),
-    )(idx, acts, cot, got)
-
-
-def product_for_x(acts, cot, got, idx, base, ncols):
+        **params_of(4 * T * D * TN, 2 * (T * D + 4 * T * TN + 4 * D * TN)),
+    )(idx, acts, cot, cot, cot, got, *after)
+
+
+def product_for_x(acts, cot, got, idx, base, ncols, after):
     tn = 2 * TN
 
-    def kernel(idx_ref, a, c, r, *rest):
+    def kernel(idx_ref, a, c, r, _, *rest):
         outs, acc = rest[:-1], rest[-1]
         acc[...] = lax.dot_general(a[...], c[...], DN, preferred_element_type=F32) + r[...].astype(F32)
         for o in range(NX):
             x = ahead(idx_ref, "x", o)
-            for out, here, there in parts_of(o, NZ // 2):
-                for z in range(here.start, here.stop):
+            for out, half in parts_of(o, NZ // 2):
+                for z in range(half.start, half.stop):
                     rows = pl.ds(pl.multiple_of((z * NX + x) * BLK, BLK), BLK)
-                    outs[out][z - here.start + there.start] = acc[rows, :].astype(BF16)
-
-    shapes = ring_shapes(NZ, ncols)
+                    outs[out][z] = acc[rows, :].astype(BF16)
+
+    shapes = [jax.ShapeDtypeStruct((NZ, BLK, ncols), BF16)] * 4
     return pl.pallas_call(
         kernel,
         grid_spec=pltpu.PrefetchScalarGridSpec(
@@ -121,6 +134,7 @@
                 WHOLE,
                 pl.BlockSpec((T, tn), lambda j, s: (0, s[0] * (HALF // tn) + base // tn + j)),
                 pl.BlockSpec((D, tn), lambda j, s: (0, j)),
+                pl.BlockSpec(memory_space=pl.ANY),
             ],
             out_specs=[pl.BlockSpec(o.shape[:2] + (tn,), lambda j, s: (0, 0, j)) for o in shapes],
             scratch_shapes=[pltpu.VMEM((D, tn), F32)],
@@ -128,45 +142,39 @@
         out_shape=shapes,
         name="product_for_x",
         **params_of(2 * T * D * ncols, 2 * (T * D + T * ncols + 2 * D * ncols)),
-    )(idx, acts, cot, got)
-
-
-def ring_shapes(n, width):
-    return [jax.ShapeDtypeStruct((k, BLK, width), BF16) for k in (n, n, n, n // 2, n // 2)]
+    )(idx, acts, cot, got, after)
 
 
 def parts_of(o, half):
     upper, lower = slice(0, half), slice(half, 2 * half)
-    return {
-        0: ((0, upper, upper), (0, lower, lower)),
-        1: ((3, upper, upper), (1, lower, lower)),
-        2: ((1, upper, upper), (2, lower, lower)),
-        3: ((2, upper, upper), (4, lower, upper)),
-    }[o]
-
-
-def pass_on(keep_up, keep_down, from_down, from_up):
-    half = keep_up.shape[0]
-
-    def kernel(ku, kd, fd, fu, up, down):
-        for k in range(half):
-            up[k] = (ku[k].astype(F32) + fd[k].astype(F32)).astype(BF16)
-            down[k] = (kd[k].astype(F32) + fu[half + k].astype(F32)).astype(BF16)
-
-    return pl.pallas_call(
-        kernel,
-        in_specs=[WHOLE] * 4,
+    arrays = ((0, 0), (3, 1), (1, 2), (2, 3))[o]
+    return ((arrays[0], upper), (arrays[1], lower))
+
+
+def pass_on(keep, from_down, from_up):
+    half = keep.shape[0] // 2
+
+    def kernel(k, fd, fu, up, down):
+        for n in range(half):
+            up[n] = (k[n].astype(F32) + fd[n].astype(F32)).astype(BF16)
+            down[n] = (k[half + n].astype(F32) + fu[half + n].astype(F32)).astype(BF16)
+
+    return pl.pallas_call(
+        kernel,
+        in_specs=[WHOLE] * 3,
         out_specs=[WHOLE] * 2,
-        out_shape=[jax.ShapeDtypeStruct(keep_up.shape, BF16)] * 2,
+        out_shape=[jax.ShapeDtypeStruct((half,) + keep.shape[1:], BF16)] * 2,
         name="pass_on",
-        **params_of(2 * keep_up.size, 12 * keep_up.size),
-    )(keep_up, keep_down, from_down, from_up)
-
-
-def ring(pieces, axis):
-    own, up, down, keep_up, keep_down = pieces
-    from_down, from_up = shift(up, axis, 4, 1), shift(down, axis, 4, 3)
-    up, down = pass_on(keep_up, keep_down, from_down, from_up)
+        **params_of(keep.size, 6 * keep.size),
+    )(keep, from_down, from_up)
+
+
+def ring(up, down, axis):
+    return shift(up, axis, 4, 1), shift(down, axis, 4, 3)
+
+
+def ring_end(own, keep, from_down, from_up, axis):
+    up, down = pass_on(keep, from_down, from_up)
     return own, from_down, from_up, shift(up, axis, 4, 1), shift(down, axis, 4, 3)
 
 
@@ -241,12 +249,18 @@
 def body(acts, cotangent, master, moment, second):
     x, c, y = (lax.axis_index(a) for a in ("x", "c", "y"))
     idx = jnp.stack([c, x, y]).astype(jnp.int32)
+    blocks = lambda p: p.reshape(NZ * NX, BLK, TN)
     theirs_c = product(acts, cotangent, idx, 0, FLOW_C)
     got_c = shift(theirs_c, "c", NC, 1)
-    theirs_b = product(acts, cotangent, idx, FLOW_C, FLOW_B)
+    theirs_b = product(acts, cotangent, idx, FLOW_C, FLOW_B, (theirs_c,))
     got_b = shift(theirs_b, "c", NC, 1)
-    over_x = ring(product_for_x(acts, cotangent, got_b, idx, FLOW_C, FLOW_B), "x")
-    over_y = ring(product_for_y(acts, cotangent, got_c, idx, 0), "y")
+    up, down = product_for_y(acts, cotangent, got_c, idx, 0, 0)
+    first_y = ring(blocks(up), blocks(down), "y")
+    own_b, up_b, down_b, keep_b = product_for_x(acts, cotangent, got_b, idx, FLOW_C, FLOW_B, up)
+    first_x = ring(up_b, down_b, "x")
+    own, keep = product_for_y(acts, cotangent, got_c, idx, 0, 1, (own_b,))
+    over_y = ring_end(blocks(own), blocks(keep), *first_y, "y")
+    over_x = ring_end(own_b, keep_b, *first_x, "x")
     over_xy = exchange(sum_and_cut(over_x, idx, "y"), "y", 4, ORDER)
     over_yx = exchange(sum_and_cut(over_y, idx, "x"), "x", 4, ORDER)
     grad = settle((over_yx, over_xy), c)

time: 114 us -> 111 us (0.974)
  starting transfers between devices: 44.5 us -> 39.1 us
    ppermute x20, starting transfers between devices: 34.4 us -> 29.5 us  [shift(): return lax.ppermute(v, axis, [(i, (i + s) % n) for i in range(n)])]
    pallas_call x1 -> x2, Pallas kernels: 6.48 us -> 7.58 us  [product_for_y(): pl.pallas_call(kernel, grid_spec=pltpu.PrefetchScalarGridSpec(num_scalar_...]
  transfers between devices with their start and end apart: 21 -> 21, of which waited for: 13 -> 11; matrix products, arithmetic and copies ran while one was open for 0% -> 0% of each run, Pallas kernels for 19% -> 20%
where the time goes in v7:
time: 111 us; the launch traced here: 109 us
  starting transfers between devices  39.1 us (35%)
  waiting for transfers between devices  36.6 us (33%)
  Pallas kernels  28.8 us (26%)
  local copies, waits for them, and re-layouts  2.09 us (2%)
  other arithmetic  1.81 us (2%)
    ppermute x20, starting transfers between devices, shift(): return lax.ppermute(v, axis, [(i, (i + s) % n) for i in range(n)])  29.5 us
    ppermute x20, waiting for transfers between devices, shift(): return lax.ppermute(v, axis, [(i, (i + s) % n) for i in range(n)])  25 us
    all_to_all x1, waiting for transfers between devices, swap(): return lax.all_to_all(v, axes, 0, 0, tiled=True)  11.6 us
    pallas_call x2, Pallas kernels, product(): pl.pallas_call(kernel, grid_spec=pltpu.PrefetchScalarGridSpec(num_scalar_...  11.5 us
    all_to_all x1, starting transfers between devices, swap(): return lax.all_to_all(v, axes, 0, 0, tiled=True)  9.6 us
    pallas_call x2, Pallas kernels, product_for_y(): pl.pallas_call(kernel, grid_spec=pltpu.PrefetchScalarGridSpec(num_scalar_...  7.58 us
    pallas_call x1, Pallas kernels, product_for_x(): pl.pallas_call(kernel, grid_spec=pltpu.PrefetchScalarGridSpec(num_scalar_...  6.66 us
  transfers between devices with their start and end apart: 21, of which 11 were waited for; matrix products, arithmetic and copies ran while one was open for 0% of the time, Pallas kernels for 20%

profile of v7, /device:TPU:1, one launch (start us, length us, event | category | flops | bytes accessed | tf_op | source)
XLA Modules:
  0.0 109.3 jit_solution(1330953149822286598)
XLA Ops:
  0.7 1.9 %copy-done = bf16[1024,1536]{1,0:T(8,128)(2,1)S(1)} copy-done((bf16[1024,1536]{1,0:T(8,128)(2,1)S(1)}, bf16[1024,1536]{1,0:T(8,128)(2,1)}, u32[]{:S(2)}) %copy-start) | copy-done | bytes 3145752
  2.6 5.8 %product_theirs.2.rest_0_ = bf16[1536,1024]{1,0:T(8,128)(2,1)S(1)} custom-call(s32[3]{0:T(128)S(1)} %pad_add_fusion.idx_ref, bf16[1024,1536]{1,0:T(8,128)(2,1)S(1)} %copy-done, bf16[1024,4096]{1,0:T(8,128)(2,1)} %c_lower.3), custom_call_target="tpu_custom_call" | custom-call | flops 3221225472 | bytes 8388608 | tf_op jit(solution)/shard_map/product_theirs/pallas_call | solution.py:49
  8.4 3.3 %collective-permute-start = (bf16[1536,1024]{1,0:T(8,128)(2,1)S(1)}, bf16[1536,1024]{1,0:T(8,128)(2,1)S(1)}, u32[]{:S(2)}, u32[]{:S(2)}) collective-permute-start(bf16[1536,1024]{1,0:T(8,128)(2,1)S(1)} %product_theirs.2.rest_0_), channel_id=1, source_target_pairs={{0,4},{4,0},{1,5},{5,1},{2,6},{6,2},{3,7},{7,3},{8,12},{12,8},{9,1... | collective-permute-start | bytes 9437192 | tf_op jit(solution)/shard_map/ppermute | solution.py:32
  11.7 5.8 %product_theirs.3 = bf16[1536,1024]{1,0:T(8,128)(2,1)S(1)} custom-call(s32[3]{0:T(128)S(1)} %pad_add_fusion.idx_ref, bf16[1024,1536]{1,0:T(8,128)(2,1)S(1)} %copy-done, bf16[1024,4096]{1,0:T(8,128)(2,1)} %c_lower.3, bf16[1536,1024]{1,0:T(8,128)(2,1)S(1)} %product_theirs.2.rest_0_), custom_call_target="tpu_custom_call" | custom-call | flops 3221225472 | bytes 8388608 | tf_op jit(solution)/shard_map/product_theirs/pallas_call | solution.py:49
  17.6 3.8 %product_for_y.2 = (bf16[1536,256]{1,0:T(8,128)(2,1)S(1)}, bf16[1536,256]{1,0:T(8,128)(2,1)S(1)}) custom-call(s32[3]{0:T(128)S(1)} %pad_add_fusion.idx_ref, bf16[1024,1536]{1,0:T(8,128)(2,1)S(1)} %copy-done, bf16[1024,4096]{1,0:T(8,128)(2,1)} %c_lower.3, bf16[1024,4096]{1,0:T(8,128)(2,1)} %c_lower.3, bf16[1024,4096]{1,0:T(8,128)(2,1)} %c_lower.3, ...), custom_call_target="tpu_custom_call" | custom-call | flops 1610612736 | bytes 8388608 | tf_op jit(solution)/shard_map/product_for_y/pallas_call | solution.py:97
  21.5 2.7 %collective-permute-start.3 = (bf16[32,48,256]{2,1,0:T(8,128)(2,1)S(1)}, bf16[32,48,256]{2,1,0:T(8,128)(2,1)S(1)}, u32[]{:S(2)}, u32[]{:S(2)}) collective-permute-start(bf16[32,48,256]{2,1,0:T(8,128)(2,1)S(1)} %bitcast.67), channel_id=1, source_target_pairs={{0,3},{1,0},{2,1},{3,2},{4,7},{5,4},{6,5},{7,6},{8,11},{9,8},{10,9... | collective-permute-start | bytes 2359304 | tf_op jit(solution)/shard_map/ppermute | solution.py:32
  24.2 6.7 %product_for_x.1 = (bf16[8,48,1024]{2,1,0:T(8,128)(2,1)S(1)}, bf16[8,48,1024]{2,1,0:T(8,128)(2,1)S(1)}, bf16[8,48,1024]{2,1,0:T(8,128)(2,1)S(1)}, bf16[8,48,1024]{2,1,0:T(8,128)(2,1)S(1)}) custom-call(s32[3]{0:T(128)S(1)} %pad_add_fusion.idx_ref, bf16[1024,1536]{1,0:T(8,128)(2,1)S(1)} %copy-done, bf16[1024,4096]{1,0:T(8,128)(2,1)} %c_lower.3, ...), custom_call_target="tpu_custom_call" | custom-call | flops 3221225472 | bytes 11534336 | tf_op jit(solution)/shard_map/product_for_x/pallas_call | solution.py:128
  30.9 2.7 %collective-permute-start.10 = (bf16[8,48,1024]{2,1,0:T(8,128)(2,1)S(1)}, bf16[8,48,1024]{2,1,0:T(8,128)(2,1)S(1)}, u32[]{:S(2)}, u32[]{:S(2)}) collective-permute-start(bf16[8,48,1024]{2,1,0:T(8,128)(2,1)S(1)} %get-tuple-element.36), channel_id=1, source_target_pairs={{0,24},{8,0},{16,8},{24,16},{1,25},{9,1},{17,9},{25,17},{2,26},{10... | collective-permute-start | bytes 2359304 | tf_op jit(solution)/shard_map/ppermute | solution.py:32
  33.6 3.8 %product_for_y.3 = (bf16[1536,256]{1,0:T(8,128)(2,1)S(1)}, bf16[1536,256]{1,0:T(8,128)(2,1)S(1)}) custom-call(s32[3]{0:T(128)S(1)} %pad_add_fusion.idx_ref, bf16[1024,1536]{1,0:T(8,128)(2,1)S(1)} %copy-done, bf16[1024,4096]{1,0:T(8,128)(2,1)} %c_lower.3, bf16[1024,4096]{1,0:T(8,128)(2,1)} %c_lower.3, bf16[1024,4096]{1,0:T(8,128)(2,1)} %c_lower.3, ...), custom_call_target="tpu_custom_call" | custom-call | flops 1610612736 | bytes 8388608 | tf_op jit(solution)/shard_map/product_for_y/pallas_call | solution.py:97
  37.4 3.9 %collective-permute-done.2.fd.from_down = bf16[32,48,256]{2,1,0:T(8,128)(2,1)S(1)} collective-permute-done((bf16[32,48,256]{2,1,0:T(8,128)(2,1)S(1)}, bf16[32,48,256]{2,1,0:T(8,128)(2,1)S(1)}, u32[]{:S(2)}, u32[]{:S(2)}) %collective-permute-start.2) | collective-permute-done | bytes 786464 | tf_op jit(solution)/shard_map/ppermute | solution.py:32
  41.6 2.7 %collective-permute-start.5 = (bf16[16,48,256]{2,1,0:T(8,128)(2,1)S(1)}, bf16[16,48,256]{2,1,0:T(8,128)(2,1)S(1)}, u32[]{:S(2)}, u32[]{:S(2)}) collective-permute-start(bf16[16,48,256]{2,1,0:T(8,128)(2,1)S(1)} %get-tuple-element.30), channel_id=1, source_target_pairs={{0,3},{1,0},{2,1},{3,2},{4,7},{5,4},{6,5},{7,6},{8,11},{9,8},{10,9... | collective-permute-start | bytes 1179656 | tf_op jit(solution)/shard_map/ppermute | solution.py:32
  44.3 5.8 %collective-permute-done.9.fd.from_down = bf16[8,48,1024]{2,1,0:T(8,128)(2,1)S(1)} collective-permute-done((bf16[8,48,1024]{2,1,0:T(8,128)(2,1)S(1)}, bf16[8,48,1024]{2,1,0:T(8,128)(2,1)S(1)}, u32[]{:S(2)}, u32[]{:S(2)}) %collective-permute-start.9) | collective-permute-done | bytes 786464 | tf_op jit(solution)/shard_map/ppermute | solution.py:32
  50.4 2.7 %collective-permute-start.12 = (bf16[4,48,1024]{2,1,0:T(8,128)(2,1)S(1)}, bf16[4,48,1024]{2,1,0:T(8,128)(2,1)S(1)}, u32[]{:S(2)}, u32[]{:S(2)}) collective-permute-start(bf16[4,48,1024]{2,1,0:T(8,128)(2,1)S(1)} %get-tuple-element.39), channel_id=1, source_target_pairs={{0,24},{8,0},{16,8},{24,16},{1,25},{9,1},{17,9},{25,17},{2,26},{10... | collective-permute-start | bytes 1179656 | tf_op jit(solution)/shard_map/ppermute | solution.py:32
  54.0 2.7 %collective-permute-start.7 = (bf16[8,48,256]{2,1,0:T(8,128)(2,1)S(1)}, bf16[8,48,256]{2,1,0:T(8,128)(2,1)S(1)}, u32[]{:S(2)}, u32[]{:S(2)}) collective-permute-start(bf16[8,48,256]{2,1,0:T(8,128)(2,1)S(1)} %get-tuple-element.33), channel_id=1, source_target_pairs={{0,24},{8,0},{16,8},{24,16},{1,25},{9,1},{17,9},{25,17},{2,26},{10... | collective-permute-start | bytes 589832 | tf_op jit(solution)/shard_map/ppermute | solution.py:32
  56.7 3.6 %collective-permute-done.11.up = bf16[4,48,1024]{2,1,0:T(8,128)(2,1)S(1)} collective-permute-done((bf16[4,48,1024]{2,1,0:T(8,128)(2,1)S(1)}, bf16[4,48,1024]{2,1,0:T(8,128)(2,1)S(1)}, u32[]{:S(2)}, u32[]{:S(2)}) %collective-permute-start.11) | collective-permute-done | bytes 393248 | tf_op jit(solution)/shard_map/ppermute | solution.py:32
  61.2 2.7 %collective-permute-start.14 = (bf16[8,48,256]{2,1,0:T(8,128)(2,1)S(1)}, bf16[8,48,256]{2,1,0:T(8,128)(2,1)S(1)}, u32[]{:S(2)}, u32[]{:S(2)}) collective-permute-start(bf16[8,48,256]{2,1,0:T(8,128)(2,1)S(1)} %get-tuple-element.42), channel_id=1, source_target_pairs={{0,3},{1,0},{2,1},{3,2},{4,7},{5,4},{6,5},{7,6},{8,11},{9,8},{10,9... | collective-permute-start | bytes 589832 | tf_op jit(solution)/shard_map/ppermute | solution.py:32
  65.4 3.6 %collective-permute-done.8.refs_3_ = bf16[8,48,256]{2,1,0:T(8,128)(2,1)S(1)} collective-permute-done((bf16[8,48,256]{2,1,0:T(8,128)(2,1)S(1)}, bf16[8,48,256]{2,1,0:T(8,128)(2,1)S(1)}, u32[]{:S(2)}, u32[]{:S(2)}) %collective-permute-start.8) | collective-permute-done | bytes 196640 | tf_op jit(solution)/shard_map/ppermute | solution.py:32
  69.0 2.7 %collective-permute-done.15.refs_7_ = bf16[8,48,256]{2,1,0:T(8,128)(2,1)S(1)} collective-permute-done((bf16[8,48,256]{2,1,0:T(8,128)(2,1)S(1)}, bf16[8,48,256]{2,1,0:T(8,128)(2,1)S(1)}, u32[]{:S(2)}, u32[]{:S(2)}) %collective-permute-start.15) | collective-permute-done | bytes 196640 | tf_op jit(solution)/shard_map/ppermute | solution.py:32
  72.7 9.6 %all-to-all-start = ((bf16[32,24,256]{2,1,0:T(8,128)(2,1)}), bf16[32,24,256]{2,1,0:T(8,128)(2,1)S(1)}, u32[]{:S(2)}, u32[]{:S(2)}) async-start(bf16[32,24,256]{2,1,0:T(8,128)(2,1)} %sum_for_z.1), calls=%async_computation | async-start | bytes 786432 | tf_op jit(solution)/shard_map/all_to_all | solution.py:40
  82.3 11.6 %all-to-all-done = bf16[32,24,256]{2,1,0:T(8,128)(2,1)S(1)} async-done(((bf16[32,24,256]{2,1,0:T(8,128)(2,1)}), bf16[32,24,256]{2,1,0:T(8,128)(2,1)S(1)}, u32[]{:S(2)}, u32[]{:S(2)}) %all-to-all-start) | async-done | bytes 393248 | tf_op jit(solution)/shard_map/all_to_all | solution.py:40
  94.0 5.8 %collective-permute-start.16 = (bf16[4,2,6,256]{3,0,2,1:T(4,128)(2,1)S(1)}, bf16[4,2,6,256]{3,0,2,1:T(4,128)(2,1)S(1)}, u32[]{:S(2)}, u32[]{:S(2)}) collective-permute-start(bf16[4,2,6,256]{3,0,2,1:T(4,128)(2,1)S(1)} %fusion.3), channel_id=1, source_target_pairs={{0,4},{4,0},{1,5},{5,1},{2,6},{6,2},{3,7},{7,3},{8,12},{12,8},{9,1... | collective-permute-start | bytes 73736 | tf_op jit(solution)/shard_map/ppermute | solution.py:32
  101.8 1.4 %collective-permute-start.18 = (bf16[6,4096]{1,0:T(8,128)(2,1)S(1)}, bf16[6,4096]{1,0:T(8,128)(2,1)S(1)}, u32[]{:S(2)}, u32[]{:S(2)}) collective-permute-start(bf16[6,4096]{1,0:T(8,128)(2,1)S(1)} %get-tuple-element.44), channel_id=1, source_target_pairs={{0,2},{1,3},{2,0},{3,1},{4,6},{5,7},{6,4},{7,5},{8,10},{9,11},{10,... | collective-permute-start | bytes 147464 | tf_op jit(solution)/shard_map/ppermute | solution.py:32
  104.6 1.8 %collective-permute-done.18 = bf16[6,4096]{1,0:T(8,128)(2,1)S(1)} collective-permute-done((bf16[6,4096]{1,0:T(8,128)(2,1)S(1)}, bf16[6,4096]{1,0:T(8,128)(2,1)S(1)}, u32[]{:S(2)}, u32[]{:S(2)}) %collective-permute-start.18) | collective-permute-done | bytes 49184 | tf_op jit(solution)/shard_map/ppermute | solution.py:32
  106.9 1.6 %collective-permute-done.17 = bf16[6,4096]{1,0:T(8,128)(2,1)S(1)} collective-permute-done((bf16[6,4096]{1,0:T(8,128)(2,1)S(1)}, bf16[6,4096]{1,0:T(8,128)(2,1)S(1)}, u32[]{:S(2)}, u32[]{:S(2)}) %collective-permute-start.17) | collective-permute-done | bytes 49184 | tf_op jit(solution)/shard_map/ppermute | solution.py:32
  (63 shorter events, 10.0 us)
Async XLA Ops:
  8.4 9.2 %collective-permute-start = (bf16[1536,1024]{1,0:T(8,128)(2,1)S(1)}, bf16[1536,1024]{1,0:T(8,128)(2,1)S(1)}, u32[]{:S(2)}, u32[]{:S(2)}) collective-permute-start(bf16[1536,1024]{1,0:T(8,128)(2,1)S(1)} %product_theirs.2.rest_0_), channel_id=1, source_target_pairs={{0,4},{4,0},{1,5},{5,1},{2,6},{6,2},{3,7},{7,3},{8,12},{12,8},{9,1... | collective-permute-start | bytes 9437192 | tf_op jit(solution)/shard_map/ppermute | solution.py:32
  17.5 6.7 %collective-permute-start.1 = (bf16[1536,1024]{1,0:T(8,128)(2,1)S(1)}, bf16[1536,1024]{1,0:T(8,128)(2,1)S(1)}, u32[]{:S(2)}, u32[]{:S(2)}) collective-permute-start(bf16[1536,1024]{1,0:T(8,128)(2,1)S(1)} %product_theirs.3), channel_id=1, source_target_pairs={{0,4},{4,0},{1,5},{5,1},{2,6},{6,2},{3,7},{7,3},{8,12},{12,8},{9,1... | collective-permute-start | bytes 9437192 | tf_op jit(solution)/shard_map/ppermute | solution.py:32
  21.4 19.9 %collective-permute-start.2 = (bf16[32,48,256]{2,1,0:T(8,128)(2,1)S(1)}, bf16[32,48,256]{2,1,0:T(8,128)(2,1)S(1)}, u32[]{:S(2)}, u32[]{:S(2)}) collective-permute-start(bf16[32,48,256]{2,1,0:T(8,128)(2,1)S(1)} %bitcast.64), channel_id=1, source_target_pairs={{0,1},{1,2},{2,3},{3,0},{4,5},{5,6},{6,7},{7,4},{8,9},{9,10},{10,1... | collective-permute-start | bytes 2359304 | tf_op jit(solution)/shard_map/ppermute | solution.py:32
  21.5 19.8 %collective-permute-start.3 = (bf16[32,48,256]{2,1,0:T(8,128)(2,1)S(1)}, bf16[32,48,256]{2,1,0:T(8,128)(2,1)S(1)}, u32[]{:S(2)}, u32[]{:S(2)}) collective-permute-start(bf16[32,48,256]{2,1,0:T(8,128)(2,1)S(1)} %bitcast.67), channel_id=1, source_target_pairs={{0,3},{1,0},{2,1},{3,2},{4,7},{5,4},{6,5},{7,6},{8,11},{9,8},{10,9... | collective-permute-start | bytes 2359304 | tf_op jit(solution)/shard_map/ppermute | solution.py:32
  30.8 19.3 %collective-permute-start.9 = (bf16[8,48,1024]{2,1,0:T(8,128)(2,1)S(1)}, bf16[8,48,1024]{2,1,0:T(8,128)(2,1)S(1)}, u32[]{:S(2)}, u32[]{:S(2)}) collective-permute-start(bf16[8,48,1024]{2,1,0:T(8,128)(2,1)S(1)} %get-tuple-element.35), channel_id=1, source_target_pairs={{0,8},{8,16},{16,24},{24,0},{1,9},{9,17},{17,25},{25,1},{2,10},{10... | collective-permute-start | bytes 2359304 | tf_op jit(solution)/shard_map/ppermute | solution.py:32
  30.9 19.2 %collective-permute-start.10 = (bf16[8,48,1024]{2,1,0:T(8,128)(2,1)S(1)}, bf16[8,48,1024]{2,1,0:T(8,128)(2,1)S(1)}, u32[]{:S(2)}, u32[]{:S(2)}) collective-permute-start(bf16[8,48,1024]{2,1,0:T(8,128)(2,1)S(1)} %get-tuple-element.36), channel_id=1, source_target_pairs={{0,24},{8,0},{16,8},{24,16},{1,25},{9,1},{17,9},{25,17},{2,26},{10... | collective-permute-start | bytes 2359304 | tf_op jit(solution)/shard_map/ppermute | solution.py:32
  41.5 11.5 %collective-permute-start.4 = (bf16[16,48,256]{2,1,0:T(8,128)(2,1)S(1)}, bf16[16,48,256]{2,1,0:T(8,128)(2,1)S(1)}, u32[]{:S(2)}, u32[]{:S(2)}) collective-permute-start(bf16[16,48,256]{2,1,0:T(8,128)(2,1)S(1)} %get-tuple-element.29), channel_id=1, source_target_pairs={{0,1},{1,2},{2,3},{3,0},{4,5},{5,6},{6,7},{7,4},{8,9},{9,10},{10,1... | collective-permute-start | bytes 1179656 | tf_op jit(solution)/shard_map/ppermute | solution.py:32
  41.6 11.5 %collective-permute-start.5 = (bf16[16,48,256]{2,1,0:T(8,128)(2,1)S(1)}, bf16[16,48,256]{2,1,0:T(8,128)(2,1)S(1)}, u32[]{:S(2)}, u32[]{:S(2)}) collective-permute-start(bf16[16,48,256]{2,1,0:T(8,128)(2,1)S(1)} %get-tuple-element.30), channel_id=1, source_target_pairs={{0,3},{1,0},{2,1},{3,2},{4,7},{5,4},{6,5},{7,6},{8,11},{9,8},{10,9... | collective-permute-start | bytes 1179656 | tf_op jit(solution)/shard_map/ppermute | solution.py:32
  50.3 9.9 %collective-permute-start.11 = (bf16[4,48,1024]{2,1,0:T(8,128)(2,1)S(1)}, bf16[4,48,1024]{2,1,0:T(8,128)(2,1)S(1)}, u32[]{:S(2)}, u32[]{:S(2)}) collective-permute-start(bf16[4,48,1024]{2,1,0:T(8,128)(2,1)S(1)} %get-tuple-element.38), channel_id=1, source_target_pairs={{0,8},{8,16},{16,24},{24,0},{1,9},{9,17},{17,25},{25,1},{2,10},{10... | collective-permute-start | bytes 1179656 | tf_op jit(solution)/shard_map/ppermute | solution.py:32
  50.4 9.8 %collective-permute-start.12 = (bf16[4,48,1024]{2,1,0:T(8,128)(2,1)S(1)}, bf16[4,48,1024]{2,1,0:T(8,128)(2,1)S(1)}, u32[]{:S(2)}, u32[]{:S(2)}) collective-permute-start(bf16[4,48,1024]{2,1,0:T(8,128)(2,1)S(1)} %get-tuple-element.39), channel_id=1, source_target_pairs={{0,24},{8,0},{16,8},{24,16},{1,25},{9,1},{17,9},{25,17},{2,26},{10... | collective-permute-start | bytes 1179656 | tf_op jit(solution)/shard_map/ppermute | solution.py:32
  53.9 10.5 %collective-permute-start.6 = (bf16[8,48,256]{2,1,0:T(8,128)(2,1)S(1)}, bf16[8,48,256]{2,1,0:T(8,128)(2,1)S(1)}, u32[]{:S(2)}, u32[]{:S(2)}) collective-permute-start(bf16[8,48,256]{2,1,0:T(8,128)(2,1)S(1)} %get-tuple-element.32), channel_id=1, source_target_pairs={{0,8},{8,16},{16,24},{24,0},{1,9},{9,17},{17,25},{25,1},{2,10},{10... | collective-permute-start | bytes 589832 | tf_op jit(solution)/shard_map/ppermute | solution.py:32
  54.0 11.4 %collective-permute-start.7 = (bf16[8,48,256]{2,1,0:T(8,128)(2,1)S(1)}, bf16[8,48,256]{2,1,0:T(8,128)(2,1)S(1)}, u32[]{:S(2)}, u32[]{:S(2)}) collective-permute-start(bf16[8,48,256]{2,1,0:T(8,128)(2,1)S(1)} %get-tuple-element.33), channel_id=1, source_target_pairs={{0,24},{8,0},{16,8},{24,16},{1,25},{9,1},{17,9},{25,17},{2,26},{10... | collective-permute-start | bytes 589832 | tf_op jit(solution)/shard_map/ppermute | solution.py:32
  56.6 44.3 %copy-start.1 = (f32[6,4096]{1,0:T(8,128)S(1)}, f32[6,4096]{1,0:T(8,128)}, u32[]{:S(2)}) copy-start(f32[6,4096]{1,0:T(8,128)} %param.7) | copy-start | bytes 294916
  56.6 44.3 %copy-start.2 = (f32[6,4096]{1,0:T(8,128)S(1)}, f32[6,4096]{1,0:T(8,128)}, u32[]{:S(2)}) copy-start(f32[6,4096]{1,0:T(8,128)} %param.8) | copy-start | bytes 294916
  56.7 44.3 %copy-start.3 = (f32[6,4096]{1,0:T(8,128)S(1)}, f32[6,4096]{1,0:T(8,128)}, u32[]{:S(2)}) copy-start(f32[6,4096]{1,0:T(8,128)} %param.9) | copy-start | bytes 294916
  56.7 12.3 %collective-permute-start.8 = (bf16[8,48,256]{2,1,0:T(8,128)(2,1)S(1)}, bf16[8,48,256]{2,1,0:T(8,128)(2,1)S(1)}, u32[]{:S(2)}, u32[]{:S(2)}) collective-permute-start(bf16[8,48,256]{2,1,0:T(8,128)(2,1)S(1)} %get-tuple-element.34), channel_id=1, source_target_pairs={{0,16},{8,24},{16,0},{24,8},{1,17},{9,25},{17,1},{25,9},{2,18},{10... | collective-permute-start | bytes 589832 | tf_op jit(solution)/shard_map/ppermute | solution.py:32
  61.1 7.9 %collective-permute-start.13 = (bf16[8,48,256]{2,1,0:T(8,128)(2,1)S(1)}, bf16[8,48,256]{2,1,0:T(8,128)(2,1)S(1)}, u32[]{:S(2)}, u32[]{:S(2)}) collective-permute-start(bf16[8,48,256]{2,1,0:T(8,128)(2,1)S(1)} %get-tuple-element.41), channel_id=1, source_target_pairs={{0,1},{1,2},{2,3},{3,0},{4,5},{5,6},{6,7},{7,4},{8,9},{9,10},{10,1... | collective-permute-start | bytes 589832 | tf_op jit(solution)/shard_map/ppermute | solution.py:32
  61.2 7.8 %collective-permute-start.14 = (bf16[8,48,256]{2,1,0:T(8,128)(2,1)S(1)}, bf16[8,48,256]{2,1,0:T(8,128)(2,1)S(1)}, u32[]{:S(2)}, u32[]{:S(2)}) collective-permute-start(bf16[8,48,256]{2,1,0:T(8,128)(2,1)S(1)} %get-tuple-element.42), channel_id=1, source_target_pairs={{0,3},{1,0},{2,1},{3,2},{4,7},{5,4},{6,5},{7,6},{8,11},{9,8},{10,9... | collective-permute-start | bytes 589832 | tf_op jit(solution)/shard_map/ppermute | solution.py:32
  64.4 7.2 %collective-permute-start.15 = (bf16[8,48,256]{2,1,0:T(8,128)(2,1)S(1)}, bf16[8,48,256]{2,1,0:T(8,128)(2,1)S(1)}, u32[]{:S(2)}, u32[]{:S(2)}) collective-permute-start(bf16[8,48,256]{2,1,0:T(8,128)(2,1)S(1)} %get-tuple-element.43), channel_id=1, source_target_pairs={{0,2},{1,3},{2,0},{3,1},{4,6},{5,7},{6,4},{7,5},{8,10},{9,11},{10,... | collective-permute-start | bytes 589832 | tf_op jit(solution)/shard_map/ppermute | solution.py:32
  72.7 21.2 %all-to-all-start = ((bf16[32,24,256]{2,1,0:T(8,128)(2,1)}), bf16[32,24,256]{2,1,0:T(8,128)(2,1)S(1)}, u32[]{:S(2)}, u32[]{:S(2)}) async-start(bf16[32,24,256]{2,1,0:T(8,128)(2,1)} %sum_for_z.1), calls=%async_computation | async-start | bytes 786432 | tf_op jit(solution)/shard_map/all_to_all | solution.py:40
  94.0 6.6 %collective-permute-start.16 = (bf16[4,2,6,256]{3,0,2,1:T(4,128)(2,1)S(1)}, bf16[4,2,6,256]{3,0,2,1:T(4,128)(2,1)S(1)}, u32[]{:S(2)}, u32[]{:S(2)}) collective-permute-start(bf16[4,2,6,256]{3,0,2,1:T(4,128)(2,1)S(1)} %fusion.3), channel_id=1, source_target_pairs={{0,4},{4,0},{1,5},{5,1},{2,6},{6,2},{3,7},{7,3},{8,12},{12,8},{9,1... | collective-permute-start | bytes 73736 | tf_op jit(solution)/shard_map/ppermute | solution.py:32
  101.8 4.6 %collective-permute-start.18 = (bf16[6,4096]{1,0:T(8,128)(2,1)S(1)}, bf16[6,4096]{1,0:T(8,128)(2,1)S(1)}, u32[]{:S(2)}, u32[]{:S(2)}) collective-permute-start(bf16[6,4096]{1,0:T(8,128)(2,1)S(1)} %get-tuple-element.44), channel_id=1, source_target_pairs={{0,2},{1,3},{2,0},{3,1},{4,6},{5,7},{6,4},{7,5},{8,10},{9,11},{10,... | collective-permute-start | bytes 147464 | tf_op jit(solution)/shard_map/ppermute | solution.py:32
  103.1 3.7 %collective-permute-start.19 = (bf16[6,4096]{1,0:T(8,128)(2,1)S(1)}, bf16[6,4096]{1,0:T(8,128)(2,1)S(1)}, u32[]{:S(2)}, u32[]{:S(2)}) collective-permute-start(bf16[6,4096]{1,0:T(8,128)(2,1)S(1)} %get-tuple-element.44), channel_id=1, source_target_pairs={{0,3},{1,0},{2,1},{3,2},{4,7},{5,4},{6,5},{7,6},{8,11},{9,8},{10,9... | collective-permute-start | bytes 147464 | tf_op jit(solution)/shard_map/ppermute | solution.py:32
  104.2 4.3 %collective-permute-start.17 = (bf16[6,4096]{1,0:T(8,128)(2,1)S(1)}, bf16[6,4096]{1,0:T(8,128)(2,1)S(1)}, u32[]{:S(2)}, u32[]{:S(2)}) collective-permute-start(bf16[6,4096]{1,0:T(8,128)(2,1)S(1)} %get-tuple-element.44), channel_id=1, source_target_pairs={{0,1},{1,2},{2,3},{3,0},{4,5},{5,6},{6,7},{7,4},{8,9},{9,10},{10,1... | collective-permute-start | bytes 147464 | tf_op jit(solution)/shard_map/ppermute | solution.py:32
  (1 other events, 1.9 us)

commit v8 on v7

--- a/solution.py
+++ b/solution.py
@@ -114,15 +114,16 @@
 def product_for_x(acts, cot, got, idx, base, ncols, after):
     tn = 2 * TN
 
-    def kernel(idx_ref, a, c, r, _, *rest):
-        outs, acc = rest[:-1], rest[-1]
-        acc[...] = lax.dot_general(a[...], c[...], DN, preferred_element_type=F32) + r[...].astype(F32)
-        for o in range(NX):
-            x = ahead(idx_ref, "x", o)
-            for out, half in parts_of(o, NZ // 2):
-                for z in range(half.start, half.stop):
-                    rows = pl.ds(pl.multiple_of((z * NX + x) * BLK, BLK), BLK)
-                    outs[out][z] = acc[rows, :].astype(BF16)
+    def kernel(idx_ref, a, c, r, _, *outs):
+        acc = lax.dot_general(a[...], c[...], DN, preferred_element_type=F32) + r[...].astype(F32)
+        acc = acc.astype(BF16).reshape(NZ, NX, BLK, tn)
+        for me in range(NX):
+
+            @pl.when(idx_ref[1] == me)
+            def _():
+                for o in range(NX):
+                    for out, half in parts_of(o, NZ // 2):
+                        outs[out][half] = acc[half, (me + o) % NX]
 
     shapes = [jax.ShapeDtypeStruct((NZ, BLK, ncols), BF16)] * 4
     return pl.pallas_call(
@@ -137,7 +138,6 @@
                 pl.BlockSpec(memory_space=pl.ANY),
             ],
             out_specs=[pl.BlockSpec(o.shape[:2] + (tn,), lambda j, s: (0, 0, j)) for o in shapes],
-            scratch_shapes=[pltpu.VMEM((D, tn), F32)],
         ),
         out_shape=shapes,
         name="product_for_x",

time: 111 us -> 111 us (level)
  no operation moved by 1% of the time
where the time goes in v8:
time: 111 us; the launch traced here: 109 us
  starting transfers between devices  39.2 us (35%)
  waiting for transfers between devices  36.4 us (33%)
  Pallas kernels  28.4 us (26%)
  local copies, waits for them, and re-layouts  2.09 us (2%)
  other arithmetic  1.81 us (2%)
    ppermute x20, starting transfers between devices, shift(): return lax.ppermute(v, axis, [(i, (i + s) % n) for i in range(n)])  29.7 us
    ppermute x20, waiting for transfers between devices, shift(): return lax.ppermute(v, axis, [(i, (i + s) % n) for i in range(n)])  24.9 us
    pallas_call x2, Pallas kernels, product(): pl.pallas_call(kernel, grid_spec=pltpu.PrefetchScalarGridSpec(num_scalar_...  11.5 us
    all_to_all x1, waiting for transfers between devices, swap(): return lax.all_to_all(v, axes, 0, 0, tiled=True)  11.5 us
    all_to_all x1, starting transfers between devices, swap(): return lax.all_to_all(v, axes, 0, 0, tiled=True)  9.55 us
    pallas_call x2, Pallas kernels, product_for_y(): pl.pallas_call(kernel, grid_spec=pltpu.PrefetchScalarGridSpec(num_scalar_...  7.58 us
    pallas_call x1, Pallas kernels, product_for_x(): pl.pallas_call(kernel, grid_spec=pltpu.PrefetchScalarGridSpec(num_scalar_...  6.18 us
  transfers between devices with their start and end apart: 21, of which 11 were waited for; matrix products, arithmetic and copies ran while one was open for 0% of the time, Pallas kernels for 20%

profile of v8, /device:TPU:1, one launch (start us, length us, event | category | flops | bytes accessed | tf_op | source)
XLA Modules:
  0.0 108.8 jit_solution(15892689392283027768)
XLA Ops:
  0.7 1.9 %copy-done = bf16[1024,1536]{1,0:T(8,128)(2,1)S(1)} copy-done((bf16[1024,1536]{1,0:T(8,128)(2,1)S(1)}, bf16[1024,1536]{1,0:T(8,128)(2,1)}, u32[]{:S(2)}) %copy-start) | copy-done | bytes 3145752
  2.6 5.8 %product_theirs.2.rest_0_ = bf16[1536,1024]{1,0:T(8,128)(2,1)S(1)} custom-call(s32[3]{0:T(128)S(1)} %pad_add_fusion.idx_ref, bf16[1024,1536]{1,0:T(8,128)(2,1)S(1)} %copy-done, bf16[1024,4096]{1,0:T(8,128)(2,1)} %c_lower.3), custom_call_target="tpu_custom_call" | custom-call | flops 3221225472 | bytes 8388608 | tf_op jit(solution)/shard_map/product_theirs/pallas_call | solution.py:49
  8.4 3.3 %collective-permute-start = (bf16[1536,1024]{1,0:T(8,128)(2,1)S(1)}, bf16[1536,1024]{1,0:T(8,128)(2,1)S(1)}, u32[]{:S(2)}, u32[]{:S(2)}) collective-permute-start(bf16[1536,1024]{1,0:T(8,128)(2,1)S(1)} %product_theirs.2.rest_0_), channel_id=1, source_target_pairs={{0,4},{4,0},{1,5},{5,1},{2,6},{6,2},{3,7},{7,3},{8,12},{12,8},{9,1... | collective-permute-start | bytes 9437192 | tf_op jit(solution)/shard_map/ppermute | solution.py:32
  11.7 5.8 %product_theirs.3 = bf16[1536,1024]{1,0:T(8,128)(2,1)S(1)} custom-call(s32[3]{0:T(128)S(1)} %pad_add_fusion.idx_ref, bf16[1024,1536]{1,0:T(8,128)(2,1)S(1)} %copy-done, bf16[1024,4096]{1,0:T(8,128)(2,1)} %c_lower.3, bf16[1536,1024]{1,0:T(8,128)(2,1)S(1)} %product_theirs.2.rest_0_), custom_call_target="tpu_custom_call" | custom-call | flops 3221225472 | bytes 8388608 | tf_op jit(solution)/shard_map/product_theirs/pallas_call | solution.py:49
  17.6 3.8 %product_for_y.2 = (bf16[1536,256]{1,0:T(8,128)(2,1)S(1)}, bf16[1536,256]{1,0:T(8,128)(2,1)S(1)}) custom-call(s32[3]{0:T(128)S(1)} %pad_add_fusion.idx_ref, bf16[1024,1536]{1,0:T(8,128)(2,1)S(1)} %copy-done, bf16[1024,4096]{1,0:T(8,128)(2,1)} %c_lower.3, bf16[1024,4096]{1,0:T(8,128)(2,1)} %c_lower.3, bf16[1024,4096]{1,0:T(8,128)(2,1)} %c_lower.3, ...), custom_call_target="tpu_custom_call" | custom-call | flops 1610612736 | bytes 8388608 | tf_op jit(solution)/shard_map/product_for_y/pallas_call | solution.py:97
  21.5 2.7 %collective-permute-start.3 = (bf16[32,48,256]{2,1,0:T(8,128)(2,1)S(1)}, bf16[32,48,256]{2,1,0:T(8,128)(2,1)S(1)}, u32[]{:S(2)}, u32[]{:S(2)}) collective-permute-start(bf16[32,48,256]{2,1,0:T(8,128)(2,1)S(1)} %bitcast.67), channel_id=1, source_target_pairs={{0,3},{1,0},{2,1},{3,2},{4,7},{5,4},{6,5},{7,6},{8,11},{9,8},{10,9... | collective-permute-start | bytes 2359304 | tf_op jit(solution)/shard_map/ppermute | solution.py:32
  24.2 6.2 %product_for_x.1 = (bf16[8,48,1024]{2,1,0:T(8,128)(2,1)S(1)}, bf16[8,48,1024]{2,1,0:T(8,128)(2,1)S(1)}, bf16[8,48,1024]{2,1,0:T(8,128)(2,1)S(1)}, bf16[8,48,1024]{2,1,0:T(8,128)(2,1)S(1)}) custom-call(s32[3]{0:T(128)S(1)} %pad_add_fusion.idx_ref, bf16[1024,1536]{1,0:T(8,128)(2,1)S(1)} %copy-done, bf16[1024,4096]{1,0:T(8,128)(2,1)} %c_lower.3, ...), custom_call_target="tpu_custom_call" | custom-call | flops 3221225472 | bytes 11534336 | tf_op jit(solution)/shard_map/product_for_x/pallas_call | solution.py:129
  30.4 2.7 %collective-permute-start.10 = (bf16[8,48,1024]{2,1,0:T(8,128)(2,1)S(1)}, bf16[8,48,1024]{2,1,0:T(8,128)(2,1)S(1)}, u32[]{:S(2)}, u32[]{:S(2)}) collective-permute-start(bf16[8,48,1024]{2,1,0:T(8,128)(2,1)S(1)} %get-tuple-element.36), channel_id=1, source_target_pairs={{0,24},{8,0},{16,8},{24,16},{1,25},{9,1},{17,9},{25,17},{2,26},{10... | collective-permute-start | bytes 2359304 | tf_op jit(solution)/shard_map/ppermute | solution.py:32
  33.1 3.8 %product_for_y.3 = (bf16[1536,256]{1,0:T(8,128)(2,1)S(1)}, bf16[1536,256]{1,0:T(8,128)(2,1)S(1)}) custom-call(s32[3]{0:T(128)S(1)} %pad_add_fusion.idx_ref, bf16[1024,1536]{1,0:T(8,128)(2,1)S(1)} %copy-done, bf16[1024,4096]{1,0:T(8,128)(2,1)} %c_lower.3, bf16[1024,4096]{1,0:T(8,128)(2,1)} %c_lower.3, bf16[1024,4096]{1,0:T(8,128)(2,1)} %c_lower.3, ...), custom_call_target="tpu_custom_call" | custom-call | flops 1610612736 | bytes 8388608 | tf_op jit(solution)/shard_map/product_for_y/pallas_call | solution.py:97
  36.9 4.4 %collective-permute-done.2.fd.from_down = bf16[32,48,256]{2,1,0:T(8,128)(2,1)S(1)} collective-permute-done((bf16[32,48,256]{2,1,0:T(8,128)(2,1)S(1)}, bf16[32,48,256]{2,1,0:T(8,128)(2,1)S(1)}, u32[]{:S(2)}, u32[]{:S(2)}) %collective-permute-start.2) | collective-permute-done | bytes 786464 | tf_op jit(solution)/shard_map/ppermute | solution.py:32
  41.6 2.7 %collective-permute-start.5 = (bf16[16,48,256]{2,1,0:T(8,128)(2,1)S(1)}, bf16[16,48,256]{2,1,0:T(8,128)(2,1)S(1)}, u32[]{:S(2)}, u32[]{:S(2)}) collective-permute-start(bf16[16,48,256]{2,1,0:T(8,128)(2,1)S(1)} %get-tuple-element.30), channel_id=1, source_target_pairs={{0,3},{1,0},{2,1},{3,2},{4,7},{5,4},{6,5},{7,6},{8,11},{9,8},{10,9... | collective-permute-start | bytes 1179656 | tf_op jit(solution)/shard_map/ppermute | solution.py:32
  44.3 5.4 %collective-permute-done.9.fd.from_down = bf16[8,48,1024]{2,1,0:T(8,128)(2,1)S(1)} collective-permute-done((bf16[8,48,1024]{2,1,0:T(8,128)(2,1)S(1)}, bf16[8,48,1024]{2,1,0:T(8,128)(2,1)S(1)}, u32[]{:S(2)}, u32[]{:S(2)}) %collective-permute-start.9) | collective-permute-done | bytes 786464 | tf_op jit(solution)/shard_map/ppermute | solution.py:32
  49.9 2.7 %collective-permute-start.12 = (bf16[4,48,1024]{2,1,0:T(8,128)(2,1)S(1)}, bf16[4,48,1024]{2,1,0:T(8,128)(2,1)S(1)}, u32[]{:S(2)}, u32[]{:S(2)}) collective-permute-start(bf16[4,48,1024]{2,1,0:T(8,128)(2,1)S(1)} %get-tuple-element.39), channel_id=1, source_target_pairs={{0,24},{8,0},{16,8},{24,16},{1,25},{9,1},{17,9},{25,17},{2,26},{10... | collective-permute-start | bytes 1179656 | tf_op jit(solution)/shard_map/ppermute | solution.py:32
  53.5 2.7 %collective-permute-start.7 = (bf16[8,48,256]{2,1,0:T(8,128)(2,1)S(1)}, bf16[8,48,256]{2,1,0:T(8,128)(2,1)S(1)}, u32[]{:S(2)}, u32[]{:S(2)}) collective-permute-start(bf16[8,48,256]{2,1,0:T(8,128)(2,1)S(1)} %get-tuple-element.33), channel_id=1, source_target_pairs={{0,24},{8,0},{16,8},{24,16},{1,25},{9,1},{17,9},{25,17},{2,26},{10... | collective-permute-start | bytes 589832 | tf_op jit(solution)/shard_map/ppermute | solution.py:32
  56.2 3.6 %collective-permute-done.11.up = bf16[4,48,1024]{2,1,0:T(8,128)(2,1)S(1)} collective-permute-done((bf16[4,48,1024]{2,1,0:T(8,128)(2,1)S(1)}, bf16[4,48,1024]{2,1,0:T(8,128)(2,1)S(1)}, u32[]{:S(2)}, u32[]{:S(2)}) %collective-permute-start.11) | collective-permute-done | bytes 393248 | tf_op jit(solution)/shard_map/ppermute | solution.py:32
  60.7 2.7 %collective-permute-start.14 = (bf16[8,48,256]{2,1,0:T(8,128)(2,1)S(1)}, bf16[8,48,256]{2,1,0:T(8,128)(2,1)S(1)}, u32[]{:S(2)}, u32[]{:S(2)}) collective-permute-start(bf16[8,48,256]{2,1,0:T(8,128)(2,1)S(1)} %get-tuple-element.42), channel_id=1, source_target_pairs={{0,3},{1,0},{2,1},{3,2},{4,7},{5,4},{6,5},{7,6},{8,11},{9,8},{10,9... | collective-permute-start | bytes 589832 | tf_op jit(solution)/shard_map/ppermute | solution.py:32
  64.9 3.6 %collective-permute-done.8.refs_3_ = bf16[8,48,256]{2,1,0:T(8,128)(2,1)S(1)} collective-permute-done((bf16[8,48,256]{2,1,0:T(8,128)(2,1)S(1)}, bf16[8,48,256]{2,1,0:T(8,128)(2,1)S(1)}, u32[]{:S(2)}, u32[]{:S(2)}) %collective-permute-start.8) | collective-permute-done | bytes 196640 | tf_op jit(solution)/shard_map/ppermute | solution.py:32
  68.5 2.7 %collective-permute-done.15.refs_7_ = bf16[8,48,256]{2,1,0:T(8,128)(2,1)S(1)} collective-permute-done((bf16[8,48,256]{2,1,0:T(8,128)(2,1)S(1)}, bf16[8,48,256]{2,1,0:T(8,128)(2,1)S(1)}, u32[]{:S(2)}, u32[]{:S(2)}) %collective-permute-start.15) | collective-permute-done | bytes 196640 | tf_op jit(solution)/shard_map/ppermute | solution.py:32
  72.2 9.5 %all-to-all-start = ((bf16[32,24,256]{2,1,0:T(8,128)(2,1)}), bf16[32,24,256]{2,1,0:T(8,128)(2,1)S(1)}, u32[]{:S(2)}, u32[]{:S(2)}) async-start(bf16[32,24,256]{2,1,0:T(8,128)(2,1)} %sum_for_z.1), calls=%async_computation | async-start | bytes 786432 | tf_op jit(solution)/shard_map/all_to_all | solution.py:40
  81.7 11.5 %all-to-all-done = bf16[32,24,256]{2,1,0:T(8,128)(2,1)S(1)} async-done(((bf16[32,24,256]{2,1,0:T(8,128)(2,1)}), bf16[32,24,256]{2,1,0:T(8,128)(2,1)S(1)}, u32[]{:S(2)}, u32[]{:S(2)}) %all-to-all-start) | async-done | bytes 393248 | tf_op jit(solution)/shard_map/all_to_all | solution.py:40
  93.4 5.9 %collective-permute-start.16 = (bf16[4,2,6,256]{3,0,2,1:T(4,128)(2,1)S(1)}, bf16[4,2,6,256]{3,0,2,1:T(4,128)(2,1)S(1)}, u32[]{:S(2)}, u32[]{:S(2)}) collective-permute-start(bf16[4,2,6,256]{3,0,2,1:T(4,128)(2,1)S(1)} %fusion.3), channel_id=1, source_target_pairs={{0,4},{4,0},{1,5},{5,1},{2,6},{6,2},{3,7},{7,3},{8,12},{12,8},{9,1... | collective-permute-start | bytes 73736 | tf_op jit(solution)/shard_map/ppermute | solution.py:32
  101.3 1.5 %collective-permute-start.18 = (bf16[6,4096]{1,0:T(8,128)(2,1)S(1)}, bf16[6,4096]{1,0:T(8,128)(2,1)S(1)}, u32[]{:S(2)}, u32[]{:S(2)}) collective-permute-start(bf16[6,4096]{1,0:T(8,128)(2,1)S(1)} %get-tuple-element.44), channel_id=1, source_target_pairs={{0,2},{1,3},{2,0},{3,1},{4,6},{5,7},{6,4},{7,5},{8,10},{9,11},{10,... | collective-permute-start | bytes 147464 | tf_op jit(solution)/shard_map/ppermute | solution.py:32
  104.2 1.7 %collective-permute-done.18 = bf16[6,4096]{1,0:T(8,128)(2,1)S(1)} collective-permute-done((bf16[6,4096]{1,0:T(8,128)(2,1)S(1)}, bf16[6,4096]{1,0:T(8,128)(2,1)S(1)}, u32[]{:S(2)}, u32[]{:S(2)}) %collective-permute-start.18) | collective-permute-done | bytes 49184 | tf_op jit(solution)/shard_map/ppermute | solution.py:32
  106.4 1.6 %collective-permute-done.17 = bf16[6,4096]{1,0:T(8,128)(2,1)S(1)} collective-permute-done((bf16[6,4096]{1,0:T(8,128)(2,1)S(1)}, bf16[6,4096]{1,0:T(8,128)(2,1)S(1)}, u32[]{:S(2)}, u32[]{:S(2)}) %collective-permute-start.17) | collective-permute-done | bytes 49184 | tf_op jit(solution)/shard_map/ppermute | solution.py:32
  (63 shorter events, 10.0 us)
Async XLA Ops:
  8.4 9.2 %collective-permute-start = (bf16[1536,1024]{1,0:T(8,128)(2,1)S(1)}, bf16[1536,1024]{1,0:T(8,128)(2,1)S(1)}, u32[]{:S(2)}, u32[]{:S(2)}) collective-permute-start(bf16[1536,1024]{1,0:T(8,128)(2,1)S(1)} %product_theirs.2.rest_0_), channel_id=1, source_target_pairs={{0,4},{4,0},{1,5},{5,1},{2,6},{6,2},{3,7},{7,3},{8,12},{12,8},{9,1... | collective-permute-start | bytes 9437192 | tf_op jit(solution)/shard_map/ppermute | solution.py:32
  17.5 6.7 %collective-permute-start.1 = (bf16[1536,1024]{1,0:T(8,128)(2,1)S(1)}, bf16[1536,1024]{1,0:T(8,128)(2,1)S(1)}, u32[]{:S(2)}, u32[]{:S(2)}) collective-permute-start(bf16[1536,1024]{1,0:T(8,128)(2,1)S(1)} %product_theirs.3), channel_id=1, source_target_pairs={{0,4},{4,0},{1,5},{5,1},{2,6},{6,2},{3,7},{7,3},{8,12},{12,8},{9,1... | collective-permute-start | bytes 9437192 | tf_op jit(solution)/shard_map/ppermute | solution.py:32
  21.4 19.9 %collective-permute-start.2 = (bf16[32,48,256]{2,1,0:T(8,128)(2,1)S(1)}, bf16[32,48,256]{2,1,0:T(8,128)(2,1)S(1)}, u32[]{:S(2)}, u32[]{:S(2)}) collective-permute-start(bf16[32,48,256]{2,1,0:T(8,128)(2,1)S(1)} %bitcast.64), channel_id=1, source_target_pairs={{0,1},{1,2},{2,3},{3,0},{4,5},{5,6},{6,7},{7,4},{8,9},{9,10},{10,1... | collective-permute-start | bytes 2359304 | tf_op jit(solution)/shard_map/ppermute | solution.py:32
  21.5 19.8 %collective-permute-start.3 = (bf16[32,48,256]{2,1,0:T(8,128)(2,1)S(1)}, bf16[32,48,256]{2,1,0:T(8,128)(2,1)S(1)}, u32[]{:S(2)}, u32[]{:S(2)}) collective-permute-start(bf16[32,48,256]{2,1,0:T(8,128)(2,1)S(1)} %bitcast.67), channel_id=1, source_target_pairs={{0,3},{1,0},{2,1},{3,2},{4,7},{5,4},{6,5},{7,6},{8,11},{9,8},{10,9... | collective-permute-start | bytes 2359304 | tf_op jit(solution)/shard_map/ppermute | solution.py:32
  30.3 19.3 %collective-permute-start.9 = (bf16[8,48,1024]{2,1,0:T(8,128)(2,1)S(1)}, bf16[8,48,1024]{2,1,0:T(8,128)(2,1)S(1)}, u32[]{:S(2)}, u32[]{:S(2)}) collective-permute-start(bf16[8,48,1024]{2,1,0:T(8,128)(2,1)S(1)} %get-tuple-element.35), channel_id=1, source_target_pairs={{0,8},{8,16},{16,24},{24,0},{1,9},{9,17},{17,25},{25,1},{2,10},{10... | collective-permute-start | bytes 2359304 | tf_op jit(solution)/shard_map/ppermute | solution.py:32
  30.4 19.2 %collective-permute-start.10 = (bf16[8,48,1024]{2,1,0:T(8,128)(2,1)S(1)}, bf16[8,48,1024]{2,1,0:T(8,128)(2,1)S(1)}, u32[]{:S(2)}, u32[]{:S(2)}) collective-permute-start(bf16[8,48,1024]{2,1,0:T(8,128)(2,1)S(1)} %get-tuple-element.36), channel_id=1, source_target_pairs={{0,24},{8,0},{16,8},{24,16},{1,25},{9,1},{17,9},{25,17},{2,26},{10... | collective-permute-start | bytes 2359304 | tf_op jit(solution)/shard_map/ppermute | solution.py:32
  41.5 11.1 %collective-permute-start.4 = (bf16[16,48,256]{2,1,0:T(8,128)(2,1)S(1)}, bf16[16,48,256]{2,1,0:T(8,128)(2,1)S(1)}, u32[]{:S(2)}, u32[]{:S(2)}) collective-permute-start(bf16[16,48,256]{2,1,0:T(8,128)(2,1)S(1)} %get-tuple-element.29), channel_id=1, source_target_pairs={{0,1},{1,2},{2,3},{3,0},{4,5},{5,6},{6,7},{7,4},{8,9},{9,10},{10,1... | collective-permute-start | bytes 1179656 | tf_op jit(solution)/shard_map/ppermute | solution.py:32
  41.6 11.0 %collective-permute-start.5 = (bf16[16,48,256]{2,1,0:T(8,128)(2,1)S(1)}, bf16[16,48,256]{2,1,0:T(8,128)(2,1)S(1)}, u32[]{:S(2)}, u32[]{:S(2)}) collective-permute-start(bf16[16,48,256]{2,1,0:T(8,128)(2,1)S(1)} %get-tuple-element.30), channel_id=1, source_target_pairs={{0,3},{1,0},{2,1},{3,2},{4,7},{5,4},{6,5},{7,6},{8,11},{9,8},{10,9... | collective-permute-start | bytes 1179656 | tf_op jit(solution)/shard_map/ppermute | solution.py:32
  49.8 9.9 %collective-permute-start.11 = (bf16[4,48,1024]{2,1,0:T(8,128)(2,1)S(1)}, bf16[4,48,1024]{2,1,0:T(8,128)(2,1)S(1)}, u32[]{:S(2)}, u32[]{:S(2)}) collective-permute-start(bf16[4,48,1024]{2,1,0:T(8,128)(2,1)S(1)} %get-tuple-element.38), channel_id=1, source_target_pairs={{0,8},{8,16},{16,24},{24,0},{1,9},{9,17},{17,25},{25,1},{2,10},{10... | collective-permute-start | bytes 1179656 | tf_op jit(solution)/shard_map/ppermute | solution.py:32
  49.9 9.8 %collective-permute-start.12 = (bf16[4,48,1024]{2,1,0:T(8,128)(2,1)S(1)}, bf16[4,48,1024]{2,1,0:T(8,128)(2,1)S(1)}, u32[]{:S(2)}, u32[]{:S(2)}) collective-permute-start(bf16[4,48,1024]{2,1,0:T(8,128)(2,1)S(1)} %get-tuple-element.39), channel_id=1, source_target_pairs={{0,24},{8,0},{16,8},{24,16},{1,25},{9,1},{17,9},{25,17},{2,26},{10... | collective-permute-start | bytes 1179656 | tf_op jit(solution)/shard_map/ppermute | solution.py:32
  53.4 10.5 %collective-permute-start.6 = (bf16[8,48,256]{2,1,0:T(8,128)(2,1)S(1)}, bf16[8,48,256]{2,1,0:T(8,128)(2,1)S(1)}, u32[]{:S(2)}, u32[]{:S(2)}) collective-permute-start(bf16[8,48,256]{2,1,0:T(8,128)(2,1)S(1)} %get-tuple-element.32), channel_id=1, source_target_pairs={{0,8},{8,16},{16,24},{24,0},{1,9},{9,17},{17,25},{25,1},{2,10},{10... | collective-permute-start | bytes 589832 | tf_op jit(solution)/shard_map/ppermute | solution.py:32
  53.5 11.4 %collective-permute-start.7 = (bf16[8,48,256]{2,1,0:T(8,128)(2,1)S(1)}, bf16[8,48,256]{2,1,0:T(8,128)(2,1)S(1)}, u32[]{:S(2)}, u32[]{:S(2)}) collective-permute-start(bf16[8,48,256]{2,1,0:T(8,128)(2,1)S(1)} %get-tuple-element.33), channel_id=1, source_target_pairs={{0,24},{8,0},{16,8},{24,16},{1,25},{9,1},{17,9},{25,17},{2,26},{10... | collective-permute-start | bytes 589832 | tf_op jit(solution)/shard_map/ppermute | solution.py:32
  56.2 44.3 %copy-start.1 = (f32[6,4096]{1,0:T(8,128)S(1)}, f32[6,4096]{1,0:T(8,128)}, u32[]{:S(2)}) copy-start(f32[6,4096]{1,0:T(8,128)} %param.7) | copy-start | bytes 294916
  56.2 44.3 %copy-start.2 = (f32[6,4096]{1,0:T(8,128)S(1)}, f32[6,4096]{1,0:T(8,128)}, u32[]{:S(2)}) copy-start(f32[6,4096]{1,0:T(8,128)} %param.8) | copy-start | bytes 294916
  56.2 44.3 %copy-start.3 = (f32[6,4096]{1,0:T(8,128)S(1)}, f32[6,4096]{1,0:T(8,128)}, u32[]{:S(2)}) copy-start(f32[6,4096]{1,0:T(8,128)} %param.9) | copy-start | bytes 294916
  56.2 12.3 %collective-permute-start.8 = (bf16[8,48,256]{2,1,0:T(8,128)(2,1)S(1)}, bf16[8,48,256]{2,1,0:T(8,128)(2,1)S(1)}, u32[]{:S(2)}, u32[]{:S(2)}) collective-permute-start(bf16[8,48,256]{2,1,0:T(8,128)(2,1)S(1)} %get-tuple-element.34), channel_id=1, source_target_pairs={{0,16},{8,24},{16,0},{24,8},{1,17},{9,25},{17,1},{25,9},{2,18},{10... | collective-permute-start | bytes 589832 | tf_op jit(solution)/shard_map/ppermute | solution.py:32
  60.6 7.9 %collective-permute-start.13 = (bf16[8,48,256]{2,1,0:T(8,128)(2,1)S(1)}, bf16[8,48,256]{2,1,0:T(8,128)(2,1)S(1)}, u32[]{:S(2)}, u32[]{:S(2)}) collective-permute-start(bf16[8,48,256]{2,1,0:T(8,128)(2,1)S(1)} %get-tuple-element.41), channel_id=1, source_target_pairs={{0,1},{1,2},{2,3},{3,0},{4,5},{5,6},{6,7},{7,4},{8,9},{9,10},{10,1... | collective-permute-start | bytes 589832 | tf_op jit(solution)/shard_map/ppermute | solution.py:32
  60.7 7.8 %collective-permute-start.14 = (bf16[8,48,256]{2,1,0:T(8,128)(2,1)S(1)}, bf16[8,48,256]{2,1,0:T(8,128)(2,1)S(1)}, u32[]{:S(2)}, u32[]{:S(2)}) collective-permute-start(bf16[8,48,256]{2,1,0:T(8,128)(2,1)S(1)} %get-tuple-element.42), channel_id=1, source_target_pairs={{0,3},{1,0},{2,1},{3,2},{4,7},{5,4},{6,5},{7,6},{8,11},{9,8},{10,9... | collective-permute-start | bytes 589832 | tf_op jit(solution)/shard_map/ppermute | solution.py:32
  64.0 7.2 %collective-permute-start.15 = (bf16[8,48,256]{2,1,0:T(8,128)(2,1)S(1)}, bf16[8,48,256]{2,1,0:T(8,128)(2,1)S(1)}, u32[]{:S(2)}, u32[]{:S(2)}) collective-permute-start(bf16[8,48,256]{2,1,0:T(8,128)(2,1)S(1)} %get-tuple-element.43), channel_id=1, source_target_pairs={{0,2},{1,3},{2,0},{3,1},{4,6},{5,7},{6,4},{7,5},{8,10},{9,11},{10,... | collective-permute-start | bytes 589832 | tf_op jit(solution)/shard_map/ppermute | solution.py:32
  72.2 21.1 %all-to-all-start = ((bf16[32,24,256]{2,1,0:T(8,128)(2,1)}), bf16[32,24,256]{2,1,0:T(8,128)(2,1)S(1)}, u32[]{:S(2)}, u32[]{:S(2)}) async-start(bf16[32,24,256]{2,1,0:T(8,128)(2,1)} %sum_for_z.1), calls=%async_computation | async-start | bytes 786432 | tf_op jit(solution)/shard_map/all_to_all | solution.py:40
  93.4 6.7 %collective-permute-start.16 = (bf16[4,2,6,256]{3,0,2,1:T(4,128)(2,1)S(1)}, bf16[4,2,6,256]{3,0,2,1:T(4,128)(2,1)S(1)}, u32[]{:S(2)}, u32[]{:S(2)}) collective-permute-start(bf16[4,2,6,256]{3,0,2,1:T(4,128)(2,1)S(1)} %fusion.3), channel_id=1, source_target_pairs={{0,4},{4,0},{1,5},{5,1},{2,6},{6,2},{3,7},{7,3},{8,12},{12,8},{9,1... | collective-permute-start | bytes 73736 | tf_op jit(solution)/shard_map/ppermute | solution.py:32
  101.3 4.6 %collective-permute-start.18 = (bf16[6,4096]{1,0:T(8,128)(2,1)S(1)}, bf16[6,4096]{1,0:T(8,128)(2,1)S(1)}, u32[]{:S(2)}, u32[]{:S(2)}) collective-permute-start(bf16[6,4096]{1,0:T(8,128)(2,1)S(1)} %get-tuple-element.44), channel_id=1, source_target_pairs={{0,2},{1,3},{2,0},{3,1},{4,6},{5,7},{6,4},{7,5},{8,10},{9,11},{10,... | collective-permute-start | bytes 147464 | tf_op jit(solution)/shard_map/ppermute | solution.py:32
  102.8 3.6 %collective-permute-start.19 = (bf16[6,4096]{1,0:T(8,128)(2,1)S(1)}, bf16[6,4096]{1,0:T(8,128)(2,1)S(1)}, u32[]{:S(2)}, u32[]{:S(2)}) collective-permute-start(bf16[6,4096]{1,0:T(8,128)(2,1)S(1)} %get-tuple-element.44), channel_id=1, source_target_pairs={{0,3},{1,0},{2,1},{3,2},{4,7},{5,4},{6,5},{7,6},{8,11},{9,8},{10,9... | collective-permute-start | bytes 147464 | tf_op jit(solution)/shard_map/ppermute | solution.py:32
  103.7 4.3 %collective-permute-start.17 = (bf16[6,4096]{1,0:T(8,128)(2,1)S(1)}, bf16[6,4096]{1,0:T(8,128)(2,1)S(1)}, u32[]{:S(2)}, u32[]{:S(2)}) collective-permute-start(bf16[6,4096]{1,0:T(8,128)(2,1)S(1)} %get-tuple-element.44), channel_id=1, source_target_pairs={{0,1},{1,2},{2,3},{3,0},{4,5},{5,6},{6,7},{7,4},{8,9},{9,10},{10,1... | collective-permute-start | bytes 147464 | tf_op jit(solution)/shard_map/ppermute | solution.py:32
  (1 other events, 1.9 us)
